TPU v7x, 128 devices: a whole 4x4x4 slice. The times are simulated.
128 devices in a mesh: band: 8 (over z, y_hi), fft: 16 (over y_lo, x, core).
Axes of the slice: x: 4, y: 4 (y_hi: 2, y_lo: 2; y = y_hi * 2 + y_lo), z: 4, core: 2. Of those that a mesh axis runs over, the one named last changes fastest.
Arguments:
- coeffs: bfloat16 [8, 384, 64, 2, 256], P('band', 'fft'), may hold values from -6 to 6
- potential: float32 [256, 256, 256], P('fft'), may hold values from -1 to 3
- pattern: int32 [384], replicated, may hold values from 0 to 1023, as said below
Outputs:
- images: bfloat16 [8, 384, 64, 2, 256], P('band', 'fft')
- matrix: float32 [2, 8, 8], P(None, 'band')
Inputs may be any that keep to these rules, and one draw needn't show every extreme that they name: `pattern`: 384 distinct stick-block numbers; block b covers the xy positions b * 64 to b * 64 + 64 - 1 (x = position // 256, y = position % 256); entry m belongs to the coefficient block m, held by fft index m // 24.
All inputs are finite; a program needn't handle non-finite values.
Results may differ from a plain program's by a relative error of at most 0.01.
Values may be sent and summed in bfloat16 or wider, within the bound.
No kernel may reach another device: no remote copies, remote signals or barrier semaphores. Data moves between devices by JAX's collectives and lax.ppermute only.
A program may use at most 128 MiB of HBM per device.

v0:
```python
import math

import jax
import jax.numpy as jnp
from jax import lax
from jax.sharding import PartitionSpec as P


def dft_table(grid_size, sign_value):
    counter = jnp.arange(grid_size, dtype=jnp.int32)
    phase_index = counter[:, None] * counter[None, :] % grid_size
    angles = phase_index.astype(jnp.float32) * (2.0 * math.pi / grid_size)
    unit_scale = 1.0 / math.sqrt(grid_size)
    cosine = jnp.cos(angles) * unit_scale
    sine_part = sign_value * jnp.sin(angles) * unit_scale
    upper_half = jnp.stack([cosine, sine_part], axis=1)
    lower_half = jnp.stack([-sine_part, cosine], axis=1)
    return jnp.stack([upper_half, lower_half], axis=0).astype(jnp.bfloat16)


def body(coeffs, potential, pattern):
    band_count, block_count, block_width = (coeffs.shape[0], coeffs.shape[1], coeffs.shape[2])
    grid_size = coeffs.shape[-1]
    plane_count = potential.shape[0]
    all_blocks = grid_size * grid_size // block_width
    forward = dft_table(grid_size, 1.0)
    backward = dft_table(grid_size, -1.0)
    flat_fwd = forward.reshape(2 * grid_size, 2 * grid_size)
    flat_bwd = backward.reshape(2 * grid_size, 2 * grid_size)
    cross_fwd = jnp.transpose(forward, (3, 2, 1, 0)).reshape(2 * grid_size, 2 * grid_size)
    cross_bwd = jnp.transpose(backward, (3, 2, 1, 0)).reshape(2 * grid_size, 2 * grid_size)
    sticks = jnp.dot(
        coeffs.reshape(band_count * block_count * block_width, 2 * grid_size),
        flat_fwd,
        preferred_element_type=jnp.float32,
    ).astype(jnp.bfloat16)
    sticks = sticks.reshape(band_count, block_count, block_width, 2, grid_size)
    planes = lax.all_to_all(sticks, "fft", split_axis=4, concat_axis=1, tiled=True)
    ordered = jnp.transpose(planes, (4, 0, 3, 1, 2))
    filled = jnp.zeros((plane_count, band_count, 2, all_blocks, block_width), jnp.bfloat16)
    filled = filled.at[:, :, :, pattern, :].set(ordered)
    filled = filled.reshape(plane_count, band_count, 2, grid_size, grid_size)
    along_y = jnp.matmul(filled[:, :, 0], flat_fwd[:grid_size], preferred_element_type=jnp.float32)
    along_y = along_y + jnp.matmul(
        filled[:, :, 1], flat_fwd[grid_size:], preferred_element_type=jnp.float32
    )
    along_y = along_y.astype(jnp.bfloat16).reshape(
        plane_count, band_count, 2 * grid_size, grid_size
    )
    along_x = jnp.matmul(cross_fwd, along_y, preferred_element_type=jnp.float32)
    along_x = along_x.reshape(plane_count, band_count, grid_size, 2, grid_size)
    scaled_field = (along_x * potential[:, None, :, None, :]).astype(jnp.bfloat16)
    scaled_field = scaled_field.reshape(plane_count, band_count, 2 * grid_size, grid_size)
    back_x = jnp.matmul(cross_bwd, scaled_field, preferred_element_type=jnp.float32).astype(
        jnp.bfloat16
    )
    back_x = back_x.reshape(plane_count, band_count, grid_size, 2 * grid_size)
    real_back = jnp.matmul(back_x, flat_bwd[:, :grid_size], preferred_element_type=jnp.float32)
    real_pick = jnp.take(
        real_back.reshape(plane_count, band_count, all_blocks, block_width), pattern, axis=2
    ).astype(jnp.bfloat16)
    imag_back = jnp.matmul(back_x, flat_bwd[:, grid_size:], preferred_element_type=jnp.float32)
    imag_pick = jnp.take(
        imag_back.reshape(plane_count, band_count, all_blocks, block_width), pattern, axis=2
    ).astype(jnp.bfloat16)
    picked = jnp.transpose(jnp.stack([real_pick, imag_pick], axis=2), (1, 3, 4, 2, 0))
    returned = lax.all_to_all(picked, "fft", split_axis=1, concat_axis=4, tiled=True)
    images = jnp.dot(
        returned.reshape(band_count * block_count * block_width, 2 * grid_size),
        flat_bwd,
        preferred_element_type=jnp.float32,
    ).astype(jnp.bfloat16)
    images = images.reshape(coeffs.shape)
    coeff_rows, image_rows = (
        lax.all_to_all(coeffs, "band", split_axis=1, concat_axis=0, tiled=True),
        lax.all_to_all(images, "band", split_axis=1, concat_axis=0, tiled=True),
    )
    all_bands = coeff_rows.shape[0]
    left_flat = coeff_rows.reshape(all_bands, -1)
    right_flat = image_rows.reshape(all_bands, -1)
    swapped = jnp.stack([image_rows[:, :, :, 1], -image_rows[:, :, :, 0]], axis=3).reshape(
        all_bands, -1
    )
    real_part = jnp.einsum("iq,jq->ij", left_flat, right_flat, preferred_element_type=jnp.float32)
    imag_part = jnp.einsum("iq,jq->ij", left_flat, swapped, preferred_element_type=jnp.float32)
    totals = lax.psum((real_part, imag_part), ("band", "fft"))
    total_count = block_count * lax.axis_size("fft") * block_width * grid_size
    matrix = jnp.stack([totals[0], totals[1]], axis=0) / total_count
    matrix_rows = lax.dynamic_slice_in_dim(
        matrix, lax.axis_index("band") * band_count, band_count, 1
    )
    return (images, matrix_rows)


def solution(mesh):
    placed = (P("band", "fft", None, None, None), P("fft", None, None), P())
    return jax.shard_map(
        body,
        mesh=mesh,
        in_specs=placed,
        out_specs=(P("band", "fft", None, None, None), P(None, "band", None)),
        check_vma=False,
    )
```

profile of v0, /device:TPU:0, one launch (start us, length us, event | category | flops | bytes accessed | tf_op | source)
XLA Modules:
  0.0 504.7 jit_solution(15081717649002539403)
XLA Ops:
  15.0 4.9 reshape.303
  19.9 5.9 %all-to-all-start = ((bf16[16,2,24576]{2,1,0:T(2,128)(2,1)}), bf16[16,2,24576]{2,1,0:T(2,128)(2,1)}, u32[]{:S(2)}, u32[]{:S(2)}) async-start(bf16[16,2,24576]{2,1,0:T(2,128)(2,1)} %reshape.303), calls=%async_computation | async-start | bytes 3145728 | tf_op jit(solution)/shard_map/all_to_all | solution.py:38
  27.4 24.3 %copy.81 = bf16[256,2,256,2]{3,2,1,0:T(8,128)(2,1)} copy(bf16[256,2,256,2]{0,2,1,3:T(8,128)(2,1)S(1)} %copy-done.2) | data formatting | bytes 1048576 | tf_op jit(solution)/shard_map/transpose | solution.py:30
  51.7 49.6 %reshape.293 = bf16[512,512,1]{1,0,2:T(8,128)(2,1)} reshape(bf16[256,2,256,2]{3,2,1,0:T(8,128)(2,1)} %copy.81) | data formatting | bytes 1048576 | tf_op jit(solution)/shard_map/reshape | solution.py:30
  103.5 24.3 %copy.80 = bf16[256,2,256,2]{3,2,1,0:T(8,128)(2,1)} copy(bf16[256,2,256,2]{0,2,1,3:T(8,128)(2,1)S(1)} %fusion.31) | data formatting | bytes 1048576 | tf_op jit(solution)/shard_map/transpose | solution.py:31
  127.8 49.6 %reshape.294 = bf16[512,512,1]{1,0,2:T(8,128)(2,1)} reshape(bf16[256,2,256,2]{3,2,1,0:T(8,128)(2,1)} %copy.80) | data formatting | bytes 1048576 | tf_op jit(solution)/shard_map/reshape | solution.py:31
  177.4 6.6 %mul.200 = f32[16,256,2,256]{3,2,1,0:T(2,128)} broadcast(f32[16,256,256]{2,1,0:T(8,128)} %param.6), dimensions={0,1,3} | broadcast | bytes 12582912 | tf_op jit(solution)/shard_map/mul | solution.py:52
  184.0 10.9 %mul.201 = f32[16,1,512,256]{3,2,0,1:T(8,128)} reshape(f32[16,256,2,256]{3,2,1,0:T(2,128)} %mul.200) | data formatting | bytes 16777216 | tf_op jit(solution)/shard_map/mul | solution.py:52
  206.2 40.9 %scatter_fusion = bf16[16,2,1024,64]{3,0,2,1:T(8,128)(2,1)} fusion(bf16[16,2,1024,64]{3,0,2,1:T(8,128)(2,1)} %broadcast.225, s32[384]{0:T(512)S(1)} %compare_select_fusion, bf16[384,16,2,64]{3,1,2,0:T(8,128)(2,1)S(1)} %bitcast.151), kind=kCustom, calls=%fused_computation.2 | custom fusion | bytes 4720128 | tf_op jit(solution)/shard_map/scatter | solution.py:41
  247.2 8.8 %copy.103 = bf16[16,2,1024,64]{3,2,0,1:T(8,128)(2,1)} copy(bf16[16,2,1024,64]{3,0,2,1:T(8,128)(2,1)} %scatter_fusion) | data formatting | bytes 8388608 | tf_op jit(solution)/shard_map/reshape | solution.py:42
  255.9 12.0 %reshape.302 = bf16[16,1,2,256,256]{4,3,0,2,1:T(8,128)(2,1)} reshape(bf16[16,2,1024,64]{3,2,0,1:T(8,128)(2,1)} %copy.103) | data formatting | bytes 8388608 | tf_op jit(solution)/shard_map/reshape | solution.py:42
  274.1 7.2 %reshape.239 = bf16[16,512,256]{2,1,0:T(8,128)(2,1)} reshape(bf16[16,256,512]{2,1,0:T(8,128)(2,1)} %add_convert_fusion) | data formatting | bytes 8388608 | tf_op jit(solution)/shard_map/reshape.7
  281.3 8.9 %convert_bitcast_fusion = bf16[16,1,512,256]{3,2,0,1:T(8,128)(2,1)} fusion(bf16[512,512,1]{1,0,2:T(8,128)(2,1)S(1)} %copy-done.6, f32[16,1,512,256]{3,2,0,1:T(8,128)} %mul.201, bf16[512,512,1]{1,0,2:T(8,128)(2,1)S(1)} %copy-done.5, bf16[16,512,256]{2,1,0:T(8,128)(2,1)} %reshape.239), kind=kOutput, calls=%fused_computation.10 | convolution fusion | flops 4301258752 | bytes 17825792 | tf_op jit(solution)/shard_map/dot_general | solution.py:54
  290.2 7.2 %reshape.241 = bf16[16,256,512]{2,1,0:T(8,128)(2,1)} reshape(bf16[16,1,512,256]{3,2,0,1:T(8,128)(2,1)} %convert_bitcast_fusion) | data formatting | bytes 8388608 | tf_op jit(solution)/shard_map/reshape.12
  297.4 5.0 fusion.17
  303.7 6.5 %reshape.243 = bf16[16,1,1024,64]{3,2,0,1:T(8,128)(2,1)} reshape(bf16[16,256,256]{2,1,0:T(8,128)(2,1)} %fusion.17) | data formatting | bytes 4194304 | tf_op jit(solution)/shard_map/reshape | solution.py:64
  310.2 6.8 %copy.113 = bf16[16,1,1024,64]{3,0,2,1:T(8,128)(2,1)} copy(bf16[16,1,1024,64]{3,2,0,1:T(8,128)(2,1)} %reshape.243) | data formatting | bytes 4194304 | tf_op jit(solution)/shard_map/reshape | solution.py:64
  320.3 6.9 %copy.114 = bf16[16,1,1024,64]{3,0,2,1:T(8,128)(2,1)} copy(bf16[16,1,1024,64]{3,2,0,1:T(8,128)(2,1)} %reshape.242) | data formatting | bytes 4194304 | tf_op jit(solution)/shard_map/reshape | solution.py:60
  338.9 28.0 %all_to_all.54 = bf16[16,2,24576]{2,1,0:T(2,128)(2,1)} all-to-all(bf16[16,2,24576]{2,1,0:T(2,128)(2,1)} %reshape.305), channel_id=1, replica_groups=mesh['band'=8,'fft'=16] {'fft'}, dimensions={0} | all-to-all | bytes 3145728 | tf_op jit(solution)/shard_map/all_to_all | solution.py:67
  366.9 7.9 %all-to-all-start.3 = ((bf16[1,24,64,2,256]{4,3,2,0,1:T(2,128)(2,1)}), bf16[1,24,64,2,256]{4,3,2,0,1:T(2,128)(2,1)}, u32[]{:S(2)}, u32[]{:S(2)}) async-start(bf16[1,24,64,2,256]{4,3,2,0,1:T(2,128)(2,1)} %bitcast.34), calls=%async_computation.3 | async-start | bytes 3145728 | tf_op jit(solution)/shard_map/all_to_all | solution.py:75
  389.7 7.5 %all-to-all-done.3 = bf16[1,24,64,2,256]{4,3,2,0,1:T(2,128)(2,1)} async-done(((bf16[1,24,64,2,256]{4,3,2,0,1:T(2,128)(2,1)}), bf16[1,24,64,2,256]{4,3,2,0,1:T(2,128)(2,1)}, u32[]{:S(2)}, u32[]{:S(2)}) %all-to-all-start.3) | async-done | bytes 1572896 | tf_op jit(solution)/shard_map/all_to_all | solution.py:75
  403.4 19.5 %all-to-all-done.2 = bf16[1,24,64,2,256]{4,3,2,0,1:T(2,128)(2,1)S(1)} async-done(((bf16[1,24,64,2,256]{4,3,2,0,1:T(2,128)(2,1)}), bf16[1,24,64,2,256]{4,3,2,0,1:T(2,128)(2,1)S(1)}, u32[]{:S(2)}, u32[]{:S(2)}) %all-to-all-start.2) | async-done | bytes 1572896 | tf_op jit(solution)/shard_map/all_to_all | solution.py:76
  425.8 4.4 pad_maximum_fusion
  441.5 62.4 %all-reduce = (f32[1,8,8]{2,1,0:T(8,128)S(1)}, f32[1,8,8]{2,1,0:T(8,128)S(1)}) all-reduce(f32[1,8,8]{2,1,0:T(8,128)S(1)} %bitcast.167, f32[1,8,8]{2,1,0:T(8,128)S(1)} %bitcast.168), channel_id=1, replica_groups=mesh['band'=8,'fft'=16] {'band','fft'}, use_global_device_ids=true, to_apply=%region_2.4 | all-reduce | flops 128 | bytes 1024 | tf_op jit(solution)/shard_map/psum | solution.py:86
  (71 shorter events, 87.6 us)
Async XLA Ops:
  19.9 5.9 %copy-start.3 = (bf16[256,2,256]{2,0,1:T(8,128)(2,1)S(1)}, bf16[256,2,256]{2,0,1:T(8,128)(2,1)}, u32[]{:S(2)}) copy-start(bf16[256,2,256]{2,0,1:T(8,128)(2,1)} %get-tuple-element.14) | copy-start | bytes 786436
  19.9 7.5 %copy-start.2 = (bf16[256,2,256,2]{0,2,1,3:T(8,128)(2,1)S(1)}, bf16[256,2,256,2]{0,2,1,3:T(8,128)(2,1)}, u32[]{:S(2)}) copy-start(bf16[256,2,256,2]{0,2,1,3:T(8,128)(2,1)} %get-tuple-element.8) | copy-start | bytes 1572868
  19.9 176.5 %all-to-all-start = ((bf16[16,2,24576]{2,1,0:T(2,128)(2,1)}), bf16[16,2,24576]{2,1,0:T(2,128)(2,1)}, u32[]{:S(2)}, u32[]{:S(2)}) async-start(bf16[16,2,24576]{2,1,0:T(2,128)(2,1)} %reshape.303), calls=%async_computation | async-start | bytes 3145728 | tf_op jit(solution)/shard_map/all_to_all | solution.py:38
  194.9 1.5 copy-start.8
  255.9 12.0 %copy-start.4 = (bf16[256,512,1]{1,0,2:T(8,128)(2,1)S(1)}, bf16[256,512,1]{1,0,2:T(8,128)(2,1)}, u32[]{:S(2)}) copy-start(bf16[256,512,1]{1,0,2:T(8,128)(2,1)} %reshape.291) | copy-start | bytes 786436
  268.0 3.0 copy-start
  274.1 7.2 %copy-start.5 = (bf16[512,512,1]{1,0,2:T(8,128)(2,1)S(1)}, bf16[512,512,1]{1,0,2:T(8,128)(2,1)}, u32[]{:S(2)}) copy-start(bf16[512,512,1]{1,0,2:T(8,128)(2,1)} %reshape.293) | copy-start | bytes 1572868
  274.1 7.2 %copy-start.6 = (bf16[512,512,1]{1,0,2:T(8,128)(2,1)S(1)}, bf16[512,512,1]{1,0,2:T(8,128)(2,1)}, u32[]{:S(2)}) copy-start(bf16[512,512,1]{1,0,2:T(8,128)(2,1)} %reshape.294) | copy-start | bytes 1572868
  290.2 7.2 %copy-start.7 = (bf16[64,8,2,256]{3,1,2,0:T(8,128)(2,1)S(1)}, bf16[64,8,2,256]{3,1,2,0:T(8,128)(2,1)}, u32[]{:S(2)}) copy-start(bf16[64,8,2,256]{3,1,2,0:T(8,128)(2,1)} %copy.107) | copy-start | bytes 1572868
  297.4 5.0 copy-start.1
  366.9 30.4 %all-to-all-start.3 = ((bf16[1,24,64,2,256]{4,3,2,0,1:T(2,128)(2,1)}), bf16[1,24,64,2,256]{4,3,2,0,1:T(2,128)(2,1)}, u32[]{:S(2)}, u32[]{:S(2)}) async-start(bf16[1,24,64,2,256]{4,3,2,0,1:T(2,128)(2,1)} %bitcast.34), calls=%async_computation.3 | async-start | bytes 3145728 | tf_op jit(solution)/shard_map/all_to_all | solution.py:75
  397.2 25.7 %all-to-all-start.2 = ((bf16[1,24,64,2,256]{4,3,2,0,1:T(2,128)(2,1)}), bf16[1,24,64,2,256]{4,3,2,0,1:T(2,128)(2,1)S(1)}, u32[]{:S(2)}, u32[]{:S(2)}) async-start(bf16[1,24,64,2,256]{4,3,2,0,1:T(2,128)(2,1)} %bitcast.33), calls=%async_computation.2 | async-start | bytes 3145728 | tf_op jit(solution)/shard_map/all_to_all | solution.py:76
where the time goes:
time: 514 us; the launch traced here: 505 us
  local copies, waits for them, and re-layouts  322 us (63%)
  blocking collectives  90.4 us (18%)
  matrix products  30.6 us (6%)
  waiting for transfers between devices  27 us (5%)
  starting transfers between devices  17.3 us (3%)
  other arithmetic  15.8 us (3%)
    psum x1, blocking collectives, body(): totals = lax.psum((real_part, imag_part), ('band', 'fft'))  62.4 us
    reshape x1, local copies, waits for them, and re-layouts, body(): jnp.transpose(forward, (3, 2, 1, 0)).reshape(2 * grid_size, 2 * grid_size)  49.6 us
    reshape x1, local copies, waits for them, and re-layouts, body(): jnp.transpose(backward, (3, 2, 1, 0)).reshape(2 * grid_size, 2 * grid_size)  49.6 us
    scatter x1, local copies, waits for them, and re-layouts, body(): filled = filled.at[:, :, :, pattern, :].set(ordered)  40.9 us
    all_to_all x1, blocking collectives, body(): lax.all_to_all(picked, 'fft', split_axis=1, concat_axis=4, tiled=True)  28 us
    transpose x1, local copies, waits for them, and re-layouts, body(): jnp.transpose(forward, (3, 2, 1, 0)).reshape(2 * grid_size, 2 * grid_size)  24.3 us
    transpose x1, local copies, waits for them, and re-layouts, body(): jnp.transpose(backward, (3, 2, 1, 0)).reshape(2 * grid_size, 2 * grid_size)  24.3 us
    reshape x2, local copies, waits for them, and re-layouts, body(): filled = filled.reshape(plane_count, band_count, 2, grid_size, grid_size)  20.8 us
  transfers between devices with their start and end apart: 3, of which 2 were waited for; matrix products, arithmetic and copies ran while one was open for 37% of the time, Pallas kernels for 0%

commit v1 on v0

v1 whole, which is shorter than its diff:
```python
import functools
import math

import jax
import jax.numpy as jnp
import ml_dtypes
import numpy as np
from jax import lax
from jax.experimental import pallas as pl
from jax.experimental.pallas import tpu as pltpu
from jax.sharding import PartitionSpec as P

F32 = jnp.float32
BF16 = jnp.bfloat16
AXES = ("band", "fft")
VMEM = pl.BlockSpec(memory_space=pltpu.VMEM)


def dft_table(size, sign):
    counter = np.arange(size)
    angles = (counter[:, None] * counter[None, :] % size) * (2.0 * math.pi / size)
    cosine = np.cos(angles) / math.sqrt(size)
    sine = sign * np.sin(angles) / math.sqrt(size)
    table = np.stack([np.stack([cosine, sine], 1), np.stack([-sine, cosine], 1)], 0)
    return table.astype(ml_dtypes.bfloat16)


def plane_table(size, bands, ffts):
    per_fft = size // ffts
    per_dev = per_fft // bands
    forward = dft_table(size, 1.0)
    p, b, f = np.meshgrid(np.arange(per_dev), np.arange(bands), np.arange(ffts), indexing="ij")
    z = (f * per_fft + b * per_dev + p).reshape(-1)
    return np.ascontiguousarray(forward[:, :, :, z].transpose(3, 2, 0, 1)).reshape(2 * size, 2 * size)


def split_table(size, parts, per_dev):
    width = size // parts
    forward = dft_table(size, 1.0).astype(np.float32)
    out = np.zeros((parts, 2, per_dev, width, 2, per_dev, width), np.float32)
    for s in range(parts):
        part = forward[:, :width, :, s::parts]
        for p in range(per_dev):
            out[s, :, p, :, :, p, :] = part
    side = 2 * per_dev * width
    return out.reshape(parts, side, side).astype(ml_dtypes.bfloat16)


def order_table(size, parts, per_dev):
    width = size // parts
    out = np.zeros((per_dev, size, parts, per_dev, width), np.float32)
    for p in range(per_dev):
        for y in range(size):
            out[p, y, y % parts, p, y // parts] = 1.0
    return out.reshape(per_dev * size, parts * per_dev * width).astype(ml_dtypes.bfloat16)


def dot(a, b):
    return jnp.dot(a, b, preferred_element_type=F32)


def dot_nt(a, b):
    return lax.dot_general(a, b, (((1,), (1,)), ((), ())), preferred_element_type=F32)


def to_planes_kernel(c_ref, t_ref, o_ref, scr):
    half = t_ref.shape[0] // 2
    blocks = scr.shape[0] // half
    low = lax.broadcasted_iota(jnp.int32, (half, 128), 1) < 64
    for g in range(blocks // 4):
        r = dot_nt(t_ref[...], c_ref[g * 256 : (g + 1) * 256, :])
        for h in range(2):
            a = r[:half, h * 128 : (h + 1) * 128]
            b = r[half:, h * 128 : (h + 1) * 128]
            m = g * 4 + h * 2
            scr[pl.ds(m, half, stride=blocks), :] = jnp.where(low, a, pltpu.roll(b, 64, 1))
            scr[pl.ds(m + 1, half, stride=blocks), :] = jnp.where(low, pltpu.roll(a, 64, 1), b)
    o_ref[...] = scr[...].astype(BF16)


def from_planes_kernel(x_ref, t_ref, o_ref, scr):
    half = t_ref.shape[0] // 2
    blocks = scr.shape[0] // half
    scr[...] = x_ref[...].astype(F32)
    for g in range(blocks // 4):
        rows = []
        for m in range(g * 4, g * 4 + 4):
            y = jnp.transpose(scr[pl.ds(m, half, stride=blocks), :]).astype(BF16)
            rows.append(jnp.concatenate([y[:64], y[64:]], axis=1))
        left = jnp.concatenate(rows, axis=0)
        o_ref[g * 256 : (g + 1) * 256, :] = dot(left, t_ref[...]).astype(BF16)


def prepare_kernel(row_ref, col_ref, v_ref, f_ref, b_ref, ord_ref, tx_ref, xt_ref, v4_ref):
    size = f_ref.shape[0] // 2
    count = row_ref.shape[1]

    def hot(code, iota, s, axis):
        turn = (s * ((code >> 1) & 3) + (code & 1)) & 3
        hit = iota == (code >> 3)
        real = jnp.where(turn == 0, 1.0, jnp.where(turn == 2, -1.0, 0.0))
        imag = jnp.where(turn == 1, 1.0, jnp.where(turn == 3, -1.0, 0.0))
        return jnp.concatenate(
            [jnp.where(hit, real, 0.0), jnp.where(hit, imag, 0.0)], axis=axis
        ).astype(BF16)

    rows = lax.broadcasted_iota(jnp.int32, (size, count), 0)
    cols = lax.broadcasted_iota(jnp.int32, (count, size), 1)
    for s in range(4):
        tx_ref[s * 2 * size : (s + 1) * 2 * size, :] = dot(
            b_ref[...], hot(row_ref[...], rows, s, 0)
        ).astype(BF16)
        xt_ref[:, s * 2 * size : (s + 1) * 2 * size] = dot(
            hot(col_ref[...], cols, s, 1), f_ref[...]
        ).astype(BF16)
    v = jnp.concatenate([v_ref[0], v_ref[1]], axis=1)
    high = v.astype(BF16)
    rest = (v - high.astype(F32)).astype(BF16)
    v4_ref[...] = dot(high, ord_ref[...]) + dot(rest, ord_ref[...])


def planes_kernel(r_ref, tx_ref, xt_ref, v4_ref, yf_ref, yb_ref, o_ref, h_scr):
    size = v4_ref.shape[0]

    def pair(i, carry):
        w = jnp.concatenate([r_ref[2 * i], r_ref[2 * i + 1]], axis=1)
        for s in range(4):
            g = dot(tx_ref[s * 2 * size : (s + 1) * 2 * size, :], w).astype(BF16)
            v = v4_ref[:, s * 128 : (s + 1) * 128]
            v = jnp.concatenate([v, v], axis=1)
            for j in range(2):
                left = jnp.concatenate(
                    [g[:size, j * 128 : (j + 1) * 128], g[size:, j * 128 : (j + 1) * 128]], axis=1
                )
                field = (dot(left, yf_ref[s]) * v).astype(BF16)
                back = dot(field, yb_ref[s]).astype(BF16)
                row = s * 2 * size
                h_scr[row : row + size, j * 128 : (j + 1) * 128] = back[:, :128]
                h_scr[row + size : row + 2 * size, j * 128 : (j + 1) * 128] = back[:, 128:]
        out = dot(xt_ref[...], h_scr[...]).astype(BF16)
        o_ref[2 * i] = out[:, :128]
        o_ref[2 * i + 1] = out[:, 128:]
        return carry

    lax.fori_loop(0, r_ref.shape[0] // 2, pair, 0)


def gram_kernel(r_ref, p_ref, o_ref, r_scr, p_scr):
    bands, count = r_ref.shape[0], r_ref.shape[1]
    rows = 2 * bands
    groups = count // 48
    for src, scr in ((r_ref, r_scr), (p_ref, p_scr)):
        for b in range(bands):
            v = src[b].astype(F32)
            for f in range(groups):
                for d in range(2):
                    start = (f * 2 + d) * 24
                    scr[pl.ds(f * 24 * rows + b * 2 + d, 24, stride=rows), :] = v[start : start + 24]
    total = jnp.zeros((rows, rows), F32)
    for q in range(groups):
        base = q * 24 * rows
        sides = []
        for scr in (r_scr, p_scr):
            v = scr[base : base + 24 * rows, :].astype(BF16)
            sides.append(jnp.concatenate([v[m * rows : (m + 1) * rows] for m in range(24)], axis=1))
        total = total + dot_nt(sides[0], sides[1])
    o_ref[...] = total


def call(kernel, out_shape, scratch, flops, args):
    read = sum(a.size * a.dtype.itemsize for a in args)
    written = sum(s.size * s.dtype.itemsize for s in jax.tree.leaves(out_shape))
    return pl.pallas_call(
        kernel,
        out_shape=out_shape,
        in_specs=[VMEM] * len(args),
        out_specs=jax.tree.map(lambda _: VMEM, out_shape),
        scratch_shapes=scratch,
        compiler_params=pltpu.CompilerParams(vmem_limit_bytes=32 * 2**20),
        cost_estimate=pl.CostEstimate(flops=flops, bytes_accessed=read + written, transcendentals=0),
    )(*args)


def body(coeffs, potential, pattern):
    block_count, block_width = coeffs.shape[1], coeffs.shape[2]
    size = coeffs.shape[-1]
    bands, ffts = lax.axis_size("band"), lax.axis_size("fft")
    devices = bands * ffts
    per_dev = size // devices
    sticks = block_count * block_width
    rows = 2 * block_count
    shape = jax.ShapeDtypeStruct

    table = jnp.asarray(plane_table(size, bands, ffts))
    forward = dft_table(size, 1.0).reshape(2 * size, 2 * size)
    y_forward = split_table(size, 4, per_dev)
    y_backward = np.ascontiguousarray(y_forward.transpose(0, 2, 1))

    sent = call(
        to_planes_kernel,
        shape((devices * rows, 128), BF16),
        [pltpu.VMEM((devices * rows, 128), F32)],
        2 * sticks * (2 * size) ** 2,
        (coeffs.reshape(sticks, 2 * size), table),
    )
    got = lax.all_to_all(
        sent.reshape(devices, rows, 128), AXES, split_axis=0, concat_axis=0, tiled=True
    )
    got = got.reshape(bands, ffts * rows, 128)

    order = pattern.reshape(ffts, 1, block_count) * 2 + jnp.arange(2, dtype=jnp.int32)[None, :, None]
    planes = lax.dynamic_slice_in_dim(potential, lax.axis_index("band") * per_dev, per_dev, 0)
    count = ffts * rows
    x_table, x_back, v4 = call(
        prepare_kernel,
        (
            shape((8 * size, count), BF16),
            shape((count, 8 * size), BF16),
            shape((size, per_dev * size), F32),
        ),
        [],
        2 * 2 * 4 * count * (2 * size) ** 2,
        (
            order.reshape(1, count),
            order.reshape(count, 1),
            planes,
            jnp.asarray(forward),
            jnp.asarray(np.ascontiguousarray(forward.T)),
            jnp.asarray(order_table(size, 4, per_dev)),
        ),
    )

    picked = call(
        planes_kernel,
        shape((bands, count, 128), BF16),
        [pltpu.VMEM((8 * size, 256), BF16)],
        2 * bands * 128 * 2 * 8 * size * count,
        (got, x_table, x_back, v4, jnp.asarray(y_forward), jnp.asarray(y_backward)),
    )
    returned = lax.all_to_all(
        picked.reshape(devices, rows, 128), AXES, split_axis=0, concat_axis=0, tiled=True
    )

    gram = call(
        gram_kernel,
        shape((2 * bands, 2 * bands), F32),
        [pltpu.VMEM((bands * count, 128), F32)] * 2,
        2 * 256 * bands * count * 128,
        (got, picked),
    )
    gram = gram.reshape(bands, 2, bands, 2)
    total = jnp.stack(
        [gram[:, 0, :, 0] + gram[:, 1, :, 1], gram[:, 0, :, 1] - gram[:, 1, :, 0]], axis=0
    )
    for axis, extent in (("fft", ffts), ("band", bands)):
        step = 1
        while step < extent:
            total = total + lax.ppermute(total, axis, [(i, i ^ step) for i in range(extent)])
            step *= 2
    matrix = total / (block_count * ffts * block_width * size)
    matrix_rows = lax.dynamic_slice_in_dim(matrix, lax.axis_index("band"), 1, 1)

    images = call(
        from_planes_kernel,
        shape((sticks, 2 * size), BF16),
        [pltpu.VMEM((devices * rows, 128), F32)],
        2 * sticks * (2 * size) ** 2,
        (returned.reshape(devices * rows, 128), table),
    )
    return (images.reshape(coeffs.shape), matrix_rows)


def solution(mesh):
    placed = (P("band", "fft", None, None, None), P("fft", None, None), P())
    return jax.shard_map(
        body,
        mesh=mesh,
        in_specs=placed,
        out_specs=(P("band", "fft", None, None, None), P(None, "band", None)),
        check_vma=False,
    )
```

time: 514 us -> 115 us (0.22); the launches traced: 505 us -> 115 us
  local copies, waits for them, and re-layouts: 322 us -> 18.3 us
  blocking collectives: 90.4 us -> 0 us
  matrix products: 30.6 us -> 0 us
  Pallas kernels: 0 us -> 30 us
  other arithmetic: 15.8 us -> 0.78 us
  starting transfers between devices: 17.3 us -> 29.3 us
  waiting for transfers between devices: 27 us -> 35.4 us
    reshape x15 -> x2, local copies, waits for them, and re-layouts: 165 us -> 1.96 us  [the longest x1 1.85 us: body(): return (images.reshape(coeffs.shape), matrix_rows)]
    psum x1 -> x0, blocking collectives: 62.4 us -> none  [body(): totals = lax.psum((real_part, imag_part), ('band', 'fft'))]
    transpose x2 -> x0, local copies, waits for them, and re-layouts: 48.6 us -> none  [the longest x1 24.3 us: body(): jnp.transpose(forward, (3, 2, 1, 0)).reshape(2 * grid_size, 2 * grid_size)]
    scatter x1 -> x0, local copies, waits for them, and re-layouts: 40.9 us -> none  [body(): filled = filled.at[:, :, :, pattern, :].set(ordered)]
    dot_general x9 -> x0, matrix products: 30.6 us -> none  [the longest x1 8.9 us: body(): jnp.matmul(cross_bwd, scaled_field, preferred_element_type=jnp.float32)]
    pallas_call x0 -> x5, Pallas kernels: none -> 30 us  [call(): pl.pallas_call(kernel, out_shape=out_shape, in_specs=[VMEM] * len(args),...]
    all_to_all x1 -> x0, blocking collectives: 28 us -> none  [body(): lax.all_to_all(picked, 'fft', split_axis=1, concat_axis=4, tiled=True)]
    ppermute x0 -> x7, waiting for transfers between devices: none -> 23.5 us  [body(): lax.ppermute(total, axis, [(i, i ^ step) for i in range(extent)])]
  transfers between devices with their start and end apart: 3 -> 9, of which waited for: 2 -> 8; matrix products, arithmetic and copies ran while one was open for 37% -> 2% of each run, Pallas kernels for 0% -> 7%
where the time goes in v1:
time: 115 us
  waiting for transfers between devices  35.4 us (31%)
  Pallas kernels  30 us (26%)
  starting transfers between devices  29.3 us (25%)
  local copies, waits for them, and re-layouts  18.3 us (16%)
    pallas_call x5, Pallas kernels, call(): pl.pallas_call(kernel, out_shape=out_shape, in_specs=[VMEM] * len(args),...  30 us
    ppermute x7, waiting for transfers between devices, body(): lax.ppermute(total, axis, [(i, i ^ step) for i in range(extent)])  23.5 us
    unnamed x29, local copies, waits for them, and re-layouts  14.9 us
    ppermute x7, starting transfers between devices, body(): lax.ppermute(total, axis, [(i, i ^ step) for i in range(extent)])  13.3 us
    all_to_all x1, waiting for transfers between devices, body(): lax.all_to_all(sent.reshape(devices, rows, 128), AXES, split_axis=0, conc...  11.9 us
    all_to_all x1, starting transfers between devices, body(): lax.all_to_all(sent.reshape(devices, rows, 128), AXES, split_axis=0, conc...  11.1 us
    all_to_all x1, starting transfers between devices, body(): lax.all_to_all(picked.reshape(devices, rows, 128), AXES, split_axis=0, co...  4.82 us
  transfers between devices with their start and end apart: 9, of which 8 were waited for; matrix products, arithmetic and copies ran while one was open for 2% of the time, Pallas kernels for 7%

profile of v1, /device:TPU:0, one launch (start us, length us, event | category | flops | bytes accessed | tf_op | source)
XLA Modules:
  0.0 114.5 jit_solution(13316220584863776841)
XLA Ops:
  0.6 1.8 %copy.17 = bf16[192,8,2,256]{3,1,2,0:T(8,128)(2,1)S(1)} copy(bf16[192,8,2,256]{3,2,1,0:T(2,128)(2,1)} %bitcast.13) | data formatting | bytes 3145728
  2.4 2.5 %shard_map.104 = bf16[6144,128]{1,0:T(8,128)(2,1)} custom-call(bf16[1536,512]{1,0:T(8,128)(2,1)S(1)} %bitcast.12, bf16[512,512]{1,0:T(8,128)(2,1)S(1)} %copy-done), custom_call_target="tpu_custom_call" | custom-call | flops 805306368 | bytes 3670016 | tf_op jit(solution)/shard_map/pallas_call | solution.py:173
  4.9 11.1 %all-to-all-start = ((bf16[128,48,128]{2,1,0:T(8,128)(2,1)}), bf16[128,48,128]{2,1,0:T(8,128)(2,1)S(1)}, u32[]{:S(2)}, u32[]{:S(2)}) async-start(bf16[128,48,128]{2,1,0:T(8,128)(2,1)} %bitcast), calls=%async_computation | async-start | bytes 3145728 | tf_op jit(solution)/shard_map/all_to_all | solution.py:206
  20.7 4.1 %shard_map.105 = (bf16[2048,768]{1,0:T(8,128)(2,1)S(1)}, bf16[768,2048]{1,0:T(8,128)(2,1)S(1)}, f32[256,512]{1,0:T(8,128)S(1)}) custom-call(s32[1,768]{1,0:T(1,128)S(1)} %add.76.row_ref, s32[768,1]{1,0:T(8,128)S(1)} %add.89.col_ref, f32[2,256,256]{2,1,0:T(8,128)S(1)} %constant_dynamic-slice_fusion.v_ref, bf16[512,512]{1,0:T(8,128)(2,1)S(1)} %copy-done.6, ...), custom_call_target="tpu_custom_call" | custom-call | flops 3221225472 | bytes 8919040 | tf_op jit(solution)/shard_map/pallas_call | solution.py:173
  24.9 1.6 %copy-done.7 = bf16[2048,768]{1,0:T(8,128)(2,1)} copy-done((bf16[2048,768]{1,0:T(8,128)(2,1)}, bf16[2048,768]{1,0:T(8,128)(2,1)S(1)}, u32[]{:S(2)}) %copy-start.7) | copy-done | bytes 3145752
  26.5 1.7 %copy-done.9 = bf16[768,2048]{1,0:T(8,128)(2,1)} copy-done((bf16[768,2048]{1,0:T(8,128)(2,1)}, bf16[768,2048]{1,0:T(8,128)(2,1)S(1)}, u32[]{:S(2)}) %copy-start.9) | copy-done | bytes 3145752
  29.0 11.9 %all-to-all-done = bf16[128,48,128]{2,1,0:T(8,128)(2,1)S(1)} async-done(((bf16[128,48,128]{2,1,0:T(8,128)(2,1)}), bf16[128,48,128]{2,1,0:T(8,128)(2,1)S(1)}, u32[]{:S(2)}, u32[]{:S(2)}) %all-to-all-start) | async-done | bytes 1572896 | tf_op jit(solution)/shard_map/all_to_all | solution.py:206
  40.9 1.9 %copy-done.8 = bf16[2048,768]{1,0:T(8,128)(2,1)S(1)} copy-done((bf16[2048,768]{1,0:T(8,128)(2,1)S(1)}, bf16[2048,768]{1,0:T(8,128)(2,1)}, u32[]{:S(2)}) %copy-start.8) | copy-done | bytes 3145752
  42.8 1.9 %copy-done.10 = bf16[768,2048]{1,0:T(8,128)(2,1)S(1)} copy-done((bf16[768,2048]{1,0:T(8,128)(2,1)S(1)}, bf16[768,2048]{1,0:T(8,128)(2,1)}, u32[]{:S(2)}) %copy-start.10) | copy-done | bytes 3145752
  45.7 18.4 %shard_map.106.p_ref = bf16[8,768,128]{2,1,0:T(8,128)(2,1)} custom-call(bf16[8,768,128]{2,1,0:T(8,128)(2,1)S(1)} %bitcast.10, bf16[2048,768]{1,0:T(8,128)(2,1)S(1)} %copy-done.8, bf16[768,2048]{1,0:T(8,128)(2,1)S(1)} %copy-done.10, f32[256,512]{1,0:T(8,128)S(1)} %copy-done.12, bf16[4,256,256]{2,1,0:T(8,128)(2,1)S(1)} %copy-done.3, ...), custom_call_target="tpu_custom_call" | custom-call | flops 6442450944 | bytes 11010048 | tf_op jit(solution)/shard_map/pallas_call | solution.py:173
  64.1 4.8 %all-to-all-start.1 = ((bf16[128,48,128]{2,1,0:T(8,128)(2,1)}), bf16[128,48,128]{2,1,0:T(8,128)(2,1)S(1)}, u32[]{:S(2)}, u32[]{:S(2)}) async-start(bf16[128,48,128]{2,1,0:T(8,128)(2,1)} %bitcast.2), calls=%async_computation.1 | async-start | bytes 3145728 | tf_op jit(solution)/shard_map/all_to_all | solution.py:240
  68.9 3.6 %shard_map.108 = f32[16,16]{1,0:T(8,128)S(1)} custom-call(bf16[8,768,128]{2,1,0:T(8,128)(2,1)S(1)} %bitcast.11, bf16[8,768,128]{2,1,0:T(8,128)(2,1)} %shard_map.106.p_ref), custom_call_target="tpu_custom_call" | custom-call | flops 402653184 | bytes 3146752 | tf_op jit(solution)/shard_map/pallas_call | solution.py:173
  74.8 12.2 %collective-permute-done.1 = f32[2,8,8]{2,1,0:T(8,128)S(1)} collective-permute-done((f32[2,8,8]{2,1,0:T(8,128)S(1)}, f32[2,8,8]{2,1,0:T(8,128)S(1)}, u32[]{:S(2)}, u32[]{:S(2)}) %collective-permute-start.1) | collective-permute-done | bytes 544 | tf_op jit(solution)/shard_map/ppermute | solution.py:258
  86.9 2.7 %collective-permute-start.2 = (f32[2,8,8]{2,1,0:T(8,128)S(1)}, f32[2,8,8]{2,1,0:T(8,128)S(1)}, u32[]{:S(2)}, u32[]{:S(2)}) collective-permute-start(f32[2,8,8]{2,1,0:T(8,128)S(1)} %fusion.4), channel_id=1, source_target_pairs={{0,4},{1,5},{2,6},{3,7},{4,0},{5,1},{6,2},{7,3},{8,12},{9,13},{10,... | collective-permute-start | bytes 1544 | tf_op jit(solution)/shard_map/ppermute | solution.py:258
  89.6 2.4 %collective-permute-done.2 = f32[2,8,8]{2,1,0:T(8,128)S(1)} collective-permute-done((f32[2,8,8]{2,1,0:T(8,128)S(1)}, f32[2,8,8]{2,1,0:T(8,128)S(1)}, u32[]{:S(2)}, u32[]{:S(2)}) %collective-permute-start.2) | collective-permute-done | bytes 544 | tf_op jit(solution)/shard_map/ppermute | solution.py:258
  92.1 1.5 %collective-permute-start.3 = (f32[2,8,8]{2,1,0:T(8,128)S(1)}, f32[2,8,8]{2,1,0:T(8,128)S(1)}, u32[]{:S(2)}, u32[]{:S(2)}) collective-permute-start(f32[2,8,8]{2,1,0:T(8,128)S(1)} %add.83), channel_id=1, source_target_pairs={{0,8},{1,9},{2,10},{3,11},{4,12},{5,13},{6,14},{7,15},{8,0},{9,1},... | collective-permute-start | bytes 1544 | tf_op jit(solution)/shard_map/ppermute | solution.py:258
  93.6 2.1 %collective-permute-done.3 = f32[2,8,8]{2,1,0:T(8,128)S(1)} collective-permute-done((f32[2,8,8]{2,1,0:T(8,128)S(1)}, f32[2,8,8]{2,1,0:T(8,128)S(1)}, u32[]{:S(2)}, u32[]{:S(2)}) %collective-permute-start.3) | collective-permute-done | bytes 544 | tf_op jit(solution)/shard_map/ppermute | solution.py:258
  95.7 3.1 %collective-permute-start.4 = (f32[2,8,8]{2,1,0:T(8,128)S(1)}, f32[2,8,8]{2,1,0:T(8,128)S(1)}, u32[]{:S(2)}, u32[]{:S(2)}) collective-permute-start(f32[2,8,8]{2,1,0:T(8,128)S(1)} %add.84), channel_id=1, source_target_pairs={{0,16},{16,0},{32,48},{48,32},{64,80},{80,64},{96,112},{112,96},{1... | collective-permute-start | bytes 1544 | tf_op jit(solution)/shard_map/ppermute | solution.py:258
  98.8 2.1 %collective-permute-done.4 = f32[2,8,8]{2,1,0:T(8,128)S(1)} collective-permute-done((f32[2,8,8]{2,1,0:T(8,128)S(1)}, f32[2,8,8]{2,1,0:T(8,128)S(1)}, u32[]{:S(2)}, u32[]{:S(2)}) %collective-permute-start.4) | collective-permute-done | bytes 544 | tf_op jit(solution)/shard_map/ppermute | solution.py:258
  100.9 1.7 %collective-permute-start.5 = (f32[2,8,8]{2,1,0:T(8,128)S(1)}, f32[2,8,8]{2,1,0:T(8,128)S(1)}, u32[]{:S(2)}, u32[]{:S(2)}) collective-permute-start(f32[2,8,8]{2,1,0:T(8,128)S(1)} %add.85), channel_id=1, source_target_pairs={{0,32},{16,48},{32,0},{48,16},{64,96},{80,112},{96,64},{112,80},{1... | collective-permute-start | bytes 1544 | tf_op jit(solution)/shard_map/ppermute | solution.py:258
  102.6 1.9 %collective-permute-done.5 = f32[2,8,8]{2,1,0:T(8,128)S(1)} collective-permute-done((f32[2,8,8]{2,1,0:T(8,128)S(1)}, f32[2,8,8]{2,1,0:T(8,128)S(1)}, u32[]{:S(2)}, u32[]{:S(2)}) %collective-permute-start.5) | collective-permute-done | bytes 544 | tf_op jit(solution)/shard_map/ppermute | solution.py:258
  104.6 3.5 %collective-permute-start.6 = (f32[2,8,8]{2,1,0:T(8,128)S(1)}, f32[2,8,8]{2,1,0:T(8,128)S(1)}, u32[]{:S(2)}, u32[]{:S(2)}) collective-permute-start(f32[2,8,8]{2,1,0:T(8,128)S(1)} %add.86), channel_id=1, source_target_pairs={{0,64},{16,80},{32,96},{48,112},{64,0},{80,16},{96,32},{112,48},{1... | collective-permute-start | bytes 1544 | tf_op jit(solution)/shard_map/ppermute | solution.py:258
  108.1 1.6 %collective-permute-done.6 = f32[2,8,8]{2,1,0:T(8,128)S(1)} collective-permute-done((f32[2,8,8]{2,1,0:T(8,128)S(1)}, f32[2,8,8]{2,1,0:T(8,128)S(1)}, u32[]{:S(2)}, u32[]{:S(2)}) %collective-permute-start.6) | collective-permute-done | bytes 544 | tf_op jit(solution)/shard_map/ppermute | solution.py:258
  112.7 1.9 %reshape.122 = bf16[1,24,64,2,256]{4,3,2,1,0:T(2,128)(2,1)} reshape(bf16[1536,512]{1,0:T(8,128)(2,1)S(1)} %shard_map.107) | data formatting | bytes 3145728 | tf_op jit(solution)/shard_map/reshape | solution.py:270
  (45 shorter events, 11.5 us)
Async XLA Ops:
  0.6 1.8 %copy-start = (bf16[512,512]{1,0:T(8,128)(2,1)S(1)}, bf16[512,512]{1,0:T(8,128)(2,1)}, u32[]{:S(2)}) copy-start(bf16[512,512]{1,0:T(8,128)(2,1)} %constant.30.clone.t_ref) | copy-start | bytes 1572868
  4.9 11.2 %copy-start.13 = (s32[384]{0:T(512)S(1)}, s32[384]{0:T(512)}, u32[]{:S(2)}) copy-start(s32[384]{0:T(512)} %param.11) | copy-start | bytes 4612
  4.9 35.9 %all-to-all-start = ((bf16[128,48,128]{2,1,0:T(8,128)(2,1)}), bf16[128,48,128]{2,1,0:T(8,128)(2,1)S(1)}, u32[]{:S(2)}, u32[]{:S(2)}) async-start(bf16[128,48,128]{2,1,0:T(8,128)(2,1)} %bitcast), calls=%async_computation | async-start | bytes 3145728 | tf_op jit(solution)/shard_map/all_to_all | solution.py:206
  17.6 1.0 copy-start.4
  18.6 1.0 copy-start.5
  19.7 1.0 copy-start.6
  20.7 20.1 %copy-start.2 = (bf16[4,256,256]{2,1,0:T(8,128)(2,1)S(1)}, bf16[4,256,256]{2,1,0:T(8,128)(2,1)}, u32[]{:S(2)}) copy-start(bf16[4,256,256]{2,1,0:T(8,128)(2,1)} %constant.35.clone.yb_ref) | copy-start | bytes 1572868
  20.7 20.1 %copy-start.3 = (bf16[4,256,256]{2,1,0:T(8,128)(2,1)S(1)}, bf16[4,256,256]{2,1,0:T(8,128)(2,1)}, u32[]{:S(2)}) copy-start(bf16[4,256,256]{2,1,0:T(8,128)(2,1)} %constant.34.clone.yf_ref) | copy-start | bytes 1572868
  24.8 1.7 %copy-start.7 = (bf16[2048,768]{1,0:T(8,128)(2,1)}, bf16[2048,768]{1,0:T(8,128)(2,1)S(1)}, u32[]{:S(2)}) copy-start(bf16[2048,768]{1,0:T(8,128)(2,1)S(1)} %get-tuple-element.5.tx_ref) | copy-start | bytes 9437188
  26.5 1.7 %copy-start.9 = (bf16[768,2048]{1,0:T(8,128)(2,1)}, bf16[768,2048]{1,0:T(8,128)(2,1)S(1)}, u32[]{:S(2)}) copy-start(bf16[768,2048]{1,0:T(8,128)(2,1)S(1)} %get-tuple-element.6.xt_ref) | copy-start | bytes 9437188
  28.2 0.8 copy-start.11
  40.9 1.9 %copy-start.8 = (bf16[2048,768]{1,0:T(8,128)(2,1)S(1)}, bf16[2048,768]{1,0:T(8,128)(2,1)}, u32[]{:S(2)}) copy-start(bf16[2048,768]{1,0:T(8,128)(2,1)} %copy-done.7) | copy-start | bytes 9437188
  42.8 1.9 %copy-start.10 = (bf16[768,2048]{1,0:T(8,128)(2,1)S(1)}, bf16[768,2048]{1,0:T(8,128)(2,1)}, u32[]{:S(2)}) copy-start(bf16[768,2048]{1,0:T(8,128)(2,1)} %copy-done.9) | copy-start | bytes 9437188
  44.6 1.0 copy-start.12
  64.1 46.2 %all-to-all-start.1 = ((bf16[128,48,128]{2,1,0:T(8,128)(2,1)}), bf16[128,48,128]{2,1,0:T(8,128)(2,1)S(1)}, u32[]{:S(2)}, u32[]{:S(2)}) async-start(bf16[128,48,128]{2,1,0:T(8,128)(2,1)} %bitcast.2), calls=%async_computation.1 | async-start | bytes 3145728 | tf_op jit(solution)/shard_map/all_to_all | solution.py:240
  72.8 1.3 %collective-permute-start = (f32[2,8,8]{2,1,0:T(8,128)S(1)}, f32[2,8,8]{2,1,0:T(8,128)S(1)}, u32[]{:S(2)}, u32[]{:S(2)}) collective-permute-start(f32[2,8,8]{2,1,0:T(8,128)S(1)} %pad_maximum_fusion), channel_id=1, source_target_pairs={{0,1},{1,0},{2,3},{3,2},{4,5},{5,4},{6,7},{7,6},{8,9},{9,8},{10,11... | collective-permute-start | bytes 1544 | tf_op jit(solution)/shard_map/ppermute | solution.py:258
  74.1 12.8 %collective-permute-start.1 = (f32[2,8,8]{2,1,0:T(8,128)S(1)}, f32[2,8,8]{2,1,0:T(8,128)S(1)}, u32[]{:S(2)}, u32[]{:S(2)}) collective-permute-start(f32[2,8,8]{2,1,0:T(8,128)S(1)} %fusion.3), channel_id=1, source_target_pairs={{0,2},{1,3},{2,0},{3,1},{4,6},{5,7},{6,4},{7,5},{8,10},{9,11},{10,... | collective-permute-start | bytes 1544 | tf_op jit(solution)/shard_map/ppermute | solution.py:258
  86.9 5.2 %collective-permute-start.2 = (f32[2,8,8]{2,1,0:T(8,128)S(1)}, f32[2,8,8]{2,1,0:T(8,128)S(1)}, u32[]{:S(2)}, u32[]{:S(2)}) collective-permute-start(f32[2,8,8]{2,1,0:T(8,128)S(1)} %fusion.4), channel_id=1, source_target_pairs={{0,4},{1,5},{2,6},{3,7},{4,0},{5,1},{6,2},{7,3},{8,12},{9,13},{10,... | collective-permute-start | bytes 1544 | tf_op jit(solution)/shard_map/ppermute | solution.py:258
  92.1 3.7 %collective-permute-start.3 = (f32[2,8,8]{2,1,0:T(8,128)S(1)}, f32[2,8,8]{2,1,0:T(8,128)S(1)}, u32[]{:S(2)}, u32[]{:S(2)}) collective-permute-start(f32[2,8,8]{2,1,0:T(8,128)S(1)} %add.83), channel_id=1, source_target_pairs={{0,8},{1,9},{2,10},{3,11},{4,12},{5,13},{6,14},{7,15},{8,0},{9,1},... | collective-permute-start | bytes 1544 | tf_op jit(solution)/shard_map/ppermute | solution.py:258
  95.7 5.2 %collective-permute-start.4 = (f32[2,8,8]{2,1,0:T(8,128)S(1)}, f32[2,8,8]{2,1,0:T(8,128)S(1)}, u32[]{:S(2)}, u32[]{:S(2)}) collective-permute-start(f32[2,8,8]{2,1,0:T(8,128)S(1)} %add.84), channel_id=1, source_target_pairs={{0,16},{16,0},{32,48},{48,32},{64,80},{80,64},{96,112},{112,96},{1... | collective-permute-start | bytes 1544 | tf_op jit(solution)/shard_map/ppermute | solution.py:258
  100.9 3.7 %collective-permute-start.5 = (f32[2,8,8]{2,1,0:T(8,128)S(1)}, f32[2,8,8]{2,1,0:T(8,128)S(1)}, u32[]{:S(2)}, u32[]{:S(2)}) collective-permute-start(f32[2,8,8]{2,1,0:T(8,128)S(1)} %add.85), channel_id=1, source_target_pairs={{0,32},{16,48},{32,0},{48,16},{64,96},{80,112},{96,64},{112,80},{1... | collective-permute-start | bytes 1544 | tf_op jit(solution)/shard_map/ppermute | solution.py:258
  104.6 5.2 %collective-permute-start.6 = (f32[2,8,8]{2,1,0:T(8,128)S(1)}, f32[2,8,8]{2,1,0:T(8,128)S(1)}, u32[]{:S(2)}, u32[]{:S(2)}) collective-permute-start(f32[2,8,8]{2,1,0:T(8,128)S(1)} %add.86), channel_id=1, source_target_pairs={{0,64},{16,80},{32,96},{48,112},{64,0},{80,16},{96,32},{112,48},{1... | collective-permute-start | bytes 1544 | tf_op jit(solution)/shard_map/ppermute | solution.py:258
  110.3 1.0 copy-start.1

commit v2 on v1

v2 whole, which is shorter than its diff:
```python
import math

import jax
import jax.numpy as jnp
import ml_dtypes
import numpy as np
from jax import lax
from jax.experimental import pallas as pl
from jax.experimental.pallas import tpu as pltpu
from jax.sharding import PartitionSpec as P

F32 = jnp.float32
BF16 = jnp.bfloat16
AXES = ("band", "fft")
VMEM = pl.BlockSpec(memory_space=pltpu.VMEM)
HBM = pl.BlockSpec(memory_space=pltpu.HBM)


def dft_table(size, sign):
    counter = np.arange(size)
    angles = (counter[:, None] * counter[None, :] % size) * (2.0 * math.pi / size)
    cosine = np.cos(angles) / math.sqrt(size)
    sine = sign * np.sin(angles) / math.sqrt(size)
    table = np.stack([np.stack([cosine, sine], 1), np.stack([-sine, cosine], 1)], 0)
    return table.astype(ml_dtypes.bfloat16)


def plane_table(size, bands, ffts):
    per_fft = size // ffts
    per_dev = per_fft // bands
    forward = dft_table(size, 1.0)
    p, b, f = np.meshgrid(np.arange(per_dev), np.arange(bands), np.arange(ffts), indexing="ij")
    z = (f * per_fft + b * per_dev + p).reshape(-1)
    return np.ascontiguousarray(forward[:, :, :, z].transpose(3, 2, 0, 1)).reshape(2 * size, 2 * size)


def split_table(size, parts, per_dev):
    width = size // parts
    forward = dft_table(size, 1.0).astype(np.float32)
    out = np.zeros((parts, 2, per_dev, width, 2, per_dev, width), np.float32)
    for s in range(parts):
        part = forward[:, :width, :, s::parts]
        for p in range(per_dev):
            out[s, :, p, :, :, p, :] = part
    side = 2 * per_dev * width
    return out.reshape(parts, side, side).astype(ml_dtypes.bfloat16)


def order_table(size, parts, per_dev):
    width = size // parts
    out = np.zeros((per_dev, size, parts, per_dev, width), np.float32)
    for p in range(per_dev):
        for y in range(size):
            out[p, y, y % parts, p, y // parts] = 1.0
    return out.reshape(per_dev * size, parts * per_dev * width).astype(ml_dtypes.bfloat16)


def dot(a, b):
    return jnp.dot(a, b, preferred_element_type=F32)


def dot_nt(a, b):
    return lax.dot_general(a, b, (((1,), (1,)), ((), ())), preferred_element_type=F32)


def to_planes_kernel(c_ref, t_ref, o_ref, scr):
    half = t_ref.shape[0] // 2
    blocks = scr.shape[0] // half
    low = lax.broadcasted_iota(jnp.int32, (half, 128), 1) < 64
    for g in range(blocks // 4):
        r = dot_nt(t_ref[...], c_ref[g * 256 : (g + 1) * 256, :])
        for h in range(2):
            a = r[:half, h * 128 : (h + 1) * 128]
            b = r[half:, h * 128 : (h + 1) * 128]
            m = g * 4 + h * 2
            scr[pl.ds(m, half, stride=blocks), :] = jnp.where(low, a, pltpu.roll(b, 64, 1))
            scr[pl.ds(m + 1, half, stride=blocks), :] = jnp.where(low, pltpu.roll(a, 64, 1), b)
    o_ref[...] = scr[...].astype(BF16)


def from_planes_kernel(x_ref, t_hbm, o_ref, m_ref, scr, table, sem):
    copy = pltpu.make_async_copy(t_hbm, table, sem)
    copy.start()
    half = t_hbm.shape[0] // 2
    blocks = scr.shape[0] // half
    rows = 2 * blocks
    total = jnp.zeros((8, 128), F32)
    for i in range(x_ref.shape[0]):
        scr[i * rows : (i + 1) * rows, :] = x_ref[i, :rows, :].astype(F32)
        total = total + x_ref[i, rows:, :].astype(F32)
    m_ref[...] = jnp.broadcast_to(total[0:1] + (total[1:2] + total[2:3]), (8, 128))
    copy.wait()
    for g in range(blocks // 4):
        parts = []
        for m in range(g * 4, g * 4 + 4):
            y = jnp.transpose(scr[pl.ds(m, half, stride=blocks), :]).astype(BF16)
            parts.append(jnp.concatenate([y[:64], y[64:]], axis=1))
        left = jnp.concatenate(parts, axis=0)
        o_ref[g * 256 : (g + 1) * 256, :] = dot(left, table[...]).astype(BF16)


def prepare_kernel(
    row_ref, col_ref, v_ref, f_ref, b_ref, ord_ref, tx_hbm, xt_hbm, v4_hbm, tx, xt, v4, sems
):
    size = f_ref.shape[0] // 2
    count = row_ref.shape[1]

    def hot(code, iota, s, axis):
        turn = (s * ((code >> 1) & 3) + (code & 1)) & 3
        hit = iota == (code >> 3)
        real = jnp.where(turn == 0, 1.0, jnp.where(turn == 2, -1.0, 0.0))
        imag = jnp.where(turn == 1, 1.0, jnp.where(turn == 3, -1.0, 0.0))
        return jnp.concatenate(
            [jnp.where(hit, real, 0.0), jnp.where(hit, imag, 0.0)], axis=axis
        ).astype(BF16)

    copies = []
    rows = lax.broadcasted_iota(jnp.int32, (size, count), 0)
    cols = lax.broadcasted_iota(jnp.int32, (count, size), 1)
    for s in range(4):
        part = slice(s * 2 * size, (s + 1) * 2 * size)
        tx[part, :] = dot(b_ref[...], hot(row_ref[...], rows, s, 0)).astype(BF16)
        copies.append(pltpu.make_async_copy(tx.at[part], tx_hbm.at[part], sems.at[s]))
        copies[-1].start()
        xt[:, part] = dot(hot(col_ref[...], cols, s, 1), f_ref[...]).astype(BF16)
    copies.append(pltpu.make_async_copy(xt, xt_hbm, sems.at[4]))
    copies[-1].start()
    v = jnp.concatenate([v_ref[0], v_ref[1]], axis=1)
    high = v.astype(BF16)
    rest = (v - high.astype(F32)).astype(BF16)
    both = dot(high, ord_ref[...]) + dot(rest, ord_ref[...])
    for s in range(4):
        v4[s] = both[:, s * 128 : (s + 1) * 128]
    copies.append(pltpu.make_async_copy(v4, v4_hbm, sems.at[5]))
    copies[-1].start()
    for copy in copies:
        copy.wait()


def planes_kernel(
    r_ref, tx_hbm, xt_hbm, v4_hbm, yf_ref, yb_ref, o_ref, tx, xt, v4, h, r_scr, p_scr, sems
):
    size = v4.shape[1]
    bands, count = r_ref.shape[0], r_ref.shape[1]
    ffts, blocks = o_ref.shape[1], count // (2 * o_ref.shape[1])
    rows, width = 2 * blocks, 2 * bands
    load_v = pltpu.make_async_copy(v4_hbm, v4, sems.at[5])
    loads = []
    for s in range(4):
        part = slice(s * 2 * size, (s + 1) * 2 * size)
        loads.append(pltpu.make_async_copy(tx_hbm.at[part], tx.at[part], sems.at[s]))
    load_xt = pltpu.make_async_copy(xt_hbm, xt, sems.at[4])
    loads[0].start()
    load_v.start()
    for copy in loads[1:]:
        copy.start()
    load_xt.start()

    def spread(scr, b, v):
        for f in range(ffts):
            for d in range(2):
                start = (f * 2 + d) * blocks
                at = pl.ds(f * blocks * width + d * bands + b, blocks, stride=width)
                scr[at, :] = v[start : start + blocks]

    for s in range(4):
        loads[s].wait()
        if s == 0:
            load_v.wait()
        w = jnp.concatenate([r_ref[b] for b in range(bands)], axis=1)
        g = dot(tx[s * 2 * size : (s + 1) * 2 * size, :], w).astype(BF16)
        left = jnp.concatenate(
            [
                jnp.concatenate(
                    [g[:size, b * 128 : (b + 1) * 128], g[size:, b * 128 : (b + 1) * 128]], axis=1
                )
                for b in range(bands)
            ],
            axis=0,
        )
        v = jnp.concatenate([v4[s], v4[s]], axis=1)
        field = (dot(left, yf_ref[s]) * jnp.concatenate([v] * bands, axis=0)).astype(BF16)
        back = dot(field, yb_ref[s]).astype(BF16)
        row = s * 2 * size
        for b in range(bands):
            part = back[b * size : (b + 1) * size]
            h[row : row + size, b * 128 : (b + 1) * 128] = part[:, :128]
            h[row + size : row + 2 * size, b * 128 : (b + 1) * 128] = part[:, 128:]
        for b in range(2 * s, 2 * s + 2):
            spread(r_scr, b, r_ref[b].astype(F32))
    load_xt.wait()
    for n in range(bands // 2):
        out = dot(xt[...], h[:, n * 256 : (n + 1) * 256])
        for j in range(2):
            b = 2 * n + j
            v = out[:, j * 128 : (j + 1) * 128]
            spread(p_scr, b, v)
            v = v.astype(BF16)
            for f in range(ffts):
                o_ref[b, f, :rows, :] = v[f * rows : (f + 1) * rows]

    gram = jnp.zeros((width, width), F32)
    for f in range(ffts):
        sides = []
        for scr in (r_scr, p_scr):
            v = scr[f * blocks * width : (f + 1) * blocks * width, :].astype(BF16)
            sides.append(
                jnp.concatenate([v[m * width : (m + 1) * width] for m in range(blocks)], axis=1)
            )
        gram = gram + dot_nt(sides[0], sides[1])
    real = gram[:bands, :bands] + gram[bands:, bands:]
    imag = gram[:bands, bands:] - gram[bands:, :bands]
    total = jnp.concatenate([real, imag, jnp.zeros((bands, 128 - width), F32)], axis=1)
    first = total.astype(BF16).astype(F32)
    second = (total - first).astype(BF16).astype(F32)
    third = total - first - second
    line = lax.broadcasted_iota(jnp.int32, (8, 128), 0)
    for b in range(bands):
        part = jnp.where(
            line == 0,
            first[b : b + 1],
            jnp.where(line == 1, second[b : b + 1], jnp.where(line == 2, third[b : b + 1], 0.0)),
        ).astype(BF16)
        for f in range(ffts):
            o_ref[b, f, rows:, :] = part


def call(kernel, out_shape, scratch, flops, args, in_hbm=(), out_hbm=False):
    read = sum(a.size * a.dtype.itemsize for a in args)
    written = sum(s.size * s.dtype.itemsize for s in jax.tree.leaves(out_shape))
    return pl.pallas_call(
        kernel,
        out_shape=out_shape,
        in_specs=[HBM if i in in_hbm else VMEM for i in range(len(args))],
        out_specs=jax.tree.map(lambda _: HBM if out_hbm else VMEM, out_shape),
        scratch_shapes=scratch,
        compiler_params=pltpu.CompilerParams(vmem_limit_bytes=40 * 2**20),
        cost_estimate=pl.CostEstimate(flops=flops, bytes_accessed=read + written, transcendentals=0),
    )(*args)


def body(coeffs, potential, pattern):
    block_count, block_width = coeffs.shape[1], coeffs.shape[2]
    size = coeffs.shape[-1]
    bands, ffts = lax.axis_size("band"), lax.axis_size("fft")
    devices = bands * ffts
    per_dev = size // devices
    sticks = block_count * block_width
    rows = 2 * block_count
    shape = jax.ShapeDtypeStruct

    table = jnp.asarray(plane_table(size, bands, ffts))
    forward = dft_table(size, 1.0).reshape(2 * size, 2 * size)
    y_forward = split_table(size, 4, per_dev)
    y_backward = np.ascontiguousarray(y_forward.transpose(0, 2, 1))

    sent = call(
        to_planes_kernel,
        shape((devices * rows, 128), BF16),
        [pltpu.VMEM((devices * rows, 128), F32)],
        2 * sticks * (2 * size) ** 2,
        (coeffs.reshape(sticks, 2 * size), table),
    )
    got = lax.all_to_all(
        sent.reshape(devices, rows, 128), AXES, split_axis=0, concat_axis=0, tiled=True
    )
    got = got.reshape(bands, ffts * rows, 128)

    order = pattern.reshape(ffts, 1, block_count) * 2 + jnp.arange(2, dtype=jnp.int32)[None, :, None]
    planes = lax.dynamic_slice_in_dim(potential, lax.axis_index("band") * per_dev, per_dev, 0)
    count = ffts * rows
    tables = (
        shape((8 * size, count), BF16),
        shape((count, 8 * size), BF16),
        shape((4, size, per_dev * size // 4), F32),
    )
    held = [pltpu.VMEM(t.shape, t.dtype) for t in tables]
    x_table, x_back, v4 = call(
        prepare_kernel,
        tables,
        held + [pltpu.SemaphoreType.DMA((6,))],
        2 * 2 * 4 * count * (2 * size) ** 2,
        (
            order.reshape(1, count),
            order.reshape(count, 1),
            planes,
            jnp.asarray(forward),
            jnp.asarray(np.ascontiguousarray(forward.T)),
            jnp.asarray(order_table(size, 4, per_dev)),
        ),
        out_hbm=True,
    )

    picked = call(
        planes_kernel,
        shape((bands, ffts, rows + 8, 128), BF16),
        held
        + [pltpu.VMEM((8 * size, bands * 128), BF16)]
        + [pltpu.VMEM((bands * count, 128), F32)] * 2
        + [pltpu.SemaphoreType.DMA((6,))],
        2 * bands * 128 * 2 * 8 * size * count,
        (got, x_table, x_back, v4, jnp.asarray(y_forward), jnp.asarray(y_backward)),
        in_hbm=(1, 2, 3),
    )
    returned = lax.all_to_all(
        picked.reshape(devices, rows + 8, 128), AXES, split_axis=0, concat_axis=0, tiled=True
    )

    images, sums = call(
        from_planes_kernel,
        (shape((sticks, 2 * size), BF16), shape((8, 128), F32)),
        [
            pltpu.VMEM((devices * rows, 128), F32),
            pltpu.VMEM((2 * size, 2 * size), BF16),
            pltpu.SemaphoreType.DMA(()),
        ],
        2 * sticks * (2 * size) ** 2,
        (returned, table),
        in_hbm=(1,),
    )
    matrix_rows = sums[0, : 2 * bands].reshape(2, 1, bands) / (block_count * ffts * block_width * size)
    return (images.reshape(coeffs.shape), matrix_rows)


def solution(mesh):
    placed = (P("band", "fft", None, None, None), P("fft", None, None), P())
    return jax.shard_map(
        body,
        mesh=mesh,
        in_specs=placed,
        out_specs=(P("band", "fft", None, None, None), P(None, "band", None)),
        check_vma=False,
    )
```

time: 115 us -> 96.3 us (0.84)
  blocking collectives: 0 us -> 31.7 us
  waiting for transfers between devices: 35.4 us -> 10 us
  starting transfers between devices: 29.3 us -> 11.1 us
  Pallas kernels: 30 us -> 23.8 us
    all_to_all x0 -> x1, blocking collectives: none -> 31.7 us  [body(): lax.all_to_all(picked.reshape(devices, rows + 8, 128), AXES, split_axis=0...]
    ppermute x7 -> x0, waiting for transfers between devices: 23.5 us -> none  [body(): lax.ppermute(total, axis, [(i, i ^ step) for i in range(extent)])]
    ppermute x7 -> x0, starting transfers between devices: 13.3 us -> none  [body(): lax.ppermute(total, axis, [(i, i ^ step) for i in range(extent)])]
    pallas_call x5 -> x4, Pallas kernels: 30 us -> 23.8 us  [call(): pl.pallas_call(kernel, out_shape=out_shape, in_specs=[HBM if i in in_hbm...]
    all_to_all x1 -> x0, starting transfers between devices: 4.82 us -> none  [body(): lax.all_to_all(picked.reshape(devices, rows, 128), AXES, split_axis=0, co...]
    all_to_all x1, waiting for transfers between devices: 11.9 us -> 10 us  [body(): lax.all_to_all(sent.reshape(devices, rows, 128), AXES, split_axis=0, conc...]
    unnamed x29 -> x27, local copies, waits for them, and re-layouts: 14.9 us -> 13.8 us
  transfers between devices with their start and end apart: 9 -> 1, of which waited for: 8 -> 1; matrix products, arithmetic and copies ran while one was open for 2% -> 2% of each run, Pallas kernels for 7% -> 6%
where the time goes in v2:
time: 96.3 us; the launch traced here: 95.2 us
  blocking collectives  31.7 us (33%)
  Pallas kernels  23.8 us (25%)
  local copies, waits for them, and re-layouts  17.8 us (18%)
  starting transfers between devices  11.1 us (12%)
  waiting for transfers between devices  10 us (10%)
    all_to_all x1, blocking collectives, body(): lax.all_to_all(picked.reshape(devices, rows + 8, 128), AXES, split_axis=0...  31.7 us
    pallas_call x4, Pallas kernels, call(): pl.pallas_call(kernel, out_shape=out_shape, in_specs=[HBM if i in in_hbm...  23.8 us
    unnamed x27, local copies, waits for them, and re-layouts  13.8 us
    all_to_all x1, starting transfers between devices, body(): lax.all_to_all(sent.reshape(devices, rows, 128), AXES, split_axis=0, conc...  11.1 us
    all_to_all x1, waiting for transfers between devices, body(): lax.all_to_all(sent.reshape(devices, rows, 128), AXES, split_axis=0, conc...  10 us
  transfers between devices with their start and end apart: 1, of which 1 were waited for; matrix products, arithmetic and copies ran while one was open for 2% of the time, Pallas kernels for 6%

profile of v2, /device:TPU:0, one launch (start us, length us, event | category | flops | bytes accessed | tf_op | source)
XLA Modules:
  0.0 95.2 jit_solution(10800164074366287292)
XLA Ops:
  0.6 0.0 copy-start
  0.6 1.8 %copy.14 = bf16[192,8,2,256]{3,1,2,0:T(8,128)(2,1)S(1)} copy(bf16[192,8,2,256]{3,2,1,0:T(2,128)(2,1)} %bitcast.10) | data formatting | bytes 3145728
  2.4 2.5 %shard_map.104 = bf16[6144,128]{1,0:T(8,128)(2,1)} custom-call(bf16[1536,512]{1,0:T(8,128)(2,1)S(1)} %bitcast.7, bf16[512,512]{1,0:T(8,128)(2,1)S(1)} %copy-done), custom_call_target="tpu_custom_call" | custom-call | flops 805306368 | bytes 3670016 | tf_op jit(solution)/shard_map/pallas_call | solution.py:231
  4.9 11.1 %all-to-all-start = ((bf16[128,48,128]{2,1,0:T(8,128)(2,1)}), bf16[128,48,128]{2,1,0:T(8,128)(2,1)S(1)}, u32[]{:S(2)}, u32[]{:S(2)}) async-start(bf16[128,48,128]{2,1,0:T(8,128)(2,1)} %bitcast), calls=%async_computation | async-start | bytes 3145728 | tf_op jit(solution)/shard_map/all_to_all | solution.py:264
  16.1 0.1 mul.19
  16.2 0.1 add.39.row_ref
  16.3 0.2 add.42.col_ref
  16.5 1.1 %constant_dynamic-slice_fusion.v_ref = f32[2,256,256]{2,1,0:T(8,128)S(1)} fusion(f32[16,256,256]{2,1,0:T(8,128)} %param.10, s32[]{:T(128)S(6)} %select_n.3), kind=kLoop, calls=%fused_computation.3 | loop fusion | bytes 1048580 | tf_op jit(solution)/shard_map/dynamic_slice | solution.py:270
  17.6 1.0 %copy-done.3 = bf16[512,512]{1,0:T(8,128)(2,1)S(1)} copy-done((bf16[512,512]{1,0:T(8,128)(2,1)S(1)}, bf16[512,512]{1,0:T(8,128)(2,1)}, u32[]{:S(2)}) %copy-start.3) | copy-done | bytes 524312
  18.6 1.0 %copy-done.4 = bf16[512,512]{1,0:T(8,128)(2,1)S(1)} copy-done((bf16[512,512]{1,0:T(8,128)(2,1)S(1)}, bf16[512,512]{1,0:T(8,128)(2,1)}, u32[]{:S(2)}) %copy-start.4) | copy-done | bytes 524312
  19.7 1.0 %copy-done.5 = bf16[512,512]{1,0:T(8,128)(2,1)S(1)} copy-done((bf16[512,512]{1,0:T(8,128)(2,1)S(1)}, bf16[512,512]{1,0:T(8,128)(2,1)}, u32[]{:S(2)}) %copy-start.5) | copy-done | bytes 524312
  20.7 6.0 %shard_map.105 = (bf16[2048,768]{1,0:T(8,128)(2,1)S(1)}, bf16[768,2048]{1,0:T(8,128)(2,1)S(1)}, f32[4,256,128]{2,1,0:T(8,128)S(1)}) custom-call(s32[1,768]{1,0:T(1,128)S(1)} %add.39.row_ref, s32[768,1]{1,0:T(8,128)S(1)} %add.42.col_ref, f32[2,256,256]{2,1,0:T(8,128)S(1)} %constant_dynamic-slice_fusion.v_ref, bf16[512,512]{1,0:T(8,128)(2,1)S(1)} %copy-done.5, ...), custom_call_target="tpu_custom_call" | custom-call | flops 3221225472 | bytes 8919040 | tf_op jit(solution)/shard_map/pallas_call | solution.py:231
  26.7 1.6 %copy-done.6 = bf16[2048,768]{1,0:T(8,128)(2,1)} copy-done((bf16[2048,768]{1,0:T(8,128)(2,1)}, bf16[2048,768]{1,0:T(8,128)(2,1)S(1)}, u32[]{:S(2)}) %copy-start.6) | copy-done | bytes 3145752
  28.4 1.7 %copy-done.8 = bf16[768,2048]{1,0:T(8,128)(2,1)} copy-done((bf16[768,2048]{1,0:T(8,128)(2,1)}, bf16[768,2048]{1,0:T(8,128)(2,1)S(1)}, u32[]{:S(2)}) %copy-start.8) | copy-done | bytes 3145752
  30.0 0.8 copy-done.10
  30.8 10.0 %all-to-all-done = bf16[128,48,128]{2,1,0:T(8,128)(2,1)S(1)} async-done(((bf16[128,48,128]{2,1,0:T(8,128)(2,1)}), bf16[128,48,128]{2,1,0:T(8,128)(2,1)S(1)}, u32[]{:S(2)}, u32[]{:S(2)}) %all-to-all-start) | async-done | bytes 1572896 | tf_op jit(solution)/shard_map/all_to_all | solution.py:264
  40.9 1.9 %copy-done.7 = bf16[2048,768]{1,0:T(8,128)(2,1)S(1)} copy-done((bf16[2048,768]{1,0:T(8,128)(2,1)S(1)}, bf16[2048,768]{1,0:T(8,128)(2,1)}, u32[]{:S(2)}) %copy-start.7) | copy-done | bytes 3145752
  42.8 1.9 %copy-done.9 = bf16[768,2048]{1,0:T(8,128)(2,1)S(1)} copy-done((bf16[768,2048]{1,0:T(8,128)(2,1)S(1)}, bf16[768,2048]{1,0:T(8,128)(2,1)}, u32[]{:S(2)}) %copy-start.9) | copy-done | bytes 3145752
  44.6 1.0 %copy-done.11 = f32[4,256,128]{2,1,0:T(8,128)S(1)} copy-done((f32[4,256,128]{2,1,0:T(8,128)S(1)}, f32[4,256,128]{2,1,0:T(8,128)}, u32[]{:S(2)}) %copy-start.11) | copy-done | bytes 524312
  45.7 14.0 %shard_map.106 = bf16[8,16,56,128]{3,2,1,0:T(8,128)(2,1)S(1)} custom-call(bf16[8,768,128]{2,1,0:T(8,128)(2,1)S(1)} %bitcast.9, bf16[2048,768]{1,0:T(8,128)(2,1)S(1)} %copy-done.7, bf16[768,2048]{1,0:T(8,128)(2,1)S(1)} %copy-done.9, f32[4,256,128]{2,1,0:T(8,128)S(1)} %copy-done.11, bf16[4,256,256]{2,1,0:T(8,128)(2,1)S(1)} %copy-done.2, ...), custom_call_target="tpu_custom_call" | custom-call | flops 6442450944 | bytes 11272192 | tf_op jit(solution)/shard_map/pallas_call | solution.py:231
  59.7 31.7 %all_to_all.10.x_ref = bf16[128,56,128]{2,1,0:T(8,128)(2,1)S(1)} all-to-all(bf16[128,56,128]{2,1,0:T(8,128)(2,1)S(1)} %bitcast.8), channel_id=1, replica_groups=mesh['band'=8,'fft'=16] {'band','fft'}, dimensions={0} | all-to-all | bytes 3670016 | tf_op jit(solution)/shard_map/all_to_all | solution.py:305
  91.4 1.3 %shard_map.107 = (bf16[1536,512]{1,0:T(8,128)(2,1)S(1)}, f32[8,128]{1,0:T(8,128)S(1)}) custom-call(bf16[128,56,128]{2,1,0:T(8,128)(2,1)S(1)} %all_to_all.10.x_ref, bf16[512,512]{1,0:T(8,128)(2,1)S(1)} %copy-done), custom_call_target="tpu_custom_call" | custom-call | flops 805306368 | bytes 3936256 | tf_op jit(solution)/shard_map/pallas_call | solution.py:231
  92.7 1.9 %reshape.93 = bf16[1,24,64,2,256]{4,3,2,1,0:T(2,128)(2,1)} reshape(bf16[1536,512]{1,0:T(8,128)(2,1)S(1)} %get-tuple-element.10) | data formatting | bytes 3145728 | tf_op jit(solution)/shard_map/reshape | solution.py:322
  94.6 0.6 div.6
  (19 shorter events, 0.1 us)
Async XLA Ops:
  0.6 1.8 %copy-start = (bf16[512,512]{1,0:T(8,128)(2,1)S(1)}, bf16[512,512]{1,0:T(8,128)(2,1)}, u32[]{:S(2)}) copy-start(bf16[512,512]{1,0:T(8,128)(2,1)} %constant.28.clone.t_ref.t_hbm) | copy-start | bytes 1572868
  4.9 11.2 %copy-start.12 = (s32[384]{0:T(512)S(1)}, s32[384]{0:T(512)}, u32[]{:S(2)}) copy-start(s32[384]{0:T(512)} %param.11) | copy-start | bytes 4612
  4.9 35.9 %all-to-all-start = ((bf16[128,48,128]{2,1,0:T(8,128)(2,1)}), bf16[128,48,128]{2,1,0:T(8,128)(2,1)S(1)}, u32[]{:S(2)}, u32[]{:S(2)}) async-start(bf16[128,48,128]{2,1,0:T(8,128)(2,1)} %bitcast), calls=%async_computation | async-start | bytes 3145728 | tf_op jit(solution)/shard_map/all_to_all | solution.py:264
  17.6 1.0 %copy-start.3 = (bf16[512,512]{1,0:T(8,128)(2,1)S(1)}, bf16[512,512]{1,0:T(8,128)(2,1)}, u32[]{:S(2)}) copy-start(bf16[512,512]{1,0:T(8,128)(2,1)} %constant.31.clone.ord_ref) | copy-start | bytes 1572868
  18.6 1.0 %copy-start.4 = (bf16[512,512]{1,0:T(8,128)(2,1)S(1)}, bf16[512,512]{1,0:T(8,128)(2,1)}, u32[]{:S(2)}) copy-start(bf16[512,512]{1,0:T(8,128)(2,1)} %constant.30.clone.b_ref) | copy-start | bytes 1572868
  19.7 1.0 %copy-start.5 = (bf16[512,512]{1,0:T(8,128)(2,1)S(1)}, bf16[512,512]{1,0:T(8,128)(2,1)}, u32[]{:S(2)}) copy-start(bf16[512,512]{1,0:T(8,128)(2,1)} %constant.29.clone.f_ref) | copy-start | bytes 1572868
  20.7 20.1 %copy-start.1 = (bf16[4,256,256]{2,1,0:T(8,128)(2,1)S(1)}, bf16[4,256,256]{2,1,0:T(8,128)(2,1)}, u32[]{:S(2)}) copy-start(bf16[4,256,256]{2,1,0:T(8,128)(2,1)} %constant.33.clone.yb_ref) | copy-start | bytes 1572868
  20.7 20.1 %copy-start.2 = (bf16[4,256,256]{2,1,0:T(8,128)(2,1)S(1)}, bf16[4,256,256]{2,1,0:T(8,128)(2,1)}, u32[]{:S(2)}) copy-start(bf16[4,256,256]{2,1,0:T(8,128)(2,1)} %constant.32.clone.yf_ref) | copy-start | bytes 1572868
  26.7 1.6 %copy-start.6 = (bf16[2048,768]{1,0:T(8,128)(2,1)}, bf16[2048,768]{1,0:T(8,128)(2,1)S(1)}, u32[]{:S(2)}) copy-start(bf16[2048,768]{1,0:T(8,128)(2,1)S(1)} %get-tuple-element.7.tx_hbm) | copy-start | bytes 9437188
  28.4 1.7 %copy-start.8 = (bf16[768,2048]{1,0:T(8,128)(2,1)}, bf16[768,2048]{1,0:T(8,128)(2,1)S(1)}, u32[]{:S(2)}) copy-start(bf16[768,2048]{1,0:T(8,128)(2,1)S(1)} %get-tuple-element.8.xt_hbm) | copy-start | bytes 9437188
  30.0 0.8 copy-start.10
  40.9 1.9 %copy-start.7 = (bf16[2048,768]{1,0:T(8,128)(2,1)S(1)}, bf16[2048,768]{1,0:T(8,128)(2,1)}, u32[]{:S(2)}) copy-start(bf16[2048,768]{1,0:T(8,128)(2,1)} %copy-done.6) | copy-start | bytes 9437188
  42.8 1.9 %copy-start.9 = (bf16[768,2048]{1,0:T(8,128)(2,1)S(1)}, bf16[768,2048]{1,0:T(8,128)(2,1)}, u32[]{:S(2)}) copy-start(bf16[768,2048]{1,0:T(8,128)(2,1)} %copy-done.8) | copy-start | bytes 9437188
  44.6 1.0 %copy-start.11 = (f32[4,256,128]{2,1,0:T(8,128)S(1)}, f32[4,256,128]{2,1,0:T(8,128)}, u32[]{:S(2)}) copy-start(f32[4,256,128]{2,1,0:T(8,128)} %copy-done.10) | copy-start | bytes 1572868

commit v3 on v2

--- a/solution.py
+++ b/solution.py
@@ -1,3 +1,4 @@
+import functools
 import math
 
 import jax
@@ -31,7 +32,8 @@
     forward = dft_table(size, 1.0)
     p, b, f = np.meshgrid(np.arange(per_dev), np.arange(bands), np.arange(ffts), indexing="ij")
     z = (f * per_fft + b * per_dev + p).reshape(-1)
-    return np.ascontiguousarray(forward[:, :, :, z].transpose(3, 2, 0, 1)).reshape(2 * size, 2 * size)
+    rows = forward[:, :, :, z].reshape(2, size, 2, per_dev, bands * ffts)
+    return np.ascontiguousarray(rows.transpose(3, 2, 4, 0, 1)).reshape(2 * size, 2 * size)
 
 
 def split_table(size, parts, per_dev):
@@ -65,35 +67,47 @@
 
 def to_planes_kernel(c_ref, t_ref, o_ref, scr):
     half = t_ref.shape[0] // 2
-    blocks = scr.shape[0] // half
+    devices = half // 2
+    rows = scr.shape[0] // devices
+    blocks = rows // 2
     low = lax.broadcasted_iota(jnp.int32, (half, 128), 1) < 64
     for g in range(blocks // 4):
         r = dot_nt(t_ref[...], c_ref[g * 256 : (g + 1) * 256, :])
         for h in range(2):
             a = r[:half, h * 128 : (h + 1) * 128]
             b = r[half:, h * 128 : (h + 1) * 128]
-            m = g * 4 + h * 2
-            scr[pl.ds(m, half, stride=blocks), :] = jnp.where(low, a, pltpu.roll(b, 64, 1))
-            scr[pl.ds(m + 1, half, stride=blocks), :] = jnp.where(low, pltpu.roll(a, 64, 1), b)
+            even = jnp.where(low, a, pltpu.roll(b, 64, 1))
+            odd = jnp.where(low, pltpu.roll(a, 64, 1), b)
+            for d in range(2):
+                at = d * blocks + g * 4 + h * 2
+                part = slice(d * devices, (d + 1) * devices)
+                scr[pl.ds(at, devices, stride=rows), :] = even[part]
+                scr[pl.ds(at + 1, devices, stride=rows), :] = odd[part]
     o_ref[...] = scr[...].astype(BF16)
 
 
-def from_planes_kernel(x_ref, t_hbm, o_ref, m_ref, scr, table, sem):
+def from_planes_kernel(count, x_ref, t_hbm, o_ref, m_ref, scr, table, sem):
     copy = pltpu.make_async_copy(t_hbm, table, sem)
     copy.start()
-    half = t_hbm.shape[0] // 2
-    blocks = scr.shape[0] // half
-    rows = 2 * blocks
-    total = jnp.zeros((8, 128), F32)
-    for i in range(x_ref.shape[0]):
-        scr[i * rows : (i + 1) * rows, :] = x_ref[i, :rows, :].astype(F32)
-        total = total + x_ref[i, rows:, :].astype(F32)
-    m_ref[...] = jnp.broadcast_to(total[0:1] + (total[1:2] + total[2:3]), (8, 128))
+    devices = t_hbm.shape[0] // 4
+    rows = scr.shape[0] // devices
+    blocks = rows // 2 - 1
+    bands = m_ref.shape[2]
+    scr[...] = x_ref[...].astype(F32)
+    line = jnp.sum(scr[pl.ds(2 * blocks, devices, stride=rows), :], axis=0, keepdims=True)
+    width = 2 * bands
+    total = line[:, :width] + (line[:, width : 2 * width] + line[:, 2 * width : 3 * width])
+    total = total / count
+    m_ref[0] = total[:, :bands]
+    m_ref[1] = total[:, bands:]
     copy.wait()
     for g in range(blocks // 4):
         parts = []
         for m in range(g * 4, g * 4 + 4):
-            y = jnp.transpose(scr[pl.ds(m, half, stride=blocks), :]).astype(BF16)
+            y = jnp.concatenate(
+                [scr[pl.ds(d * blocks + m, devices, stride=rows), :] for d in range(2)], axis=0
+            )
+            y = jnp.transpose(y).astype(BF16)
             parts.append(jnp.concatenate([y[:64], y[64:]], axis=1))
         left = jnp.concatenate(parts, axis=0)
         o_ref[g * 256 : (g + 1) * 256, :] = dot(left, table[...]).astype(BF16)
@@ -138,12 +152,14 @@
 
 
 def planes_kernel(
-    r_ref, tx_hbm, xt_hbm, v4_hbm, yf_ref, yb_ref, o_ref, tx, xt, v4, h, r_scr, p_scr, sems
+    groups, r_ref, tx_hbm, xt_hbm, v4_hbm, yf_ref, yb_ref, o_ref, tx, xt, v4, h, r_scr, p_scr, sems
 ):
     size = v4.shape[1]
     bands, count = r_ref.shape[0], r_ref.shape[1]
-    ffts, blocks = o_ref.shape[1], count // (2 * o_ref.shape[1])
-    rows, width = 2 * blocks, 2 * bands
+    ffts = sum(groups)
+    rows, blocks = count // ffts, count // ffts // 2
+    message = p_scr.shape[0] // (bands * ffts)
+    width = 2 * bands
     load_v = pltpu.make_async_copy(v4_hbm, v4, sems.at[5])
     loads = []
     for s in range(4):
@@ -155,13 +171,6 @@
     for copy in loads[1:]:
         copy.start()
     load_xt.start()
-
-    def spread(scr, b, v):
-        for f in range(ffts):
-            for d in range(2):
-                start = (f * 2 + d) * blocks
-                at = pl.ds(f * blocks * width + d * bands + b, blocks, stride=width)
-                scr[at, :] = v[start : start + blocks]
 
     for s in range(4):
         loads[s].wait()
@@ -187,45 +196,48 @@
             h[row : row + size, b * 128 : (b + 1) * 128] = part[:, :128]
             h[row + size : row + 2 * size, b * 128 : (b + 1) * 128] = part[:, 128:]
         for b in range(2 * s, 2 * s + 2):
-            spread(r_scr, b, r_ref[b].astype(F32))
+            r_scr[b * count : (b + 1) * count, :] = r_ref[b].astype(F32)
+
+    def side(scr, start, stride):
+        tiles = []
+        for m in range(blocks):
+            real = scr[pl.ds(start + m, bands, stride=stride), :]
+            imag = scr[pl.ds(start + blocks + m, bands, stride=stride), :]
+            tiles.append(jnp.concatenate([real, imag], axis=0).astype(BF16))
+        return jnp.concatenate(tiles, axis=1)
+
     load_xt.wait()
-    for n in range(bands // 2):
-        out = dot(xt[...], h[:, n * 256 : (n + 1) * 256])
-        for j in range(2):
-            b = 2 * n + j
-            v = out[:, j * 128 : (j + 1) * 128]
-            spread(p_scr, b, v)
-            v = v.astype(BF16)
-            for f in range(ffts):
-                o_ref[b, f, :rows, :] = v[f * rows : (f + 1) * rows]
-
     gram = jnp.zeros((width, width), F32)
-    for f in range(ffts):
-        sides = []
-        for scr in (r_scr, p_scr):
-            v = scr[f * blocks * width : (f + 1) * blocks * width, :].astype(BF16)
-            sides.append(
-                jnp.concatenate([v[m * width : (m + 1) * width] for m in range(blocks)], axis=1)
-            )
-        gram = gram + dot_nt(sides[0], sides[1])
+    first = 0
+    for group in groups:
+        out = dot(xt[first * rows : (first + group) * rows, :], h[...])
+        for f in range(first, first + group):
+            for b in range(bands):
+                at = (b * ffts + f) * message
+                start = (f - first) * rows
+                p_scr[at : at + rows, :] = out[start : start + rows, b * 128 : (b + 1) * 128]
+        for f in range(first, first + group):
+            left = side(r_scr, f * rows, count)
+            gram = gram + dot_nt(left, side(p_scr, f * message, ffts * message))
+        first += group
+
     real = gram[:bands, :bands] + gram[bands:, bands:]
     imag = gram[:bands, bands:] - gram[bands:, :bands]
-    total = jnp.concatenate([real, imag, jnp.zeros((bands, 128 - width), F32)], axis=1)
-    first = total.astype(BF16).astype(F32)
-    second = (total - first).astype(BF16).astype(F32)
-    third = total - first - second
-    line = lax.broadcasted_iota(jnp.int32, (8, 128), 0)
+    total = jnp.concatenate([real, imag], axis=1)
+    high = total.astype(BF16).astype(F32)
+    middle = (total - high).astype(BF16).astype(F32)
+    low = total - high - middle
+    lines = jnp.concatenate([high, middle, low, jnp.zeros((bands, 128 - 3 * width), F32)], axis=1)
+    empty = jnp.zeros((message - rows - 1, 128), F32)
     for b in range(bands):
-        part = jnp.where(
-            line == 0,
-            first[b : b + 1],
-            jnp.where(line == 1, second[b : b + 1], jnp.where(line == 2, third[b : b + 1], 0.0)),
-        ).astype(BF16)
+        part = jnp.concatenate([lines[b : b + 1], empty], axis=0)
         for f in range(ffts):
-            o_ref[b, f, rows:, :] = part
-
-
-def call(kernel, out_shape, scratch, flops, args, in_hbm=(), out_hbm=False):
+            at = (b * ffts + f) * message + rows
+            p_scr[at : at + message - rows, :] = part
+    o_ref[...] = p_scr[...].astype(BF16)
+
+
+def call(kernel, out_shape, scratch, flops, args, in_hbm=(), out_hbm=False, limit=40):
     read = sum(a.size * a.dtype.itemsize for a in args)
     written = sum(s.size * s.dtype.itemsize for s in jax.tree.leaves(out_shape))
     return pl.pallas_call(
@@ -234,7 +246,7 @@
         in_specs=[HBM if i in in_hbm else VMEM for i in range(len(args))],
         out_specs=jax.tree.map(lambda _: HBM if out_hbm else VMEM, out_shape),
         scratch_shapes=scratch,
-        compiler_params=pltpu.CompilerParams(vmem_limit_bytes=40 * 2**20),
+        compiler_params=pltpu.CompilerParams(vmem_limit_bytes=limit * 2**20),
         cost_estimate=pl.CostEstimate(flops=flops, bytes_accessed=read + written, transcendentals=0),
     )(*args)
 
@@ -289,36 +301,39 @@
             jnp.asarray(order_table(size, 4, per_dev)),
         ),
         out_hbm=True,
-    )
-
+        limit=57,
+    )
+
+    message = rows + 2
     picked = call(
-        planes_kernel,
-        shape((bands, ffts, rows + 8, 128), BF16),
+        functools.partial(planes_kernel, (6, 5, 5)),
+        shape((devices * message, 128), BF16),
         held
         + [pltpu.VMEM((8 * size, bands * 128), BF16)]
-        + [pltpu.VMEM((bands * count, 128), F32)] * 2
+        + [pltpu.VMEM((bands * count, 128), F32), pltpu.VMEM((devices * message, 128), F32)]
         + [pltpu.SemaphoreType.DMA((6,))],
         2 * bands * 128 * 2 * 8 * size * count,
         (got, x_table, x_back, v4, jnp.asarray(y_forward), jnp.asarray(y_backward)),
         in_hbm=(1, 2, 3),
+        limit=57,
     )
     returned = lax.all_to_all(
-        picked.reshape(devices, rows + 8, 128), AXES, split_axis=0, concat_axis=0, tiled=True
-    )
-
-    images, sums = call(
-        from_planes_kernel,
-        (shape((sticks, 2 * size), BF16), shape((8, 128), F32)),
+        picked.reshape(devices, message // 2, 2, 128), AXES, split_axis=0, concat_axis=0, tiled=True
+    )
+
+    total_count = block_count * ffts * block_width * size
+    images, matrix_rows = call(
+        functools.partial(from_planes_kernel, total_count),
+        (shape((sticks, 2 * size), BF16), shape((2, 1, bands), F32)),
         [
-            pltpu.VMEM((devices * rows, 128), F32),
+            pltpu.VMEM((devices * message, 128), F32),
             pltpu.VMEM((2 * size, 2 * size), BF16),
             pltpu.SemaphoreType.DMA(()),
         ],
         2 * sticks * (2 * size) ** 2,
-        (returned, table),
+        (returned.reshape(devices * message, 128), table),
         in_hbm=(1,),
     )
-    matrix_rows = sums[0, : 2 * bands].reshape(2, 1, bands) / (block_count * ffts * block_width * size)
     return (images.reshape(coeffs.shape), matrix_rows)
 
 

time: 96.3 us -> 95.2 us (0.989)
  local copies, waits for them, and re-layouts: 17.8 us -> 8.4 us
  Pallas kernels: 23.8 us -> 29.9 us
  waiting for transfers between devices: 10 us -> 13.6 us
  blocking collectives: 31.7 us -> 30.4 us
    unnamed x27 -> x7, local copies, waits for them, and re-layouts: 13.8 us -> 2.94 us
    pallas_call x4, Pallas kernels: 23.8 us -> 29.9 us  [call(): pl.pallas_call(kernel, out_shape=out_shape, in_specs=[HBM if i in in_hbm...]
    all_to_all x1, waiting for transfers between devices: 10 us -> 13.6 us  [body(): lax.all_to_all(sent.reshape(devices, rows, 128), AXES, split_axis=0, conc...]
    add x2, local copies, waits for them, and re-layouts: 0.27 us -> 1.62 us  [body(): pattern.reshape(ffts, 1, block_count) * 2]
    all_to_all x1, blocking collectives: 31.7 us -> 30.4 us  [body(): lax.all_to_all(picked.reshape(devices, message // 2, 2, 128), AXES, split...]
  transfers between devices with their start and end apart: 1 -> 1, of which waited for: 1 -> 1; matrix products, arithmetic and copies ran while one was open for 2% -> 4% of each run, Pallas kernels for 6% -> 8%
where the time goes in v3:
time: 95.2 us; the launch traced here: 94.3 us
  blocking collectives  30.4 us (32%)
  Pallas kernels  29.9 us (31%)
  waiting for transfers between devices  13.6 us (14%)
  starting transfers between devices  11.3 us (12%)
  local copies, waits for them, and re-layouts  8.4 us (9%)
    all_to_all x1, blocking collectives, body(): lax.all_to_all(picked.reshape(devices, message // 2, 2, 128), AXES, split...  30.4 us
    pallas_call x4, Pallas kernels, call(): pl.pallas_call(kernel, out_shape=out_shape, in_specs=[HBM if i in in_hbm...  29.9 us
    all_to_all x1, waiting for transfers between devices, body(): lax.all_to_all(sent.reshape(devices, rows, 128), AXES, split_axis=0, conc...  13.6 us
    all_to_all x1, starting transfers between devices, body(): lax.all_to_all(sent.reshape(devices, rows, 128), AXES, split_axis=0, conc...  11.3 us
    unnamed x7, local copies, waits for them, and re-layouts  2.94 us
  transfers between devices with their start and end apart: 1, of which 1 were waited for; matrix products, arithmetic and copies ran while one was open for 4% of the time, Pallas kernels for 8%

profile of v3, /device:TPU:0, one launch (start us, length us, event | category | flops | bytes accessed | tf_op | source)
XLA Modules:
  0.0 94.3 jit_solution(16266009245258293499)
XLA Ops:
  0.6 0.0 copy-start
  0.6 1.8 %copy.12 = bf16[192,8,2,256]{3,1,2,0:T(8,128)(2,1)S(1)} copy(bf16[192,8,2,256]{3,2,1,0:T(2,128)(2,1)} %bitcast.10) | data formatting | bytes 3145728
  2.4 0.0 copy-done
  2.4 3.0 %shard_map.104 = bf16[6144,128]{1,0:T(8,128)(2,1)} custom-call(bf16[1536,512]{1,0:T(8,128)(2,1)S(1)} %bitcast.7, bf16[512,512]{1,0:T(8,128)(2,1)S(1)} %copy-done), custom_call_target="tpu_custom_call" | custom-call | flops 805306368 | bytes 3670016 | tf_op jit(solution)/shard_map/pallas_call | solution.py:243
  5.4 0.0 copy-start.2
  5.4 11.3 %all-to-all-start = ((bf16[128,48,128]{2,1,0:T(8,128)(2,1)}), bf16[128,48,128]{2,1,0:T(8,128)(2,1)S(1)}, u32[]{:S(2)}, u32[]{:S(2)}) async-start(bf16[128,48,128]{2,1,0:T(8,128)(2,1)} %bitcast), calls=%async_computation | async-start | bytes 3145728 | tf_op jit(solution)/shard_map/all_to_all | solution.py:276
  16.8 0.0 copy-done.2
  16.8 0.1 mul.19
  16.9 0.7 add.39.row_ref
  17.6 0.9 add.42.col_ref
  18.5 1.9 %constant_dynamic-slice_fusion.v_ref = f32[2,256,256]{2,1,0:T(8,128)} fusion(f32[16,256,256]{2,1,0:T(8,128)} %param.10, s32[]{:T(128)S(6)} %select_n.3), kind=kLoop, calls=%fused_computation.2 | loop fusion | bytes 1048580 | tf_op jit(solution)/shard_map/dynamic_slice | solution.py:282
  20.4 7.4 %shard_map.105 = (bf16[2048,768]{1,0:T(8,128)(2,1)}, bf16[768,2048]{1,0:T(8,128)(2,1)}, f32[4,256,128]{2,1,0:T(8,128)}) custom-call(s32[1,768]{1,0:T(1,128)} %add.39.row_ref, s32[768,1]{1,0:T(8,128)} %add.42.col_ref, f32[2,256,256]{2,1,0:T(8,128)} %constant_dynamic-slice_fusion.v_ref, bf16[512,512]{1,0:T(8,128)(2,1)} %constant.26.clone.f_ref, ...), custom_call_target="tpu_custom_call" | custom-call | flops 3221225472 | bytes 8919040 | tf_op jit(solution)/shard_map/pallas_call | solution.py:243
  27.8 13.6 %all-to-all-done = bf16[128,48,128]{2,1,0:T(8,128)(2,1)S(1)} async-done(((bf16[128,48,128]{2,1,0:T(8,128)(2,1)}), bf16[128,48,128]{2,1,0:T(8,128)(2,1)S(1)}, u32[]{:S(2)}, u32[]{:S(2)}) %all-to-all-start) | async-done | bytes 1572896 | tf_op jit(solution)/shard_map/all_to_all | solution.py:276
  41.4 0.0 copy-start.1
  41.4 1.1 %copy-done.1 = bf16[128,48,128]{2,1,0:T(8,128)(2,1)} copy-done((bf16[128,48,128]{2,1,0:T(8,128)(2,1)}, bf16[128,48,128]{2,1,0:T(8,128)(2,1)S(1)}, u32[]{:S(2)}) %copy-start.1) | copy-done | bytes 1572888
  42.5 18.2 %shard_map.106 = bf16[6400,128]{1,0:T(8,128)(2,1)} custom-call(bf16[8,768,128]{2,1,0:T(8,128)(2,1)} %bitcast.11, bf16[2048,768]{1,0:T(8,128)(2,1)} %get-tuple-element.7.tx_hbm, bf16[768,2048]{1,0:T(8,128)(2,1)} %get-tuple-element.8.xt_hbm, f32[4,256,128]{2,1,0:T(8,128)} %get-tuple-element.9.v4_hbm, bf16[4,256,256]{2,1,0:T(8,128)(2,1)} %constant.29.clone.yf_ref, ...), custom_call_target="tpu_custom_call" | custom-call | flops 6442450944 | bytes 11075584 | tf_op jit(solution)/shard_map/pallas_call | solution.py:243
  60.7 30.4 %all_to_all.10 = bf16[128,25,2,128]{3,2,1,0:T(2,128)(2,1)S(1)} all-to-all(bf16[128,25,2,128]{3,2,1,0:T(2,128)(2,1)} %bitcast.9), channel_id=1, replica_groups=mesh['band'=8,'fft'=16] {'band','fft'}, dimensions={0} | all-to-all | bytes 3276800 | tf_op jit(solution)/shard_map/all_to_all | solution.py:320
  91.0 1.4 %shard_map.107 = (bf16[1536,512]{1,0:T(8,128)(2,1)S(1)}, f32[2,1,8]{2,1,0:T(1,128)}) custom-call(bf16[6400,128]{1,0:T(8,128)(2,1)S(1)} %bitcast.8, bf16[512,512]{1,0:T(8,128)(2,1)S(1)} %copy-done), custom_call_target="tpu_custom_call" | custom-call | flops 805306368 | bytes 3735616 | tf_op jit(solution)/shard_map/pallas_call | solution.py:243
  92.4 1.9 %reshape.83 = bf16[1,24,64,2,256]{4,3,2,1,0:T(2,128)(2,1)} reshape(bf16[1536,512]{1,0:T(8,128)(2,1)S(1)} %get-tuple-element.10) | data formatting | bytes 3145728 | tf_op jit(solution)/shard_map/reshape | solution.py:337
  (2 shorter events, 0.0 us)
Async XLA Ops:
  0.6 1.8 %copy-start = (bf16[512,512]{1,0:T(8,128)(2,1)S(1)}, bf16[512,512]{1,0:T(8,128)(2,1)}, u32[]{:S(2)}) copy-start(bf16[512,512]{1,0:T(8,128)(2,1)} %constant.25.clone.t_ref.t_hbm) | copy-start | bytes 1572868
  5.4 11.3 %copy-start.2 = (s32[384]{0:T(512)S(1)}, s32[384]{0:T(512)}, u32[]{:S(2)}) copy-start(s32[384]{0:T(512)} %param.11) | copy-start | bytes 4612
  5.4 35.9 %all-to-all-start = ((bf16[128,48,128]{2,1,0:T(8,128)(2,1)}), bf16[128,48,128]{2,1,0:T(8,128)(2,1)S(1)}, u32[]{:S(2)}, u32[]{:S(2)}) async-start(bf16[128,48,128]{2,1,0:T(8,128)(2,1)} %bitcast), calls=%async_computation | async-start | bytes 3145728 | tf_op jit(solution)/shard_map/all_to_all | solution.py:276
  41.4 1.1 %copy-start.1 = (bf16[128,48,128]{2,1,0:T(8,128)(2,1)}, bf16[128,48,128]{2,1,0:T(8,128)(2,1)S(1)}, u32[]{:S(2)}) copy-start(bf16[128,48,128]{2,1,0:T(8,128)(2,1)S(1)} %all-to-all-done) | copy-start | bytes 4718596

commit v4 on v3

--- a/solution.py
+++ b/solution.py
@@ -152,13 +152,15 @@
 
 
 def planes_kernel(
-    groups, r_ref, tx_hbm, xt_hbm, v4_hbm, yf_ref, yb_ref, o_ref, tx, xt, v4, h, r_scr, p_scr, sems
+    groups, r_ref, tx_hbm, xt_hbm, v4_hbm, yf_ref, yb_ref, o_ref,
+    tx, xt, v4, h, r_scr, p_scr, left_scr, right_scr, sems,
 ):
     size = v4.shape[1]
     bands, count = r_ref.shape[0], r_ref.shape[1]
     ffts = sum(groups)
     rows, blocks = count // ffts, count // ffts // 2
-    message = p_scr.shape[0] // (bands * ffts)
+    message = o_ref.shape[0] // (bands * ffts)
+    pitch = p_scr.shape[0] // bands
     width = 2 * bands
     load_v = pltpu.make_async_copy(v4_hbm, v4, sems.at[5])
     loads = []
@@ -171,11 +173,19 @@
     for copy in loads[1:]:
         copy.start()
     load_xt.start()
+    for b in range(bands):
+        r_scr[b * count : (b + 1) * count, :] = r_ref[b].astype(F32)
+
+    def side(scr, start, stride):
+        tiles = []
+        for m in range(blocks):
+            real = scr[pl.ds(start + m, bands, stride=stride), :]
+            imag = scr[pl.ds(start + blocks + m, bands, stride=stride), :]
+            tiles.append(jnp.concatenate([real, imag], axis=0).astype(BF16))
+        return jnp.concatenate(tiles, axis=1)
 
     for s in range(4):
         loads[s].wait()
-        if s == 0:
-            load_v.wait()
         w = jnp.concatenate([r_ref[b] for b in range(bands)], axis=1)
         g = dot(tx[s * 2 * size : (s + 1) * 2 * size, :], w).astype(BF16)
         left = jnp.concatenate(
@@ -187,6 +197,10 @@
             ],
             axis=0,
         )
+        if s == 0:
+            load_v.wait()
+        for f in range(s * ffts // 4, (s + 1) * ffts // 4):
+            left_scr[f * width : (f + 1) * width, :] = side(r_scr, f * rows, count)
         v = jnp.concatenate([v4[s], v4[s]], axis=1)
         field = (dot(left, yf_ref[s]) * jnp.concatenate([v] * bands, axis=0)).astype(BF16)
         back = dot(field, yb_ref[s]).astype(BF16)
@@ -195,56 +209,75 @@
             part = back[b * size : (b + 1) * size]
             h[row : row + size, b * 128 : (b + 1) * 128] = part[:, :128]
             h[row + size : row + 2 * size, b * 128 : (b + 1) * 128] = part[:, 128:]
-        for b in range(2 * s, 2 * s + 2):
-            r_scr[b * count : (b + 1) * count, :] = r_ref[b].astype(F32)
-
-    def side(scr, start, stride):
-        tiles = []
-        for m in range(blocks):
-            real = scr[pl.ds(start + m, bands, stride=stride), :]
-            imag = scr[pl.ds(start + blocks + m, bands, stride=stride), :]
-            tiles.append(jnp.concatenate([real, imag], axis=0).astype(BF16))
-        return jnp.concatenate(tiles, axis=1)
 
     load_xt.wait()
-    gram = jnp.zeros((width, width), F32)
+    ready = []
+
+    def pack(f):
+        right_scr[f * width : (f + 1) * width, :] = side(p_scr, f * message, pitch)
+
+    def products(sources):
+        part = slice(sources[0] * width, (sources[-1] + 1) * width)
+        square = dot_nt(left_scr[part, :], right_scr[part, :])
+        block = lax.broadcasted_iota(jnp.int32, square.shape, 0) // width
+        same = block == lax.broadcasted_iota(jnp.int32, square.shape, 1) // width
+        square = jnp.where(same, square, 0.0)
+        total = sum(square[f * width : (f + 1) * width] for f in range(len(sources)))
+        return jnp.concatenate([total, jnp.zeros((width, 128 - total.shape[1]), F32)], axis=1)
+
+    gram = jnp.zeros((width, 128), F32)
     first = 0
     for group in groups:
-        out = dot(xt[first * rows : (first + group) * rows, :], h[...])
-        for f in range(first, first + group):
-            for b in range(bands):
-                at = (b * ffts + f) * message
-                start = (f - first) * rows
-                p_scr[at : at + rows, :] = out[start : start + rows, b * 128 : (b + 1) * 128]
-        for f in range(first, first + group):
-            left = side(r_scr, f * rows, count)
-            gram = gram + dot_nt(left, side(p_scr, f * message, ffts * message))
+        for n in range(bands // 2):
+            if n < 2:
+                for f in ready[n::2]:
+                    pack(f)
+            if n == 2 and ready:
+                gram = gram + products(ready)
+            out = dot(xt[first * rows : (first + group) * rows, :], h[:, n * 256 : (n + 1) * 256])
+            for f in range(group):
+                for j in range(2):
+                    at = (2 * n + j) * pitch + (first + f) * message
+                    part = out[f * rows : (f + 1) * rows, j * 128 : (j + 1) * 128]
+                    p_scr[at : at + rows, :] = part
+        ready = list(range(first, first + group))
         first += group
-
-    real = gram[:bands, :bands] + gram[bands:, bands:]
-    imag = gram[:bands, bands:] - gram[bands:, :bands]
-    total = jnp.concatenate([real, imag], axis=1)
+    for f in ready:
+        pack(f)
+    band = ffts * message
+    for b in range(bands):
+        o_ref[b * band : (b + 1) * band, :] = p_scr[b * pitch : b * pitch + band, :].astype(BF16)
+    gram = gram + products(ready)
+    for shift in (64, 32, 16):
+        gram = gram + pltpu.roll(gram, shift, 1)
+    lane = lax.broadcasted_iota(jnp.int32, (bands, 128), 1)
+    turned = pltpu.roll(gram[bands:], bands, 1)
+    total = gram[:bands] + jnp.where(lane % width < bands, turned, -turned)
     high = total.astype(BF16).astype(F32)
     middle = (total - high).astype(BF16).astype(F32)
     low = total - high - middle
-    lines = jnp.concatenate([high, middle, low, jnp.zeros((bands, 128 - 3 * width), F32)], axis=1)
-    empty = jnp.zeros((message - rows - 1, 128), F32)
+    lines = jnp.where(lane < width, high, jnp.where(lane < 2 * width, middle, low))
+    lines = jnp.where(lane < 3 * width, lines, 0.0)
     for b in range(bands):
-        part = jnp.concatenate([lines[b : b + 1], empty], axis=0)
+        part = jnp.broadcast_to(lines[b : b + 1], (message - rows, 128)).astype(BF16)
         for f in range(ffts):
             at = (b * ffts + f) * message + rows
-            p_scr[at : at + message - rows, :] = part
-    o_ref[...] = p_scr[...].astype(BF16)
+            o_ref[at : at + message - rows, :] = part
 
 
 def call(kernel, out_shape, scratch, flops, args, in_hbm=(), out_hbm=False, limit=40):
     read = sum(a.size * a.dtype.itemsize for a in args)
-    written = sum(s.size * s.dtype.itemsize for s in jax.tree.leaves(out_shape))
+    outs = jax.tree.leaves(out_shape, is_leaf=lambda s: hasattr(s, "shape"))
+    written = sum(math.prod(s.shape) * jnp.dtype(s.dtype).itemsize for s in outs)
+    args = [
+        pltpu.with_memory_space_constraint(a, pltpu.HBM) if i in in_hbm else a
+        for i, a in enumerate(args)
+    ]
     return pl.pallas_call(
         kernel,
         out_shape=out_shape,
         in_specs=[HBM if i in in_hbm else VMEM for i in range(len(args))],
-        out_specs=jax.tree.map(lambda _: HBM if out_hbm else VMEM, out_shape),
+        out_specs=[HBM if out_hbm else VMEM] * len(outs) if isinstance(out_shape, tuple) else VMEM,
         scratch_shapes=scratch,
         compiler_params=pltpu.CompilerParams(vmem_limit_bytes=limit * 2**20),
         cost_estimate=pl.CostEstimate(flops=flops, bytes_accessed=read + written, transcendentals=0),
@@ -282,9 +315,9 @@
     planes = lax.dynamic_slice_in_dim(potential, lax.axis_index("band") * per_dev, per_dev, 0)
     count = ffts * rows
     tables = (
-        shape((8 * size, count), BF16),
-        shape((count, 8 * size), BF16),
-        shape((4, size, per_dev * size // 4), F32),
+        pltpu.HBM((8 * size, count), BF16),
+        pltpu.HBM((count, 8 * size), BF16),
+        pltpu.HBM((4, size, per_dev * size // 4), F32),
     )
     held = [pltpu.VMEM(t.shape, t.dtype) for t in tables]
     x_table, x_back, v4 = call(
@@ -301,21 +334,24 @@
             jnp.asarray(order_table(size, 4, per_dev)),
         ),
         out_hbm=True,
-        limit=57,
     )
 
     message = rows + 2
     picked = call(
-        functools.partial(planes_kernel, (6, 5, 5)),
+        functools.partial(planes_kernel, (6, 6, 4)),
         shape((devices * message, 128), BF16),
         held
-        + [pltpu.VMEM((8 * size, bands * 128), BF16)]
-        + [pltpu.VMEM((bands * count, 128), F32), pltpu.VMEM((devices * message, 128), F32)]
-        + [pltpu.SemaphoreType.DMA((6,))],
+        + [
+            pltpu.VMEM((8 * size, bands * 128), BF16),
+            pltpu.VMEM((bands * count, 128), F32),
+            pltpu.VMEM((devices * message + 8 * bands, 128), F32),
+            pltpu.VMEM((ffts * 2 * bands, block_count * 128), BF16),
+            pltpu.VMEM((ffts * 2 * bands, block_count * 128), BF16),
+            pltpu.SemaphoreType.DMA((6,)),
+        ],
         2 * bands * 128 * 2 * 8 * size * count,
         (got, x_table, x_back, v4, jnp.asarray(y_forward), jnp.asarray(y_backward)),
         in_hbm=(1, 2, 3),
-        limit=57,
     )
     returned = lax.all_to_all(
         picked.reshape(devices, message // 2, 2, 128), AXES, split_axis=0, concat_axis=0, tiled=True

time: 95.2 us -> 90.6 us (0.952)
  Pallas kernels: 29.9 us -> 25.6 us
  waiting for transfers between devices: 13.6 us -> 15.2 us
  local copies, waits for them, and re-layouts: 8.4 us -> 7.17 us
    pallas_call x4, Pallas kernels: 29.9 us -> 25.6 us  [call(): pl.pallas_call(kernel, out_shape=out_shape, in_specs=[HBM if i in in_hbm...]
    all_to_all x1, waiting for transfers between devices: 13.6 us -> 15.2 us  [body(): lax.all_to_all(sent.reshape(devices, rows, 128), AXES, split_axis=0, conc...]
    add x2, local copies, waits for them, and re-layouts: 1.62 us -> 0.27 us  [body(): pattern.reshape(ffts, 1, block_count) * 2]
    unnamed x7 -> x15, local copies, waits for them, and re-layouts: 2.94 us -> 3.89 us
  transfers between devices with their start and end apart: 1 -> 1, of which waited for: 1 -> 1; matrix products, arithmetic and copies ran while one was open for 4% -> 2% of each run, Pallas kernels for 8% -> 6%
where the time goes in v4:
time: 90.6 us; the launch traced here: 89.6 us
  blocking collectives  29.6 us (33%)
  Pallas kernels  25.6 us (28%)
  waiting for transfers between devices  15.2 us (17%)
  starting transfers between devices  11.3 us (12%)
  local copies, waits for them, and re-layouts  7.17 us (8%)
    all_to_all x1, blocking collectives, body(): lax.all_to_all(picked.reshape(devices, message // 2, 2, 128), AXES, split...  29.6 us
    pallas_call x4, Pallas kernels, call(): pl.pallas_call(kernel, out_shape=out_shape, in_specs=[HBM if i in in_hbm...  25.6 us
    all_to_all x1, waiting for transfers between devices, body(): lax.all_to_all(sent.reshape(devices, rows, 128), AXES, split_axis=0, conc...  15.2 us
    all_to_all x1, starting transfers between devices, body(): lax.all_to_all(sent.reshape(devices, rows, 128), AXES, split_axis=0, conc...  11.3 us
    unnamed x15, local copies, waits for them, and re-layouts  3.89 us
    reshape x1, local copies, waits for them, and re-layouts, body(): return (images.reshape(coeffs.shape), matrix_rows)  1.85 us
  transfers between devices with their start and end apart: 1, of which 1 were waited for; matrix products, arithmetic and copies ran while one was open for 2% of the time, Pallas kernels for 6%

profile of v4, /device:TPU:0, one launch (start us, length us, event | category | flops | bytes accessed | tf_op | source)
XLA Modules:
  0.0 89.6 jit_solution(7114388756073709653)
XLA Ops:
  0.6 0.0 copy-start
  0.6 1.8 %copy.12 = bf16[192,8,2,256]{3,1,2,0:T(8,128)(2,1)S(1)} copy(bf16[192,8,2,256]{3,2,1,0:T(2,128)(2,1)} %bitcast.11) | data formatting | bytes 3145728
  2.4 0.0 copy-done
  2.4 3.0 %shard_map.104 = bf16[6144,128]{1,0:T(8,128)(2,1)} custom-call(bf16[1536,512]{1,0:T(8,128)(2,1)S(1)} %bitcast.7, bf16[512,512]{1,0:T(8,128)(2,1)S(1)} %copy-done), custom_call_target="tpu_custom_call" | custom-call | flops 805306368 | bytes 3670016 | tf_op jit(solution)/shard_map/pallas_call | solution.py:276
  5.4 0.0 copy-start.6
  5.4 0.0 copy-start.3
  5.4 11.3 %all-to-all-start = ((bf16[128,48,128]{2,1,0:T(8,128)(2,1)}), bf16[128,48,128]{2,1,0:T(8,128)(2,1)S(1)}, u32[]{:S(2)}, u32[]{:S(2)}) async-start(bf16[128,48,128]{2,1,0:T(8,128)(2,1)} %bitcast), calls=%async_computation | async-start | bytes 3145728 | tf_op jit(solution)/shard_map/all_to_all | solution.py:309
  16.8 0.0 copy-done.6
  16.8 0.1 mul.19
  16.9 0.1 add.39.row_ref
  17.0 0.2 add.42.col_ref
  17.2 1.1 %constant_dynamic-slice_fusion.v_ref = f32[2,256,256]{2,1,0:T(8,128)S(1)} fusion(f32[16,256,256]{2,1,0:T(8,128)} %param.10, s32[]{:T(128)S(6)} %select_n.3), kind=kLoop, calls=%fused_computation.2 | loop fusion | bytes 1048580 | tf_op jit(solution)/shard_map/dynamic_slice | solution.py:315
  18.3 0.0 copy-done.3
  18.3 0.0 copy-start.4
  18.3 1.0 %copy-done.4 = bf16[512,512]{1,0:T(8,128)(2,1)S(1)} copy-done((bf16[512,512]{1,0:T(8,128)(2,1)S(1)}, bf16[512,512]{1,0:T(8,128)(2,1)}, u32[]{:S(2)}) %copy-start.4) | copy-done | bytes 524312
  19.3 1.0 %copy-done.5 = bf16[512,512]{1,0:T(8,128)(2,1)S(1)} copy-done((bf16[512,512]{1,0:T(8,128)(2,1)S(1)}, bf16[512,512]{1,0:T(8,128)(2,1)}, u32[]{:S(2)}) %copy-start.5) | copy-done | bytes 524312
  20.4 5.7 %shard_map.105 = (bf16[2048,768]{1,0:T(8,128)(2,1)}, bf16[768,2048]{1,0:T(8,128)(2,1)}, f32[4,256,128]{2,1,0:T(8,128)}) custom-call(s32[1,768]{1,0:T(1,128)S(1)} %add.39.row_ref, s32[768,1]{1,0:T(8,128)S(1)} %add.42.col_ref, f32[2,256,256]{2,1,0:T(8,128)S(1)} %constant_dynamic-slice_fusion.v_ref, bf16[512,512]{1,0:T(8,128)(2,1)S(1)} %copy-done.5, ...), custom_call_target="tpu_custom_call" | custom-call | flops 3221225472 | bytes 8919040 | tf_op jit(solution)/shard_map/pallas_call | solution.py:276
  26.1 15.2 %all-to-all-done = bf16[128,48,128]{2,1,0:T(8,128)(2,1)S(1)} async-done(((bf16[128,48,128]{2,1,0:T(8,128)(2,1)}), bf16[128,48,128]{2,1,0:T(8,128)(2,1)S(1)}, u32[]{:S(2)}, u32[]{:S(2)}) %all-to-all-start) | async-done | bytes 1572896 | tf_op jit(solution)/shard_map/all_to_all | solution.py:309
  41.4 0.0 copy-done.1
  41.4 0.0 copy-done.2
  41.4 14.7 %shard_map.106 = bf16[6400,128]{1,0:T(8,128)(2,1)S(1)} custom-call(bf16[8,768,128]{2,1,0:T(8,128)(2,1)S(1)} %bitcast.10, bf16[2048,768]{1,0:T(8,128)(2,1)} %get-tuple-element.7.tx_hbm, bf16[768,2048]{1,0:T(8,128)(2,1)} %get-tuple-element.8.xt_hbm, f32[4,256,128]{2,1,0:T(8,128)} %get-tuple-element.9.v4_hbm, bf16[4,256,256]{2,1,0:T(8,128)(2,1)S(1)} %copy-done.2, ...), custom_call_target="tpu_custom_call" | custom-call | flops 6442450944 | bytes 11075584 | tf_op jit(solution)/shard_map/pallas_call | solution.py:276
  56.1 29.6 %all_to_all.10 = bf16[128,25,2,128]{3,2,1,0:T(2,128)(2,1)S(1)} all-to-all(bf16[128,25,2,128]{3,2,1,0:T(2,128)(2,1)S(1)} %bitcast.8), channel_id=1, replica_groups=mesh['band'=8,'fft'=16] {'band','fft'}, dimensions={0} | all-to-all | bytes 3276800 | tf_op jit(solution)/shard_map/all_to_all | solution.py:356
  85.6 2.1 %shard_map.107 = (bf16[1536,512]{1,0:T(8,128)(2,1)S(1)}, f32[2,1,8]{2,1,0:T(1,128)}) custom-call(bf16[6400,128]{1,0:T(8,128)(2,1)S(1)} %bitcast.9, bf16[512,512]{1,0:T(8,128)(2,1)} %constant.25.clone.t_ref.t_hbm), custom_call_target="tpu_custom_call" | custom-call | flops 805306368 | bytes 3735616 | tf_op jit(solution)/shard_map/pallas_call | solution.py:276
  87.8 1.9 %reshape.83 = bf16[1,24,64,2,256]{4,3,2,1,0:T(2,128)(2,1)} reshape(bf16[1536,512]{1,0:T(8,128)(2,1)S(1)} %get-tuple-element.10) | data formatting | bytes 3145728 | tf_op jit(solution)/shard_map/reshape | solution.py:373
  (5 shorter events, 0.0 us)
Async XLA Ops:
  0.6 1.8 %copy-start = (bf16[512,512]{1,0:T(8,128)(2,1)S(1)}, bf16[512,512]{1,0:T(8,128)(2,1)}, u32[]{:S(2)}) copy-start(bf16[512,512]{1,0:T(8,128)(2,1)} %constant.25.clone.t_ref.t_hbm) | copy-start | bytes 1572868
  5.4 11.3 %copy-start.6 = (s32[384]{0:T(512)S(1)}, s32[384]{0:T(512)}, u32[]{:S(2)}) copy-start(s32[384]{0:T(512)} %param.11) | copy-start | bytes 4612
  5.4 12.8 %copy-start.3 = (bf16[512,512]{1,0:T(8,128)(2,1)S(1)}, bf16[512,512]{1,0:T(8,128)(2,1)}, u32[]{:S(2)}) copy-start(bf16[512,512]{1,0:T(8,128)(2,1)} %constant.28.clone.ord_ref) | copy-start | bytes 1572868
  5.4 35.9 %all-to-all-start = ((bf16[128,48,128]{2,1,0:T(8,128)(2,1)}), bf16[128,48,128]{2,1,0:T(8,128)(2,1)S(1)}, u32[]{:S(2)}, u32[]{:S(2)}) async-start(bf16[128,48,128]{2,1,0:T(8,128)(2,1)} %bitcast), calls=%async_computation | async-start | bytes 3145728 | tf_op jit(solution)/shard_map/all_to_all | solution.py:309
  18.3 1.0 %copy-start.4 = (bf16[512,512]{1,0:T(8,128)(2,1)S(1)}, bf16[512,512]{1,0:T(8,128)(2,1)}, u32[]{:S(2)}) copy-start(bf16[512,512]{1,0:T(8,128)(2,1)} %constant.27.clone.b_ref) | copy-start | bytes 1572868
  19.3 1.0 %copy-start.5 = (bf16[512,512]{1,0:T(8,128)(2,1)S(1)}, bf16[512,512]{1,0:T(8,128)(2,1)}, u32[]{:S(2)}) copy-start(bf16[512,512]{1,0:T(8,128)(2,1)} %constant.26.clone.f_ref) | copy-start | bytes 1572868
  20.4 21.0 %copy-start.1 = (bf16[4,256,256]{2,1,0:T(8,128)(2,1)S(1)}, bf16[4,256,256]{2,1,0:T(8,128)(2,1)}, u32[]{:S(2)}) copy-start(bf16[4,256,256]{2,1,0:T(8,128)(2,1)} %constant.30.clone.yb_ref) | copy-start | bytes 1572868
  20.4 21.0 %copy-start.2 = (bf16[4,256,256]{2,1,0:T(8,128)(2,1)S(1)}, bf16[4,256,256]{2,1,0:T(8,128)(2,1)}, u32[]{:S(2)}) copy-start(bf16[4,256,256]{2,1,0:T(8,128)(2,1)} %constant.29.clone.yf_ref) | copy-start | bytes 1572868

commit v5 on v4

--- a/solution.py
+++ b/solution.py
@@ -66,30 +66,23 @@
 
 
 def to_planes_kernel(c_ref, t_ref, o_ref, scr):
-    half = t_ref.shape[0] // 2
+    half = t_ref.shape[1] // 2
     devices = half // 2
     rows = scr.shape[0] // devices
     blocks = rows // 2
-    low = lax.broadcasted_iota(jnp.int32, (half, 128), 1) < 64
     for g in range(blocks // 4):
-        r = dot_nt(t_ref[...], c_ref[g * 256 : (g + 1) * 256, :])
-        for h in range(2):
-            a = r[:half, h * 128 : (h + 1) * 128]
-            b = r[half:, h * 128 : (h + 1) * 128]
-            even = jnp.where(low, a, pltpu.roll(b, 64, 1))
-            odd = jnp.where(low, pltpu.roll(a, 64, 1), b)
+        r = dot(c_ref[g * 256 : (g + 1) * 256, :], t_ref[...])
+        for i in range(4):
+            part = r[i * 64 : (i + 1) * 64]
+            part = jnp.transpose(jnp.concatenate([part[:, :half], part[:, half:]], axis=0))
             for d in range(2):
-                at = d * blocks + g * 4 + h * 2
-                part = slice(d * devices, (d + 1) * devices)
-                scr[pl.ds(at, devices, stride=rows), :] = even[part]
-                scr[pl.ds(at + 1, devices, stride=rows), :] = odd[part]
+                at = pl.ds(d * blocks + g * 4 + i, devices, stride=rows)
+                scr[at, :] = part[d * devices : (d + 1) * devices]
     o_ref[...] = scr[...].astype(BF16)
 
 
-def from_planes_kernel(count, x_ref, t_hbm, o_ref, m_ref, scr, table, sem):
-    copy = pltpu.make_async_copy(t_hbm, table, sem)
-    copy.start()
-    devices = t_hbm.shape[0] // 4
+def from_planes_kernel(count, x_ref, t_ref, o_ref, m_ref, scr):
+    devices = t_ref.shape[0] // 4
     rows = scr.shape[0] // devices
     blocks = rows // 2 - 1
     bands = m_ref.shape[2]
@@ -100,7 +93,6 @@
     total = total / count
     m_ref[0] = total[:, :bands]
     m_ref[1] = total[:, bands:]
-    copy.wait()
     for g in range(blocks // 4):
         parts = []
         for m in range(g * 4, g * 4 + 4):
@@ -110,7 +102,7 @@
             y = jnp.transpose(y).astype(BF16)
             parts.append(jnp.concatenate([y[:64], y[64:]], axis=1))
         left = jnp.concatenate(parts, axis=0)
-        o_ref[g * 256 : (g + 1) * 256, :] = dot(left, table[...]).astype(BF16)
+        o_ref[g * 256 : (g + 1) * 256, :] = dot(left, t_ref[...]).astype(BF16)
 
 
 def prepare_kernel(
@@ -294,7 +286,7 @@
     rows = 2 * block_count
     shape = jax.ShapeDtypeStruct
 
-    table = jnp.asarray(plane_table(size, bands, ffts))
+    table = plane_table(size, bands, ffts)
     forward = dft_table(size, 1.0).reshape(2 * size, 2 * size)
     y_forward = split_table(size, 4, per_dev)
     y_backward = np.ascontiguousarray(y_forward.transpose(0, 2, 1))
@@ -304,7 +296,7 @@
         shape((devices * rows, 128), BF16),
         [pltpu.VMEM((devices * rows, 128), F32)],
         2 * sticks * (2 * size) ** 2,
-        (coeffs.reshape(sticks, 2 * size), table),
+        (coeffs.reshape(sticks, 2 * size), jnp.asarray(np.ascontiguousarray(table.T))),
     )
     got = lax.all_to_all(
         sent.reshape(devices, rows, 128), AXES, split_axis=0, concat_axis=0, tiled=True
@@ -361,14 +353,9 @@
     images, matrix_rows = call(
         functools.partial(from_planes_kernel, total_count),
         (shape((sticks, 2 * size), BF16), shape((2, 1, bands), F32)),
-        [
-            pltpu.VMEM((devices * message, 128), F32),
-            pltpu.VMEM((2 * size, 2 * size), BF16),
-            pltpu.SemaphoreType.DMA(()),
-        ],
+        [pltpu.VMEM((devices * message, 128), F32)],
         2 * sticks * (2 * size) ** 2,
-        (returned.reshape(devices * message, 128), table),
-        in_hbm=(1,),
+        (returned.reshape(devices * message, 128), jnp.asarray(table)),
     )
     return (images.reshape(coeffs.shape), matrix_rows)
 

time: 90.6 us -> 89.8 us (level)
    unnamed x15 -> x17, local copies, waits for them, and re-layouts: 3.89 us -> 3.9 us
where the time goes in v5:
time: 89.8 us; the launch traced here: 88.9 us
  blocking collectives  29.6 us (33%)
  Pallas kernels  24.8 us (28%)
  waiting for transfers between devices  15.2 us (17%)
  starting transfers between devices  11.3 us (13%)
  local copies, waits for them, and re-layouts  7.16 us (8%)
    all_to_all x1, blocking collectives, body(): lax.all_to_all(picked.reshape(devices, message // 2, 2, 128), AXES, split...  29.6 us
    pallas_call x4, Pallas kernels, call(): pl.pallas_call(kernel, out_shape=out_shape, in_specs=[HBM if i in in_hbm...  24.8 us
    all_to_all x1, waiting for transfers between devices, body(): lax.all_to_all(sent.reshape(devices, rows, 128), AXES, split_axis=0, conc...  15.2 us
    all_to_all x1, starting transfers between devices, body(): lax.all_to_all(sent.reshape(devices, rows, 128), AXES, split_axis=0, conc...  11.3 us
    unnamed x17, local copies, waits for them, and re-layouts  3.9 us
    reshape x1, local copies, waits for them, and re-layouts, body(): return (images.reshape(coeffs.shape), matrix_rows)  1.83 us
  transfers between devices with their start and end apart: 1, of which 1 were waited for; matrix products, arithmetic and copies ran while one was open for 2% of the time, Pallas kernels for 6%

profile of v5, /device:TPU:0, one launch (start us, length us, event | category | flops | bytes accessed | tf_op | source)
XLA Modules:
  0.0 88.9 jit_solution(16273200523488165935)
XLA Ops:
  0.6 0.0 copy-start
  0.6 1.8 %copy.13 = bf16[192,8,2,256]{3,1,2,0:T(8,128)(2,1)S(1)} copy(bf16[192,8,2,256]{3,2,1,0:T(2,128)(2,1)} %bitcast.11) | data formatting | bytes 3145728
  2.4 0.0 copy-done
  2.4 2.7 %shard_map.113 = bf16[6144,128]{1,0:T(8,128)(2,1)} custom-call(bf16[1536,512]{1,0:T(8,128)(2,1)S(1)} %bitcast.7, bf16[512,512]{1,0:T(8,128)(2,1)S(1)} %copy-done), custom_call_target="tpu_custom_call" | custom-call | flops 805306368 | bytes 3670016 | tf_op jit(solution)/shard_map/pallas_call | solution.py:268
  5.2 11.3 %all-to-all-start = ((bf16[128,48,128]{2,1,0:T(8,128)(2,1)}), bf16[128,48,128]{2,1,0:T(8,128)(2,1)S(1)}, u32[]{:S(2)}, u32[]{:S(2)}) async-start(bf16[128,48,128]{2,1,0:T(8,128)(2,1)} %bitcast), calls=%async_computation | async-start | bytes 3145728 | tf_op jit(solution)/shard_map/all_to_all | solution.py:301
  16.5 0.0 copy-done.7
  16.5 0.1 mul.19
  16.6 0.1 add.39.row_ref
  16.7 0.2 add.42.col_ref
  16.9 1.1 %constant_dynamic-slice_fusion.v_ref = f32[2,256,256]{2,1,0:T(8,128)S(1)} fusion(f32[16,256,256]{2,1,0:T(8,128)} %param.11, s32[]{:T(128)S(6)} %select_n.3), kind=kLoop, calls=%fused_computation.2 | loop fusion | bytes 1048580 | tf_op jit(solution)/shard_map/dynamic_slice | solution.py:307
  18.0 0.0 copy-done.4
  18.0 0.0 copy-start.5
  18.0 1.0 %copy-done.5 = bf16[512,512]{1,0:T(8,128)(2,1)S(1)} copy-done((bf16[512,512]{1,0:T(8,128)(2,1)S(1)}, bf16[512,512]{1,0:T(8,128)(2,1)}, u32[]{:S(2)}) %copy-start.5) | copy-done | bytes 524312
  19.0 1.0 %copy-done.6 = bf16[512,512]{1,0:T(8,128)(2,1)S(1)} copy-done((bf16[512,512]{1,0:T(8,128)(2,1)S(1)}, bf16[512,512]{1,0:T(8,128)(2,1)}, u32[]{:S(2)}) %copy-start.6) | copy-done | bytes 524312
  20.1 5.8 %shard_map.114 = (bf16[2048,768]{1,0:T(8,128)(2,1)}, bf16[768,2048]{1,0:T(8,128)(2,1)}, f32[4,256,128]{2,1,0:T(8,128)}) custom-call(s32[1,768]{1,0:T(1,128)S(1)} %add.39.row_ref, s32[768,1]{1,0:T(8,128)S(1)} %add.42.col_ref, f32[2,256,256]{2,1,0:T(8,128)S(1)} %constant_dynamic-slice_fusion.v_ref, bf16[512,512]{1,0:T(8,128)(2,1)S(1)} %copy-done.6, ...), custom_call_target="tpu_custom_call" | custom-call | flops 3221225472 | bytes 8919040 | tf_op jit(solution)/shard_map/pallas_call | solution.py:268
  25.9 15.2 %all-to-all-done = bf16[128,48,128]{2,1,0:T(8,128)(2,1)S(1)} async-done(((bf16[128,48,128]{2,1,0:T(8,128)(2,1)}), bf16[128,48,128]{2,1,0:T(8,128)(2,1)S(1)}, u32[]{:S(2)}, u32[]{:S(2)}) %all-to-all-start) | async-done | bytes 1572896 | tf_op jit(solution)/shard_map/all_to_all | solution.py:301
  41.1 0.0 copy-done.2
  41.1 0.0 copy-done.3
  41.1 14.7 %shard_map.115 = bf16[6400,128]{1,0:T(8,128)(2,1)S(1)} custom-call(bf16[8,768,128]{2,1,0:T(8,128)(2,1)S(1)} %bitcast.10, bf16[2048,768]{1,0:T(8,128)(2,1)} %get-tuple-element.7.tx_hbm, bf16[768,2048]{1,0:T(8,128)(2,1)} %get-tuple-element.8.xt_hbm, f32[4,256,128]{2,1,0:T(8,128)} %get-tuple-element.9.v4_hbm, bf16[4,256,256]{2,1,0:T(8,128)(2,1)S(1)} %copy-done.3, ...), custom_call_target="tpu_custom_call" | custom-call | flops 6442450944 | bytes 11075584 | tf_op jit(solution)/shard_map/pallas_call | solution.py:268
  55.8 0.0 copy-start.1
  55.8 29.6 %all_to_all.10 = bf16[128,25,2,128]{3,2,1,0:T(2,128)(2,1)S(1)} all-to-all(bf16[128,25,2,128]{3,2,1,0:T(2,128)(2,1)S(1)} %bitcast.8), channel_id=1, replica_groups=mesh['band'=8,'fft'=16] {'band','fft'}, dimensions={0} | all-to-all | bytes 3276800 | tf_op jit(solution)/shard_map/all_to_all | solution.py:348
  85.4 0.0 copy-done.1
  85.4 1.7 %shard_map.116 = (bf16[1536,512]{1,0:T(8,128)(2,1)S(1)}, f32[2,1,8]{2,1,0:T(1,128)}) custom-call(bf16[6400,128]{1,0:T(8,128)(2,1)S(1)} %bitcast.9, bf16[512,512]{1,0:T(8,128)(2,1)S(1)} %copy-done.1), custom_call_target="tpu_custom_call" | custom-call | flops 805306368 | bytes 3735616 | tf_op jit(solution)/shard_map/pallas_call | solution.py:268
  87.1 1.8 %reshape.83 = bf16[1,24,64,2,256]{4,3,2,1,0:T(2,128)(2,1)} reshape(bf16[1536,512]{1,0:T(8,128)(2,1)S(1)} %get-tuple-element.10) | data formatting | bytes 3145728 | tf_op jit(solution)/shard_map/reshape | solution.py:360
  (7 shorter events, 0.0 us)
Async XLA Ops:
  0.6 1.8 %copy-start = (bf16[512,512]{1,0:T(8,128)(2,1)S(1)}, bf16[512,512]{1,0:T(8,128)(2,1)}, u32[]{:S(2)}) copy-start(bf16[512,512]{1,0:T(8,128)(2,1)} %constant.27.clone.t_ref) | copy-start | bytes 1572868
  5.1 11.3 %copy-start.7 = (s32[384]{0:T(512)S(1)}, s32[384]{0:T(512)}, u32[]{:S(2)}) copy-start(s32[384]{0:T(512)} %param.12) | copy-start | bytes 4612
  5.2 12.8 %copy-start.4 = (bf16[512,512]{1,0:T(8,128)(2,1)S(1)}, bf16[512,512]{1,0:T(8,128)(2,1)}, u32[]{:S(2)}) copy-start(bf16[512,512]{1,0:T(8,128)(2,1)} %constant.30.clone.ord_ref) | copy-start | bytes 1572868
  5.2 35.9 %all-to-all-start = ((bf16[128,48,128]{2,1,0:T(8,128)(2,1)}), bf16[128,48,128]{2,1,0:T(8,128)(2,1)S(1)}, u32[]{:S(2)}, u32[]{:S(2)}) async-start(bf16[128,48,128]{2,1,0:T(8,128)(2,1)} %bitcast), calls=%async_computation | async-start | bytes 3145728 | tf_op jit(solution)/shard_map/all_to_all | solution.py:301
  18.0 1.0 %copy-start.5 = (bf16[512,512]{1,0:T(8,128)(2,1)S(1)}, bf16[512,512]{1,0:T(8,128)(2,1)}, u32[]{:S(2)}) copy-start(bf16[512,512]{1,0:T(8,128)(2,1)} %constant.29.clone.b_ref) | copy-start | bytes 1572868
  19.0 1.0 %copy-start.6 = (bf16[512,512]{1,0:T(8,128)(2,1)S(1)}, bf16[512,512]{1,0:T(8,128)(2,1)}, u32[]{:S(2)}) copy-start(bf16[512,512]{1,0:T(8,128)(2,1)} %constant.28.clone.f_ref) | copy-start | bytes 1572868
  20.1 21.0 %copy-start.2 = (bf16[4,256,256]{2,1,0:T(8,128)(2,1)S(1)}, bf16[4,256,256]{2,1,0:T(8,128)(2,1)}, u32[]{:S(2)}) copy-start(bf16[4,256,256]{2,1,0:T(8,128)(2,1)} %constant.32.clone.yb_ref) | copy-start | bytes 1572868
  20.1 21.0 %copy-start.3 = (bf16[4,256,256]{2,1,0:T(8,128)(2,1)S(1)}, bf16[4,256,256]{2,1,0:T(8,128)(2,1)}, u32[]{:S(2)}) copy-start(bf16[4,256,256]{2,1,0:T(8,128)(2,1)} %constant.31.clone.yf_ref) | copy-start | bytes 1572868
  55.8 29.6 %copy-start.1 = (bf16[512,512]{1,0:T(8,128)(2,1)S(1)}, bf16[512,512]{1,0:T(8,128)(2,1)}, u32[]{:S(2)}) copy-start(bf16[512,512]{1,0:T(8,128)(2,1)} %constant.33.clone.t_ref) | copy-start | bytes 1572868

commit v6 on v5

--- a/solution.py
+++ b/solution.py
@@ -81,7 +81,7 @@
     o_ref[...] = scr[...].astype(BF16)
 
 
-def from_planes_kernel(count, x_ref, t_ref, o_ref, m_ref, scr):
+def from_planes_kernel(count, x_ref, t_ref, o_hbm, m_ref, scr, out, low, high, sems):
     devices = t_ref.shape[0] // 4
     rows = scr.shape[0] // devices
     blocks = rows // 2 - 1
@@ -93,6 +93,7 @@
     total = total / count
     m_ref[0] = total[:, :bands]
     m_ref[1] = total[:, bands:]
+    copies = []
     for g in range(blocks // 4):
         parts = []
         for m in range(g * 4, g * 4 + 4):
@@ -101,8 +102,18 @@
             )
             y = jnp.transpose(y).astype(BF16)
             parts.append(jnp.concatenate([y[:64], y[64:]], axis=1))
-        left = jnp.concatenate(parts, axis=0)
-        o_ref[g * 256 : (g + 1) * 256, :] = dot(left, t_ref[...]).astype(BF16)
+        value = dot(jnp.concatenate(parts, axis=0), t_ref[...])
+        for half, lanes in ((low, 0), (high, 128)):
+            for d in range(2):
+                at = d * 256 + lanes
+                half[g % 2, pl.ds(d, 256, stride=2), :] = value[:, at : at + 128]
+        pairs = jnp.concatenate([low[g % 2], high[g % 2]], axis=1).astype(BF16)
+        out[g * 256 : (g + 1) * 256] = pairs.reshape(256, 2, 256)
+        part = pl.ds(g * 256, 256)
+        copies.append(pltpu.make_async_copy(out.at[part], o_hbm.at[part], sems.at[g]))
+        copies[-1].start()
+    for copy in copies:
+        copy.wait()
 
 
 def prepare_kernel(
@@ -144,8 +155,8 @@
 
 
 def planes_kernel(
-    groups, r_ref, tx_hbm, xt_hbm, v4_hbm, yf_ref, yb_ref, o_ref,
-    tx, xt, v4, h, r_scr, p_scr, left_scr, right_scr, sems,
+    groups, r_ref, tx_hbm, xt_hbm, v4_hbm, yf_hbm, yb_hbm, o_ref,
+    tx, xt, v4, yf, yb, h, r_scr, p_scr, left_scr, right_scr, sems,
 ):
     size = v4.shape[1]
     bands, count = r_ref.shape[0], r_ref.shape[1]
@@ -155,13 +166,17 @@
     pitch = p_scr.shape[0] // bands
     width = 2 * bands
     load_v = pltpu.make_async_copy(v4_hbm, v4, sems.at[5])
+    load_f = pltpu.make_async_copy(yf_hbm, yf, sems.at[6])
+    load_b = pltpu.make_async_copy(yb_hbm, yb, sems.at[7])
     loads = []
     for s in range(4):
         part = slice(s * 2 * size, (s + 1) * 2 * size)
         loads.append(pltpu.make_async_copy(tx_hbm.at[part], tx.at[part], sems.at[s]))
     load_xt = pltpu.make_async_copy(xt_hbm, xt, sems.at[4])
     loads[0].start()
+    load_f.start()
     load_v.start()
+    load_b.start()
     for copy in loads[1:]:
         copy.start()
     load_xt.start()
@@ -190,12 +205,14 @@
             axis=0,
         )
         if s == 0:
+            load_f.wait()
             load_v.wait()
+            load_b.wait()
         for f in range(s * ffts // 4, (s + 1) * ffts // 4):
             left_scr[f * width : (f + 1) * width, :] = side(r_scr, f * rows, count)
         v = jnp.concatenate([v4[s], v4[s]], axis=1)
-        field = (dot(left, yf_ref[s]) * jnp.concatenate([v] * bands, axis=0)).astype(BF16)
-        back = dot(field, yb_ref[s]).astype(BF16)
+        field = (dot(left, yf[s]) * jnp.concatenate([v] * bands, axis=0)).astype(BF16)
+        back = dot(field, yb[s]).astype(BF16)
         row = s * 2 * size
         for b in range(bands):
             part = back[b * size : (b + 1) * size]
@@ -257,23 +274,24 @@
             o_ref[at : at + message - rows, :] = part
 
 
-def call(kernel, out_shape, scratch, flops, args, in_hbm=(), out_hbm=False, limit=40):
+def call(kernel, out_shape, scratch, flops, args, in_hbm=(), out_hbm=(), limit=40):
     read = sum(a.size * a.dtype.itemsize for a in args)
-    outs = jax.tree.leaves(out_shape, is_leaf=lambda s: hasattr(s, "shape"))
+    outs = out_shape if isinstance(out_shape, tuple) else (out_shape,)
     written = sum(math.prod(s.shape) * jnp.dtype(s.dtype).itemsize for s in outs)
     args = [
         pltpu.with_memory_space_constraint(a, pltpu.HBM) if i in in_hbm else a
         for i, a in enumerate(args)
     ]
-    return pl.pallas_call(
+    results = pl.pallas_call(
         kernel,
-        out_shape=out_shape,
+        out_shape=outs,
         in_specs=[HBM if i in in_hbm else VMEM for i in range(len(args))],
-        out_specs=[HBM if out_hbm else VMEM] * len(outs) if isinstance(out_shape, tuple) else VMEM,
+        out_specs=[HBM if i in out_hbm else VMEM for i in range(len(outs))],
         scratch_shapes=scratch,
         compiler_params=pltpu.CompilerParams(vmem_limit_bytes=limit * 2**20),
         cost_estimate=pl.CostEstimate(flops=flops, bytes_accessed=read + written, transcendentals=0),
     )(*args)
+    return results if isinstance(out_shape, tuple) else results[0]
 
 
 def body(coeffs, potential, pattern):
@@ -293,7 +311,7 @@
 
     sent = call(
         to_planes_kernel,
-        shape((devices * rows, 128), BF16),
+        pltpu.VMEM((devices * rows, 128), BF16),
         [pltpu.VMEM((devices * rows, 128), F32)],
         2 * sticks * (2 * size) ** 2,
         (coeffs.reshape(sticks, 2 * size), jnp.asarray(np.ascontiguousarray(table.T))),
@@ -325,7 +343,7 @@
             jnp.asarray(np.ascontiguousarray(forward.T)),
             jnp.asarray(order_table(size, 4, per_dev)),
         ),
-        out_hbm=True,
+        out_hbm=(0, 1, 2),
     )
 
     message = rows + 2
@@ -334,16 +352,18 @@
         shape((devices * message, 128), BF16),
         held
         + [
+            pltpu.VMEM(y_forward.shape, BF16),
+            pltpu.VMEM(y_forward.shape, BF16),
             pltpu.VMEM((8 * size, bands * 128), BF16),
             pltpu.VMEM((bands * count, 128), F32),
             pltpu.VMEM((devices * message + 8 * bands, 128), F32),
             pltpu.VMEM((ffts * 2 * bands, block_count * 128), BF16),
             pltpu.VMEM((ffts * 2 * bands, block_count * 128), BF16),
-            pltpu.SemaphoreType.DMA((6,)),
+            pltpu.SemaphoreType.DMA((8,)),
         ],
         2 * bands * 128 * 2 * 8 * size * count,
         (got, x_table, x_back, v4, jnp.asarray(y_forward), jnp.asarray(y_backward)),
-        in_hbm=(1, 2, 3),
+        in_hbm=(1, 2, 3, 4, 5),
     )
     returned = lax.all_to_all(
         picked.reshape(devices, message // 2, 2, 128), AXES, split_axis=0, concat_axis=0, tiled=True
@@ -352,10 +372,17 @@
     total_count = block_count * ffts * block_width * size
     images, matrix_rows = call(
         functools.partial(from_planes_kernel, total_count),
-        (shape((sticks, 2 * size), BF16), shape((2, 1, bands), F32)),
-        [pltpu.VMEM((devices * message, 128), F32)],
+        (pltpu.HBM((sticks, 2, size), BF16), shape((2, 1, bands), F32)),
+        [
+            pltpu.VMEM((devices * message, 128), F32),
+            pltpu.VMEM((sticks, 2, size), BF16),
+            pltpu.VMEM((2, 512, 128), F32),
+            pltpu.VMEM((2, 512, 128), F32),
+            pltpu.SemaphoreType.DMA((block_count // 4,)),
+        ],
         2 * sticks * (2 * size) ** 2,
         (returned.reshape(devices * message, 128), jnp.asarray(table)),
+        out_hbm=(0,),
     )
     return (images.reshape(coeffs.shape), matrix_rows)
 

time: 89.8 us -> 89.4 us (level)
  local copies, waits for them, and re-layouts: 7.16 us -> 4.56 us
  Pallas kernels: 24.8 us -> 26.1 us
    reshape x1 -> x0, local copies, waits for them, and re-layouts: 1.83 us -> none  [body(): return (images.reshape(coeffs.shape), matrix_rows)]
    unnamed x17 -> x15, local copies, waits for them, and re-layouts: 3.9 us -> 2.42 us
    pallas_call x4, Pallas kernels: 24.8 us -> 26.1 us  [call(): pl.pallas_call(kernel, out_shape=outs, in_specs=[HBM if i in in_hbm else...]
  transfers between devices with their start and end apart: 1 -> 1, of which waited for: 1 -> 1; matrix products, arithmetic and copies ran while one was open for 2% -> 2% of each run, Pallas kernels for 6% -> 7%
where the time goes in v6:
time: 89.4 us; the launch traced here: 88.5 us
  blocking collectives  29.6 us (33%)
  Pallas kernels  26.1 us (29%)
  waiting for transfers between devices  16 us (18%)
  starting transfers between devices  11.3 us (13%)
  local copies, waits for them, and re-layouts  4.56 us (5%)
  between operations  0.96 us (1%)
    all_to_all x1, blocking collectives, body(): lax.all_to_all(picked.reshape(devices, message // 2, 2, 128), AXES, split...  29.6 us
    pallas_call x4, Pallas kernels, call(): pl.pallas_call(kernel, out_shape=outs, in_specs=[HBM if i in in_hbm else...  26.1 us
    all_to_all x1, waiting for transfers between devices, body(): lax.all_to_all(sent.reshape(devices, rows, 128), AXES, split_axis=0, conc...  16 us
    all_to_all x1, starting transfers between devices, body(): lax.all_to_all(sent.reshape(devices, rows, 128), AXES, split_axis=0, conc...  11.3 us
    unnamed x15, local copies, waits for them, and re-layouts  2.42 us
  transfers between devices with their start and end apart: 1, of which 1 were waited for; matrix products, arithmetic and copies ran while one was open for 2% of the time, Pallas kernels for 7%

profile of v6, /device:TPU:0, one launch (start us, length us, event | category | flops | bytes accessed | tf_op | source)
XLA Modules:
  0.0 88.5 jit_solution(10914308805822520256)
XLA Ops:
  0.6 0.0 copy-start
  0.6 1.8 %copy.13 = bf16[192,8,2,256]{3,1,2,0:T(8,128)(2,1)S(1)} copy(bf16[192,8,2,256]{3,2,1,0:T(2,128)(2,1)} %bitcast.12) | data formatting | bytes 3145728
  2.4 0.0 copy-done
  2.4 2.7 %shard_map.113 = bf16[6144,128]{1,0:T(8,128)(2,1)} custom-call(bf16[1536,512]{1,0:T(8,128)(2,1)S(1)} %bitcast.8, bf16[512,512]{1,0:T(8,128)(2,1)S(1)} %copy-done), custom_call_target="tpu_custom_call" | custom-call | flops 805306368 | bytes 3670016 | tf_op jit(solution)/shard_map/pallas_call | solution.py:285
  5.1 0.0 copy-start.6
  5.2 0.0 copy-start.2
  5.2 11.3 %all-to-all-start = ((bf16[128,48,128]{2,1,0:T(8,128)(2,1)}), bf16[128,48,128]{2,1,0:T(8,128)(2,1)S(1)}, u32[]{:S(2)}, u32[]{:S(2)}) async-start(bf16[128,48,128]{2,1,0:T(8,128)(2,1)} %bitcast), calls=%async_computation | async-start | bytes 3145728 | tf_op jit(solution)/shard_map/all_to_all | solution.py:319
  16.5 0.0 copy-done.6
  16.5 0.1 mul.19
  16.6 0.0 copy-start.5
  16.6 0.6 copy-done.5
  17.2 0.1 add.39.row_ref
  17.3 0.9 %add.42.col_ref = s32[768,1]{1,0:T(8,128)S(1)} reshape(s32[16,2,24]{2,1,0:T(2,128)} %copy-done.5) | data formatting | bytes 6144 | tf_op jit(solution)/shard_map/add | solution.py:324
  18.2 1.1 %constant_dynamic-slice_fusion.v_ref = f32[2,256,256]{2,1,0:T(8,128)S(1)} fusion(f32[16,256,256]{2,1,0:T(8,128)} %param.11, s32[]{:T(128)S(6)} %select_n.3), kind=kLoop, calls=%fused_computation.2 | loop fusion | bytes 1048580 | tf_op jit(solution)/shard_map/dynamic_slice | solution.py:325
  19.3 0.0 copy-done.2
  19.3 0.0 copy-done.3
  19.3 0.0 copy-done.4
  19.3 5.8 %shard_map.114 = (bf16[2048,768]{1,0:T(8,128)(2,1)}, bf16[768,2048]{1,0:T(8,128)(2,1)}, f32[4,256,128]{2,1,0:T(8,128)}) custom-call(s32[1,768]{1,0:T(1,128)S(1)} %add.39.row_ref, s32[768,1]{1,0:T(8,128)S(1)} %add.42.col_ref, f32[2,256,256]{2,1,0:T(8,128)S(1)} %constant_dynamic-slice_fusion.v_ref, bf16[512,512]{1,0:T(8,128)(2,1)S(1)} %copy-done.4, ...), custom_call_target="tpu_custom_call" | custom-call | flops 3221225472 | bytes 8919040 | tf_op jit(solution)/shard_map/pallas_call | solution.py:285
  25.1 16.0 %all-to-all-done = bf16[128,48,128]{2,1,0:T(8,128)(2,1)S(1)} async-done(((bf16[128,48,128]{2,1,0:T(8,128)(2,1)}), bf16[128,48,128]{2,1,0:T(8,128)(2,1)S(1)}, u32[]{:S(2)}, u32[]{:S(2)}) %all-to-all-start) | async-done | bytes 1572896 | tf_op jit(solution)/shard_map/all_to_all | solution.py:319
  41.1 14.7 %shard_map.115 = bf16[6400,128]{1,0:T(8,128)(2,1)S(1)} custom-call(bf16[8,768,128]{2,1,0:T(8,128)(2,1)S(1)} %bitcast.11, bf16[2048,768]{1,0:T(8,128)(2,1)} %get-tuple-element.7.tx_hbm, bf16[768,2048]{1,0:T(8,128)(2,1)} %get-tuple-element.8.xt_hbm, f32[4,256,128]{2,1,0:T(8,128)} %get-tuple-element.9.v4_hbm, bf16[4,256,256]{2,1,0:T(8,128)(2,1)} %constant.31.clone.yf_hbm, ...), custom_call_target="tpu_custom_call" | custom-call | flops 6442450944 | bytes 11075584 | tf_op jit(solution)/shard_map/pallas_call | solution.py:285
  55.8 0.0 copy-start.1
  55.8 29.6 %all_to_all.10 = bf16[128,25,2,128]{3,2,1,0:T(2,128)(2,1)S(1)} all-to-all(bf16[128,25,2,128]{3,2,1,0:T(2,128)(2,1)S(1)} %bitcast.9), channel_id=1, replica_groups=mesh['band'=8,'fft'=16] {'band','fft'}, dimensions={0} | all-to-all | bytes 3276800 | tf_op jit(solution)/shard_map/all_to_all | solution.py:368
  85.4 0.0 copy-done.1
  85.4 2.9 %shard_map.116 = (bf16[1536,2,256]{2,1,0:T(2,128)(2,1)}, f32[2,1,8]{2,1,0:T(1,128)}) custom-call(bf16[6400,128]{1,0:T(8,128)(2,1)S(1)} %bitcast.10, bf16[512,512]{1,0:T(8,128)(2,1)S(1)} %copy-done.1), custom_call_target="tpu_custom_call" | custom-call | flops 805306368 | bytes 3735616 | tf_op jit(solution)/shard_map/pallas_call | solution.py:285
  (4 shorter events, 0.0 us)
Async XLA Ops:
  0.6 1.8 %copy-start = (bf16[512,512]{1,0:T(8,128)(2,1)S(1)}, bf16[512,512]{1,0:T(8,128)(2,1)}, u32[]{:S(2)}) copy-start(bf16[512,512]{1,0:T(8,128)(2,1)} %constant.27.clone.t_ref) | copy-start | bytes 1572868
  5.1 11.4 %copy-start.6 = (s32[384]{0:T(512)S(1)}, s32[384]{0:T(512)}, u32[]{:S(2)}) copy-start(s32[384]{0:T(512)} %param.12) | copy-start | bytes 4612
  5.2 14.2 %copy-start.2 = (bf16[512,512]{1,0:T(8,128)(2,1)S(1)}, bf16[512,512]{1,0:T(8,128)(2,1)}, u32[]{:S(2)}) copy-start(bf16[512,512]{1,0:T(8,128)(2,1)} %constant.30.clone.ord_ref) | copy-start | bytes 1572868
  5.2 14.2 %copy-start.3 = (bf16[512,512]{1,0:T(8,128)(2,1)S(1)}, bf16[512,512]{1,0:T(8,128)(2,1)}, u32[]{:S(2)}) copy-start(bf16[512,512]{1,0:T(8,128)(2,1)} %constant.29.clone.b_ref) | copy-start | bytes 1572868
  5.2 14.2 %copy-start.4 = (bf16[512,512]{1,0:T(8,128)(2,1)S(1)}, bf16[512,512]{1,0:T(8,128)(2,1)}, u32[]{:S(2)}) copy-start(bf16[512,512]{1,0:T(8,128)(2,1)} %constant.28.clone.f_ref) | copy-start | bytes 1572868
  5.2 35.9 %all-to-all-start = ((bf16[128,48,128]{2,1,0:T(8,128)(2,1)}), bf16[128,48,128]{2,1,0:T(8,128)(2,1)S(1)}, u32[]{:S(2)}, u32[]{:S(2)}) async-start(bf16[128,48,128]{2,1,0:T(8,128)(2,1)} %bitcast), calls=%async_computation | async-start | bytes 3145728 | tf_op jit(solution)/shard_map/all_to_all | solution.py:319
  16.6 0.6 copy-start.5
  55.8 29.6 %copy-start.1 = (bf16[512,512]{1,0:T(8,128)(2,1)S(1)}, bf16[512,512]{1,0:T(8,128)(2,1)}, u32[]{:S(2)}) copy-start(bf16[512,512]{1,0:T(8,128)(2,1)} %constant.33.clone.t_ref) | copy-start | bytes 1572868

commit v7 on v6

--- a/solution.py
+++ b/solution.py
@@ -87,12 +87,10 @@
     blocks = rows // 2 - 1
     bands = m_ref.shape[2]
     scr[...] = x_ref[...].astype(F32)
-    line = jnp.sum(scr[pl.ds(2 * blocks, devices, stride=rows), :], axis=0, keepdims=True)
-    width = 2 * bands
-    total = line[:, :width] + (line[:, width : 2 * width] + line[:, 2 * width : 3 * width])
-    total = total / count
+    total = sum(scr[pl.ds(2 * blocks + i, devices, stride=rows), :] for i in range(2))
+    total = jnp.sum(total, axis=0, keepdims=True) / count
     m_ref[0] = total[:, :bands]
-    m_ref[1] = total[:, bands:]
+    m_ref[1] = total[:, bands : 2 * bands]
     copies = []
     for g in range(blocks // 4):
         parts = []
@@ -156,15 +154,13 @@
 
 def planes_kernel(
     groups, r_ref, tx_hbm, xt_hbm, v4_hbm, yf_hbm, yb_hbm, o_ref,
-    tx, xt, v4, yf, yb, h, r_scr, p_scr, left_scr, right_scr, sems,
+    tx, xt, v4, yf, yb, h, r_scr, p_scr, sems,
 ):
     size = v4.shape[1]
     bands, count = r_ref.shape[0], r_ref.shape[1]
     ffts = sum(groups)
     rows, blocks = count // ffts, count // ffts // 2
     message = o_ref.shape[0] // (bands * ffts)
-    pitch = p_scr.shape[0] // bands
-    width = 2 * bands
     load_v = pltpu.make_async_copy(v4_hbm, v4, sems.at[5])
     load_f = pltpu.make_async_copy(yf_hbm, yf, sems.at[6])
     load_b = pltpu.make_async_copy(yb_hbm, yb, sems.at[7])
@@ -183,14 +179,6 @@
     for b in range(bands):
         r_scr[b * count : (b + 1) * count, :] = r_ref[b].astype(F32)
 
-    def side(scr, start, stride):
-        tiles = []
-        for m in range(blocks):
-            real = scr[pl.ds(start + m, bands, stride=stride), :]
-            imag = scr[pl.ds(start + blocks + m, bands, stride=stride), :]
-            tiles.append(jnp.concatenate([real, imag], axis=0).astype(BF16))
-        return jnp.concatenate(tiles, axis=1)
-
     for s in range(4):
         loads[s].wait()
         w = jnp.concatenate([r_ref[b] for b in range(bands)], axis=1)
@@ -208,8 +196,6 @@
             load_f.wait()
             load_v.wait()
             load_b.wait()
-        for f in range(s * ffts // 4, (s + 1) * ffts // 4):
-            left_scr[f * width : (f + 1) * width, :] = side(r_scr, f * rows, count)
         v = jnp.concatenate([v4[s], v4[s]], axis=1)
         field = (dot(left, yf[s]) * jnp.concatenate([v] * bands, axis=0)).astype(BF16)
         back = dot(field, yb[s]).astype(BF16)
@@ -220,55 +206,44 @@
             h[row + size : row + 2 * size, b * 128 : (b + 1) * 128] = part[:, 128:]
 
     load_xt.wait()
-    ready = []
-
-    def pack(f):
-        right_scr[f * width : (f + 1) * width, :] = side(p_scr, f * message, pitch)
-
-    def products(sources):
-        part = slice(sources[0] * width, (sources[-1] + 1) * width)
-        square = dot_nt(left_scr[part, :], right_scr[part, :])
-        block = lax.broadcasted_iota(jnp.int32, square.shape, 0) // width
-        same = block == lax.broadcasted_iota(jnp.int32, square.shape, 1) // width
-        square = jnp.where(same, square, 0.0)
-        total = sum(square[f * width : (f + 1) * width] for f in range(len(sources)))
-        return jnp.concatenate([total, jnp.zeros((width, 128 - total.shape[1]), F32)], axis=1)
-
-    gram = jnp.zeros((width, 128), F32)
+    sums = {}
+
+    def add(key, value):
+        value = value[:8] + value[8:16] + value[16:24]
+        sums[key] = sums[key] + value if key in sums else value
+
     first = 0
     for group in groups:
-        for n in range(bands // 2):
-            if n < 2:
-                for f in ready[n::2]:
-                    pack(f)
-            if n == 2 and ready:
-                gram = gram + products(ready)
+        for n in reversed(range(bands // 2)):
             out = dot(xt[first * rows : (first + group) * rows, :], h[:, n * 256 : (n + 1) * 256])
             for f in range(group):
+                block = out[f * rows : (f + 1) * rows]
                 for j in range(2):
-                    at = (2 * n + j) * pitch + (first + f) * message
-                    part = out[f * rows : (f + 1) * rows, j * 128 : (j + 1) * 128]
-                    p_scr[at : at + rows, :] = part
-        ready = list(range(first, first + group))
+                    at = ((2 * n + j) * ffts + first + f) * message
+                    p_scr[at : at + rows, :] = block[:, j * 128 : (j + 1) * 128]
+                for i in range(2 * n + 2):
+                    at = i * count + (first + f) * rows
+                    real, imag = r_scr[at : at + blocks, :], r_scr[at + blocks : at + rows, :]
+                    for j in range(max(i, 2 * n), 2 * n + 2):
+                        part = block[:, (j - 2 * n) * 128 : (j - 2 * n + 1) * 128]
+                        add((i, j, 0), real * part[:blocks] + imag * part[blocks:])
+                        add((i, j, 1), real * part[blocks:] - imag * part[:blocks])
+            if first + group == ffts:
+                done = slice(2 * n * ffts * message, (2 * n + 2) * ffts * message)
+                o_ref[done, :] = p_scr[done, :].astype(BF16)
         first += group
-    for f in ready:
-        pack(f)
-    band = ffts * message
+
+    sums = {key: jnp.sum(value, axis=0, keepdims=True) for key, value in sums.items()}
+    lines = []
+    for i in range(bands):
+        lines += [sums[min(i, j), max(i, j), 0] for j in range(bands)]
+        lines += [sums[i, j, 1] if i <= j else -sums[j, i, 1] for j in range(bands)]
+    total = jnp.sum(jnp.transpose(jnp.concatenate(lines, axis=0)), axis=0, keepdims=True)
+    high = total.astype(BF16).astype(F32)
+    pair = jnp.concatenate([high, total - high], axis=0)
     for b in range(bands):
-        o_ref[b * band : (b + 1) * band, :] = p_scr[b * pitch : b * pitch + band, :].astype(BF16)
-    gram = gram + products(ready)
-    for shift in (64, 32, 16):
-        gram = gram + pltpu.roll(gram, shift, 1)
-    lane = lax.broadcasted_iota(jnp.int32, (bands, 128), 1)
-    turned = pltpu.roll(gram[bands:], bands, 1)
-    total = gram[:bands] + jnp.where(lane % width < bands, turned, -turned)
-    high = total.astype(BF16).astype(F32)
-    middle = (total - high).astype(BF16).astype(F32)
-    low = total - high - middle
-    lines = jnp.where(lane < width, high, jnp.where(lane < 2 * width, middle, low))
-    lines = jnp.where(lane < 3 * width, lines, 0.0)
-    for b in range(bands):
-        part = jnp.broadcast_to(lines[b : b + 1], (message - rows, 128)).astype(BF16)
+        part = pair if b == 0 else pltpu.roll(pair, 128 - b * 2 * bands, 1)
+        part = part.astype(BF16)
         for f in range(ffts):
             at = (b * ffts + f) * message + rows
             o_ref[at : at + message - rows, :] = part
@@ -348,7 +323,7 @@
 
     message = rows + 2
     picked = call(
-        functools.partial(planes_kernel, (6, 6, 4)),
+        functools.partial(planes_kernel, (16,)),
         shape((devices * message, 128), BF16),
         held
         + [
@@ -356,9 +331,7 @@
             pltpu.VMEM(y_forward.shape, BF16),
             pltpu.VMEM((8 * size, bands * 128), BF16),
             pltpu.VMEM((bands * count, 128), F32),
-            pltpu.VMEM((devices * message + 8 * bands, 128), F32),
-            pltpu.VMEM((ffts * 2 * bands, block_count * 128), BF16),
-            pltpu.VMEM((ffts * 2 * bands, block_count * 128), BF16),
+            pltpu.VMEM((devices * message, 128), F32),
             pltpu.SemaphoreType.DMA((8,)),
         ],
         2 * bands * 128 * 2 * 8 * size * count,

time: 89.4 us -> 87.4 us (0.978)
  Pallas kernels: 26.1 us -> 24.1 us
    pallas_call x4, Pallas kernels: 26.1 us -> 24.1 us  [call(): pl.pallas_call(kernel, out_shape=outs, in_specs=[HBM if i in in_hbm else...]
where the time goes in v7:
time: 87.4 us; the launch traced here: 86.6 us
  blocking collectives  29.6 us (34%)
  Pallas kernels  24.1 us (28%)
  waiting for transfers between devices  16 us (18%)
  starting transfers between devices  11.3 us (13%)
  local copies, waits for them, and re-layouts  4.56 us (5%)
  between operations  0.96 us (1%)
    all_to_all x1, blocking collectives, body(): lax.all_to_all(picked.reshape(devices, message // 2, 2, 128), AXES, split...  29.6 us
    pallas_call x4, Pallas kernels, call(): pl.pallas_call(kernel, out_shape=outs, in_specs=[HBM if i in in_hbm else...  24.1 us
    all_to_all x1, waiting for transfers between devices, body(): lax.all_to_all(sent.reshape(devices, rows, 128), AXES, split_axis=0, conc...  16 us
    all_to_all x1, starting transfers between devices, body(): lax.all_to_all(sent.reshape(devices, rows, 128), AXES, split_axis=0, conc...  11.3 us
    unnamed x15, local copies, waits for them, and re-layouts  2.42 us
  transfers between devices with their start and end apart: 1, of which 1 were waited for; matrix products, arithmetic and copies ran while one was open for 2% of the time, Pallas kernels for 7%

profile of v7, /device:TPU:0, one launch (start us, length us, event | category | flops | bytes accessed | tf_op | source)
XLA Modules:
  0.0 86.6 jit_solution(14869991694334657594)
XLA Ops:
  0.6 0.0 copy-start
  0.6 1.8 %copy.13 = bf16[192,8,2,256]{3,1,2,0:T(8,128)(2,1)S(1)} copy(bf16[192,8,2,256]{3,2,1,0:T(2,128)(2,1)} %bitcast.12) | data formatting | bytes 3145728
  2.4 0.0 copy-done
  2.4 2.7 %shard_map.113 = bf16[6144,128]{1,0:T(8,128)(2,1)} custom-call(bf16[1536,512]{1,0:T(8,128)(2,1)S(1)} %bitcast.8, bf16[512,512]{1,0:T(8,128)(2,1)S(1)} %copy-done), custom_call_target="tpu_custom_call" | custom-call | flops 805306368 | bytes 3670016 | tf_op jit(solution)/shard_map/pallas_call | solution.py:260
  5.1 0.0 copy-start.6
  5.2 0.0 copy-start.2
  5.2 11.3 %all-to-all-start = ((bf16[128,48,128]{2,1,0:T(8,128)(2,1)}), bf16[128,48,128]{2,1,0:T(8,128)(2,1)S(1)}, u32[]{:S(2)}, u32[]{:S(2)}) async-start(bf16[128,48,128]{2,1,0:T(8,128)(2,1)} %bitcast), calls=%async_computation | async-start | bytes 3145728 | tf_op jit(solution)/shard_map/all_to_all | solution.py:294
  16.5 0.0 copy-done.6
  16.5 0.1 mul.19
  16.6 0.0 copy-start.5
  16.6 0.6 copy-done.5
  17.2 0.1 add.39.row_ref
  17.3 0.9 %add.42.col_ref = s32[768,1]{1,0:T(8,128)S(1)} reshape(s32[16,2,24]{2,1,0:T(2,128)} %copy-done.5) | data formatting | bytes 6144 | tf_op jit(solution)/shard_map/add | solution.py:299
  18.2 1.1 %constant_dynamic-slice_fusion.v_ref = f32[2,256,256]{2,1,0:T(8,128)S(1)} fusion(f32[16,256,256]{2,1,0:T(8,128)} %param.11, s32[]{:T(128)S(6)} %select_n.3), kind=kLoop, calls=%fused_computation.2 | loop fusion | bytes 1048580 | tf_op jit(solution)/shard_map/dynamic_slice | solution.py:300
  19.3 0.0 copy-done.2
  19.3 0.0 copy-done.3
  19.3 0.0 copy-done.4
  19.3 5.8 %shard_map.114 = (bf16[2048,768]{1,0:T(8,128)(2,1)}, bf16[768,2048]{1,0:T(8,128)(2,1)}, f32[4,256,128]{2,1,0:T(8,128)}) custom-call(s32[1,768]{1,0:T(1,128)S(1)} %add.39.row_ref, s32[768,1]{1,0:T(8,128)S(1)} %add.42.col_ref, f32[2,256,256]{2,1,0:T(8,128)S(1)} %constant_dynamic-slice_fusion.v_ref, bf16[512,512]{1,0:T(8,128)(2,1)S(1)} %copy-done.4, ...), custom_call_target="tpu_custom_call" | custom-call | flops 3221225472 | bytes 8919040 | tf_op jit(solution)/shard_map/pallas_call | solution.py:260
  25.1 16.0 %all-to-all-done = bf16[128,48,128]{2,1,0:T(8,128)(2,1)S(1)} async-done(((bf16[128,48,128]{2,1,0:T(8,128)(2,1)}), bf16[128,48,128]{2,1,0:T(8,128)(2,1)S(1)}, u32[]{:S(2)}, u32[]{:S(2)}) %all-to-all-start) | async-done | bytes 1572896 | tf_op jit(solution)/shard_map/all_to_all | solution.py:294
  41.1 12.8 %shard_map.115 = bf16[6400,128]{1,0:T(8,128)(2,1)S(1)} custom-call(bf16[8,768,128]{2,1,0:T(8,128)(2,1)S(1)} %bitcast.11, bf16[2048,768]{1,0:T(8,128)(2,1)} %get-tuple-element.7.tx_hbm, bf16[768,2048]{1,0:T(8,128)(2,1)} %get-tuple-element.8.xt_hbm, f32[4,256,128]{2,1,0:T(8,128)} %get-tuple-element.9.v4_hbm, bf16[4,256,256]{2,1,0:T(8,128)(2,1)} %constant.31.clone.yf_hbm, ...), custom_call_target="tpu_custom_call" | custom-call | flops 6442450944 | bytes 11075584 | tf_op jit(solution)/shard_map/pallas_call | solution.py:260
  53.9 0.0 copy-start.1
  53.9 29.6 %all_to_all.10 = bf16[128,25,2,128]{3,2,1,0:T(2,128)(2,1)S(1)} all-to-all(bf16[128,25,2,128]{3,2,1,0:T(2,128)(2,1)S(1)} %bitcast.9), channel_id=1, replica_groups=mesh['band'=8,'fft'=16] {'band','fft'}, dimensions={0} | all-to-all | bytes 3276800 | tf_op jit(solution)/shard_map/all_to_all | solution.py:341
  83.5 0.0 copy-done.1
  83.5 2.9 %shard_map.116 = (bf16[1536,2,256]{2,1,0:T(2,128)(2,1)}, f32[2,1,8]{2,1,0:T(1,128)}) custom-call(bf16[6400,128]{1,0:T(8,128)(2,1)S(1)} %bitcast.10, bf16[512,512]{1,0:T(8,128)(2,1)S(1)} %copy-done.1), custom_call_target="tpu_custom_call" | custom-call | flops 805306368 | bytes 3735616 | tf_op jit(solution)/shard_map/pallas_call | solution.py:260
  (4 shorter events, 0.0 us)
Async XLA Ops:
  0.6 1.8 %copy-start = (bf16[512,512]{1,0:T(8,128)(2,1)S(1)}, bf16[512,512]{1,0:T(8,128)(2,1)}, u32[]{:S(2)}) copy-start(bf16[512,512]{1,0:T(8,128)(2,1)} %constant.27.clone.t_ref) | copy-start | bytes 1572868
  5.1 11.4 %copy-start.6 = (s32[384]{0:T(512)S(1)}, s32[384]{0:T(512)}, u32[]{:S(2)}) copy-start(s32[384]{0:T(512)} %param.12) | copy-start | bytes 4612
  5.2 14.2 %copy-start.2 = (bf16[512,512]{1,0:T(8,128)(2,1)S(1)}, bf16[512,512]{1,0:T(8,128)(2,1)}, u32[]{:S(2)}) copy-start(bf16[512,512]{1,0:T(8,128)(2,1)} %constant.30.clone.ord_ref) | copy-start | bytes 1572868
  5.2 14.2 %copy-start.3 = (bf16[512,512]{1,0:T(8,128)(2,1)S(1)}, bf16[512,512]{1,0:T(8,128)(2,1)}, u32[]{:S(2)}) copy-start(bf16[512,512]{1,0:T(8,128)(2,1)} %constant.29.clone.b_ref) | copy-start | bytes 1572868
  5.2 14.2 %copy-start.4 = (bf16[512,512]{1,0:T(8,128)(2,1)S(1)}, bf16[512,512]{1,0:T(8,128)(2,1)}, u32[]{:S(2)}) copy-start(bf16[512,512]{1,0:T(8,128)(2,1)} %constant.28.clone.f_ref) | copy-start | bytes 1572868
  5.2 35.9 %all-to-all-start = ((bf16[128,48,128]{2,1,0:T(8,128)(2,1)}), bf16[128,48,128]{2,1,0:T(8,128)(2,1)S(1)}, u32[]{:S(2)}, u32[]{:S(2)}) async-start(bf16[128,48,128]{2,1,0:T(8,128)(2,1)} %bitcast), calls=%async_computation | async-start | bytes 3145728 | tf_op jit(solution)/shard_map/all_to_all | solution.py:294
  16.6 0.6 copy-start.5
  53.9 29.6 %copy-start.1 = (bf16[512,512]{1,0:T(8,128)(2,1)S(1)}, bf16[512,512]{1,0:T(8,128)(2,1)}, u32[]{:S(2)}) copy-start(bf16[512,512]{1,0:T(8,128)(2,1)} %constant.33.clone.t_ref) | copy-start | bytes 1572868

commit v8 on v7

--- a/solution.py
+++ b/solution.py
@@ -65,23 +65,31 @@
     return lax.dot_general(a, b, (((1,), (1,)), ((), ())), preferred_element_type=F32)
 
 
-def to_planes_kernel(c_ref, t_ref, o_ref, scr):
-    half = t_ref.shape[1] // 2
-    devices = half // 2
-    rows = scr.shape[0] // devices
+def to_planes_kernel(c_ref, t_ref, o_hbm, out, first, second, sems):
+    side = t_ref.shape[1] // 2
+    devices = side // 4
+    rows = first.shape[0] // devices
     blocks = rows // 2
-    for g in range(blocks // 4):
-        r = dot(c_ref[g * 256 : (g + 1) * 256, :], t_ref[...])
-        for i in range(4):
-            part = r[i * 64 : (i + 1) * 64]
-            part = jnp.transpose(jnp.concatenate([part[:, :half], part[:, half:]], axis=0))
-            for d in range(2):
-                at = pl.ds(d * blocks + g * 4 + i, devices, stride=rows)
-                scr[at, :] = part[d * devices : (d + 1) * devices]
-    o_ref[...] = scr[...].astype(BF16)
-
-
-def from_planes_kernel(count, x_ref, t_ref, o_hbm, m_ref, scr, out, low, high, sems):
+    copies = []
+    for n, scr in enumerate((first, second)):
+        for g in range(blocks // 4):
+            r = dot(c_ref[g * 256 : (g + 1) * 256, :], t_ref[:, n * side : (n + 1) * side])
+            for i in range(4):
+                part = r[i * 64 : (i + 1) * 64]
+                part = jnp.concatenate([part[:, : side // 2], part[:, side // 2 :]], axis=0)
+                part = jnp.transpose(part)
+                for d in range(2):
+                    at = pl.ds(d * blocks + g * 4 + i, devices, stride=rows)
+                    scr[at, :] = part[d * devices : (d + 1) * devices]
+        half = pl.ds(n * devices * rows, devices * rows)
+        out[half, :] = scr[...].astype(BF16)
+        copies.append(pltpu.make_async_copy(out.at[half], o_hbm.at[half], sems.at[n]))
+        copies[-1].start()
+    for copy in copies:
+        copy.wait()
+
+
+def from_planes_kernel(count, x_ref, t_ref, o_hbm, m_ref, scr, out, pairs0, pairs1, sems):
     devices = t_ref.shape[0] // 4
     rows = scr.shape[0] // devices
     blocks = rows // 2 - 1
@@ -101,13 +109,13 @@
             y = jnp.transpose(y).astype(BF16)
             parts.append(jnp.concatenate([y[:64], y[64:]], axis=1))
         value = dot(jnp.concatenate(parts, axis=0), t_ref[...])
-        for half, lanes in ((low, 0), (high, 128)):
-            for d in range(2):
-                at = d * 256 + lanes
-                half[g % 2, pl.ds(d, 256, stride=2), :] = value[:, at : at + 128]
-        pairs = jnp.concatenate([low[g % 2], high[g % 2]], axis=1).astype(BF16)
-        out[g * 256 : (g + 1) * 256] = pairs.reshape(256, 2, 256)
-        part = pl.ds(g * 256, 256)
+        pairs = (pairs0, pairs1)[g % 2]
+        for d in range(2):
+            for k in range(2):
+                at = d * 256 + k * 128
+                pairs[pl.ds(2 * k + d, 256, stride=4), :] = value[:, at : at + 128]
+        part = pl.ds(g * 1024, 1024)
+        out[part, :] = pairs[...].astype(BF16)
         copies.append(pltpu.make_async_copy(out.at[part], o_hbm.at[part], sems.at[g]))
         copies[-1].start()
     for copy in copies:
@@ -115,7 +123,7 @@
 
 
 def prepare_kernel(
-    row_ref, col_ref, v_ref, f_ref, b_ref, ord_ref, tx_hbm, xt_hbm, v4_hbm, tx, xt, v4, sems
+    row_ref, col_ref, v_ref, f_ref, b_ref, ord_ref, tx_hbm, xt_hbm, v4_hbm, tx0, tx, xt, v4, sems
 ):
     size = f_ref.shape[0] // 2
     count = row_ref.shape[1]
@@ -135,8 +143,11 @@
     for s in range(4):
         part = slice(s * 2 * size, (s + 1) * 2 * size)
         tx[part, :] = dot(b_ref[...], hot(row_ref[...], rows, s, 0)).astype(BF16)
-        copies.append(pltpu.make_async_copy(tx.at[part], tx_hbm.at[part], sems.at[s]))
-        copies[-1].start()
+        if s == 0:
+            tx0[...] = tx[part, :]
+        else:
+            copies.append(pltpu.make_async_copy(tx.at[part], tx_hbm.at[part], sems.at[s]))
+            copies[-1].start()
         xt[:, part] = dot(hot(col_ref[...], cols, s, 1), f_ref[...]).astype(BF16)
     copies.append(pltpu.make_async_copy(xt, xt_hbm, sems.at[4]))
     copies[-1].start()
@@ -153,7 +164,7 @@
 
 
 def planes_kernel(
-    groups, r_ref, tx_hbm, xt_hbm, v4_hbm, yf_hbm, yb_hbm, o_ref,
+    groups, r_ref, tx0, tx_hbm, xt_hbm, v4_hbm, yf_hbm, yb_hbm, o_ref,
     tx, xt, v4, yf, yb, h, r_scr, p_scr, sems,
 ):
     size = v4.shape[1]
@@ -165,24 +176,24 @@
     load_f = pltpu.make_async_copy(yf_hbm, yf, sems.at[6])
     load_b = pltpu.make_async_copy(yb_hbm, yb, sems.at[7])
     loads = []
-    for s in range(4):
+    for s in range(1, 4):
         part = slice(s * 2 * size, (s + 1) * 2 * size)
         loads.append(pltpu.make_async_copy(tx_hbm.at[part], tx.at[part], sems.at[s]))
     load_xt = pltpu.make_async_copy(xt_hbm, xt, sems.at[4])
-    loads[0].start()
     load_f.start()
     load_v.start()
     load_b.start()
-    for copy in loads[1:]:
+    for copy in loads:
         copy.start()
     load_xt.start()
     for b in range(bands):
         r_scr[b * count : (b + 1) * count, :] = r_ref[b].astype(F32)
 
     for s in range(4):
-        loads[s].wait()
+        if s > 0:
+            loads[s - 1].wait()
         w = jnp.concatenate([r_ref[b] for b in range(bands)], axis=1)
-        g = dot(tx[s * 2 * size : (s + 1) * 2 * size, :], w).astype(BF16)
+        g = dot(tx0[...] if s == 0 else tx[s * 2 * size : (s + 1) * 2 * size, :], w).astype(BF16)
         left = jnp.concatenate(
             [
                 jnp.concatenate(
@@ -280,16 +291,24 @@
     shape = jax.ShapeDtypeStruct
 
     table = plane_table(size, bands, ffts)
+    halves = table.reshape(2 * per_dev, 2, devices // 2, 2 * size)
+    halves = halves.transpose(1, 0, 2, 3).reshape(2 * size, 2 * size)
     forward = dft_table(size, 1.0).reshape(2 * size, 2 * size)
     y_forward = split_table(size, 4, per_dev)
     y_backward = np.ascontiguousarray(y_forward.transpose(0, 2, 1))
 
     sent = call(
         to_planes_kernel,
-        pltpu.VMEM((devices * rows, 128), BF16),
-        [pltpu.VMEM((devices * rows, 128), F32)],
+        pltpu.HBM((devices * rows, 128), BF16),
+        [
+            pltpu.VMEM((devices * rows, 128), BF16),
+            pltpu.VMEM((devices * rows // 2, 128), F32),
+            pltpu.VMEM((devices * rows // 2, 128), F32),
+            pltpu.SemaphoreType.DMA((2,)),
+        ],
         2 * sticks * (2 * size) ** 2,
-        (coeffs.reshape(sticks, 2 * size), jnp.asarray(np.ascontiguousarray(table.T))),
+        (coeffs.reshape(sticks, 2 * size), jnp.asarray(np.ascontiguousarray(halves.T))),
+        out_hbm=(0,),
     )
     got = lax.all_to_all(
         sent.reshape(devices, rows, 128), AXES, split_axis=0, concat_axis=0, tiled=True
@@ -305,9 +324,9 @@
         pltpu.HBM((4, size, per_dev * size // 4), F32),
     )
     held = [pltpu.VMEM(t.shape, t.dtype) for t in tables]
-    x_table, x_back, v4 = call(
+    x_table, x_back, v4, x_first = call(
         prepare_kernel,
-        tables,
+        tables + (shape((2 * size, count), BF16),),
         held + [pltpu.SemaphoreType.DMA((6,))],
         2 * 2 * 4 * count * (2 * size) ** 2,
         (
@@ -335,8 +354,8 @@
             pltpu.SemaphoreType.DMA((8,)),
         ],
         2 * bands * 128 * 2 * 8 * size * count,
-        (got, x_table, x_back, v4, jnp.asarray(y_forward), jnp.asarray(y_backward)),
-        in_hbm=(1, 2, 3, 4, 5),
+        (got, x_first, x_table, x_back, v4, jnp.asarray(y_forward), jnp.asarray(y_backward)),
+        in_hbm=(2, 3, 4, 5, 6),
     )
     returned = lax.all_to_all(
         picked.reshape(devices, message // 2, 2, 128), AXES, split_axis=0, concat_axis=0, tiled=True
@@ -345,18 +364,18 @@
     total_count = block_count * ffts * block_width * size
     images, matrix_rows = call(
         functools.partial(from_planes_kernel, total_count),
-        (pltpu.HBM((sticks, 2, size), BF16), shape((2, 1, bands), F32)),
+        (pltpu.HBM((4 * sticks, 128), BF16), shape((2, 1, bands), F32)),
         [
             pltpu.VMEM((devices * message, 128), F32),
-            pltpu.VMEM((sticks, 2, size), BF16),
-            pltpu.VMEM((2, 512, 128), F32),
-            pltpu.VMEM((2, 512, 128), F32),
-            pltpu.SemaphoreType.DMA((block_count // 4,)),
-        ],
+            pltpu.VMEM((4 * sticks, 128), BF16),
+        ]
+        + [pltpu.VMEM((1024, 128), F32)] * 2
+        + [pltpu.SemaphoreType.DMA((block_count // 4,))],
         2 * sticks * (2 * size) ** 2,
         (returned.reshape(devices * message, 128), jnp.asarray(table)),
         out_hbm=(0,),
     )
+    images = images.reshape(sticks, 2, 2, 128).transpose(0, 2, 1, 3)
     return (images.reshape(coeffs.shape), matrix_rows)
 
 

time: 87.4 us -> 88.4 us (1.011)
  local copies, waits for them, and re-layouts: 4.56 us -> 6.59 us
  waiting for transfers between devices: 16 us -> 15.1 us
    unnamed x15 -> x19, local copies, waits for them, and re-layouts: 2.42 us -> 4.45 us
where the time goes in v8:
time: 88.4 us; the launch traced here: 87.6 us
  blocking collectives  29.6 us (33%)
  Pallas kernels  24 us (27%)
  waiting for transfers between devices  15.1 us (17%)
  starting transfers between devices  11.3 us (13%)
  local copies, waits for them, and re-layouts  6.59 us (7%)
  between operations  1 us (1%)
    all_to_all x1, blocking collectives, body(): lax.all_to_all(picked.reshape(devices, message // 2, 2, 128), AXES, split...  29.6 us
    pallas_call x4, Pallas kernels, call(): pl.pallas_call(kernel, out_shape=outs, in_specs=[HBM if i in in_hbm else...  24 us
    all_to_all x1, waiting for transfers between devices, body(): lax.all_to_all(sent.reshape(devices, rows, 128), AXES, split_axis=0, conc...  15.1 us
    all_to_all x1, starting transfers between devices, body(): lax.all_to_all(sent.reshape(devices, rows, 128), AXES, split_axis=0, conc...  11.3 us
    unnamed x19, local copies, waits for them, and re-layouts  4.45 us
  transfers between devices with their start and end apart: 1, of which 1 were waited for; matrix products, arithmetic and copies ran while one was open for 2% of the time, Pallas kernels for 7%

profile of v8, /device:TPU:0, one launch (start us, length us, event | category | flops | bytes accessed | tf_op | source)
XLA Modules:
  0.0 87.6 jit_solution(8431159361372444593)
XLA Ops:
  0.6 0.0 copy-start
  0.6 1.8 %copy.15 = bf16[192,8,2,256]{3,1,2,0:T(8,128)(2,1)S(1)} copy(bf16[192,8,2,256]{3,2,1,0:T(2,128)(2,1)} %bitcast.17) | data formatting | bytes 3145728
  2.4 0.0 copy-done
  2.4 2.5 %shard_map.113 = bf16[6144,128]{1,0:T(8,128)(2,1)} custom-call(bf16[1536,512]{1,0:T(8,128)(2,1)S(1)} %bitcast.12, bf16[512,512]{1,0:T(8,128)(2,1)S(1)} %copy-done), custom_call_target="tpu_custom_call" | custom-call | flops 805306368 | bytes 3670016 | tf_op jit(solution)/shard_map/pallas_call | solution.py:271
  5.0 0.0 copy-start.8
  5.0 0.0 copy-start.2
  5.0 0.0 copy-start.3
  5.0 0.0 copy-start.4
  5.0 11.3 %all-to-all-start = ((bf16[128,48,128]{2,1,0:T(8,128)(2,1)}), bf16[128,48,128]{2,1,0:T(8,128)(2,1)S(1)}, u32[]{:S(2)}, u32[]{:S(2)}) async-start(bf16[128,48,128]{2,1,0:T(8,128)(2,1)} %bitcast.16), calls=%async_computation | async-start | bytes 3145728 | tf_op jit(solution)/shard_map/all_to_all | solution.py:313
  16.4 0.1 mul.19
  16.5 0.0 copy-start.7
  16.5 0.6 copy-done.7
  17.1 0.1 add.39.row_ref
  17.2 0.9 %add.42.col_ref = s32[768,1]{1,0:T(8,128)S(1)} reshape(s32[16,2,24]{2,1,0:T(2,128)} %copy-done.7) | data formatting | bytes 6144 | tf_op jit(solution)/shard_map/add | solution.py:318
  18.1 1.1 %constant_dynamic-slice_fusion.v_ref = f32[2,256,256]{2,1,0:T(8,128)S(1)} fusion(f32[16,256,256]{2,1,0:T(8,128)} %param.11, s32[]{:T(128)S(6)} %select_n.3), kind=kLoop, calls=%fused_computation.2 | loop fusion | bytes 1048580 | tf_op jit(solution)/shard_map/dynamic_slice | solution.py:319
  19.2 5.7 %shard_map.114 = (bf16[2048,768]{1,0:T(8,128)(2,1)}, bf16[768,2048]{1,0:T(8,128)(2,1)}, f32[4,256,128]{2,1,0:T(8,128)}, bf16[512,768]{1,0:T(8,128)(2,1)S(1)}) custom-call(s32[1,768]{1,0:T(1,128)S(1)} %add.39.row_ref, s32[768,1]{1,0:T(8,128)S(1)} %add.42.col_ref, f32[2,256,256]{2,1,0:T(8,128)S(1)} %constant_dynamic-slice_fusion.v_ref, ...), custom_call_target="tpu_custom_call" | custom-call | flops 3221225472 | bytes 9705472 | tf_op jit(solution)/shard_map/pallas_call | solution.py:271
  24.9 0.9 %copy-done.5 = bf16[512,768]{1,0:T(8,128)(2,1)} copy-done((bf16[512,768]{1,0:T(8,128)(2,1)}, bf16[512,768]{1,0:T(8,128)(2,1)S(1)}, u32[]{:S(2)}) %copy-start.5) | copy-done | bytes 786456
  25.8 15.1 %all-to-all-done = bf16[128,48,128]{2,1,0:T(8,128)(2,1)S(1)} async-done(((bf16[128,48,128]{2,1,0:T(8,128)(2,1)}), bf16[128,48,128]{2,1,0:T(8,128)(2,1)S(1)}, u32[]{:S(2)}, u32[]{:S(2)}) %all-to-all-start) | async-done | bytes 1572896 | tf_op jit(solution)/shard_map/all_to_all | solution.py:313
  40.9 1.1 %copy-done.6 = bf16[512,768]{1,0:T(8,128)(2,1)S(1)} copy-done((bf16[512,768]{1,0:T(8,128)(2,1)S(1)}, bf16[512,768]{1,0:T(8,128)(2,1)}, u32[]{:S(2)}) %copy-start.6) | copy-done | bytes 786456
  42.1 13.0 %shard_map.115 = bf16[6400,128]{1,0:T(8,128)(2,1)S(1)} custom-call(bf16[8,768,128]{2,1,0:T(8,128)(2,1)S(1)} %bitcast.15, bf16[512,768]{1,0:T(8,128)(2,1)S(1)} %copy-done.6, bf16[2048,768]{1,0:T(8,128)(2,1)} %get-tuple-element.9.tx_hbm, bf16[768,2048]{1,0:T(8,128)(2,1)} %get-tuple-element.10.xt_hbm, f32[4,256,128]{2,1,0:T(8,128)} %get-tuple-element.11.v4_hbm, ...), custom_call_target="tpu_custom_call" | custom-call | flops 6442450944 | bytes 11862016 | tf_op jit(solution)/shard_map/pallas_call | solution.py:271
  55.1 0.0 copy-start.1
  55.1 29.6 %all_to_all.10 = bf16[128,25,2,128]{3,2,1,0:T(2,128)(2,1)S(1)} all-to-all(bf16[128,25,2,128]{3,2,1,0:T(2,128)(2,1)S(1)} %bitcast.13), channel_id=1, replica_groups=mesh['band'=8,'fft'=16] {'band','fft'}, dimensions={0} | all-to-all | bytes 3276800 | tf_op jit(solution)/shard_map/all_to_all | solution.py:360
  84.7 0.0 copy-done.1
  84.7 2.7 %shard_map.116 = (bf16[6144,128]{1,0:T(8,128)(2,1)}, f32[2,1,8]{2,1,0:T(1,128)}) custom-call(bf16[6400,128]{1,0:T(8,128)(2,1)S(1)} %bitcast.14, bf16[512,512]{1,0:T(8,128)(2,1)S(1)} %copy-done.1), custom_call_target="tpu_custom_call" | custom-call | flops 805306368 | bytes 3735616 | tf_op jit(solution)/shard_map/pallas_call | solution.py:271
  (8 shorter events, 0.0 us)
Async XLA Ops:
  0.6 1.8 %copy-start = (bf16[512,512]{1,0:T(8,128)(2,1)S(1)}, bf16[512,512]{1,0:T(8,128)(2,1)}, u32[]{:S(2)}) copy-start(bf16[512,512]{1,0:T(8,128)(2,1)} %constant.27.clone.t_ref) | copy-start | bytes 1572868
  5.0 11.4 %copy-start.8 = (s32[384]{0:T(512)S(1)}, s32[384]{0:T(512)}, u32[]{:S(2)}) copy-start(s32[384]{0:T(512)} %param.12) | copy-start | bytes 4612
  5.0 14.2 %copy-start.2 = (bf16[512,512]{1,0:T(8,128)(2,1)S(1)}, bf16[512,512]{1,0:T(8,128)(2,1)}, u32[]{:S(2)}) copy-start(bf16[512,512]{1,0:T(8,128)(2,1)} %constant.30.clone.ord_ref) | copy-start | bytes 1572868
  5.0 14.2 %copy-start.3 = (bf16[512,512]{1,0:T(8,128)(2,1)S(1)}, bf16[512,512]{1,0:T(8,128)(2,1)}, u32[]{:S(2)}) copy-start(bf16[512,512]{1,0:T(8,128)(2,1)} %constant.29.clone.b_ref) | copy-start | bytes 1572868
  5.0 14.2 %copy-start.4 = (bf16[512,512]{1,0:T(8,128)(2,1)S(1)}, bf16[512,512]{1,0:T(8,128)(2,1)}, u32[]{:S(2)}) copy-start(bf16[512,512]{1,0:T(8,128)(2,1)} %constant.28.clone.f_ref) | copy-start | bytes 1572868
  5.0 35.9 %all-to-all-start = ((bf16[128,48,128]{2,1,0:T(8,128)(2,1)}), bf16[128,48,128]{2,1,0:T(8,128)(2,1)S(1)}, u32[]{:S(2)}, u32[]{:S(2)}) async-start(bf16[128,48,128]{2,1,0:T(8,128)(2,1)} %bitcast.16), calls=%async_computation | async-start | bytes 3145728 | tf_op jit(solution)/shard_map/all_to_all | solution.py:313
  16.5 0.6 copy-start.7
  24.9 0.9 %copy-start.5 = (bf16[512,768]{1,0:T(8,128)(2,1)}, bf16[512,768]{1,0:T(8,128)(2,1)S(1)}, u32[]{:S(2)}) copy-start(bf16[512,768]{1,0:T(8,128)(2,1)S(1)} %get-tuple-element.8.tx0) | copy-start | bytes 2359300
  40.9 1.1 %copy-start.6 = (bf16[512,768]{1,0:T(8,128)(2,1)S(1)}, bf16[512,768]{1,0:T(8,128)(2,1)}, u32[]{:S(2)}) copy-start(bf16[512,768]{1,0:T(8,128)(2,1)} %copy-done.5) | copy-start | bytes 2359300
  55.1 29.6 %copy-start.1 = (bf16[512,512]{1,0:T(8,128)(2,1)S(1)}, bf16[512,512]{1,0:T(8,128)(2,1)}, u32[]{:S(2)}) copy-start(bf16[512,512]{1,0:T(8,128)(2,1)} %constant.33.clone.t_ref) | copy-start | bytes 1572868

commit v9 on v8

--- a/solution.py
+++ b/solution.py
@@ -123,7 +123,7 @@
 
 
 def prepare_kernel(
-    row_ref, col_ref, v_ref, f_ref, b_ref, ord_ref, tx_hbm, xt_hbm, v4_hbm, tx0, tx, xt, v4, sems
+    row_ref, col_ref, v_ref, f_ref, b_ref, ord_ref, tx_hbm, xt_hbm, v4_hbm, tx, xt, v4, sems
 ):
     size = f_ref.shape[0] // 2
     count = row_ref.shape[1]
@@ -143,11 +143,8 @@
     for s in range(4):
         part = slice(s * 2 * size, (s + 1) * 2 * size)
         tx[part, :] = dot(b_ref[...], hot(row_ref[...], rows, s, 0)).astype(BF16)
-        if s == 0:
-            tx0[...] = tx[part, :]
-        else:
-            copies.append(pltpu.make_async_copy(tx.at[part], tx_hbm.at[part], sems.at[s]))
-            copies[-1].start()
+        copies.append(pltpu.make_async_copy(tx.at[part], tx_hbm.at[part], sems.at[s]))
+        copies[-1].start()
         xt[:, part] = dot(hot(col_ref[...], cols, s, 1), f_ref[...]).astype(BF16)
     copies.append(pltpu.make_async_copy(xt, xt_hbm, sems.at[4]))
     copies[-1].start()
@@ -164,7 +161,7 @@
 
 
 def planes_kernel(
-    groups, r_ref, tx0, tx_hbm, xt_hbm, v4_hbm, yf_hbm, yb_hbm, o_ref,
+    groups, r_ref, tx_hbm, xt_hbm, v4_hbm, yf_hbm, yb_hbm, o_ref,
     tx, xt, v4, yf, yb, h, r_scr, p_scr, sems,
 ):
     size = v4.shape[1]
@@ -176,24 +173,24 @@
     load_f = pltpu.make_async_copy(yf_hbm, yf, sems.at[6])
     load_b = pltpu.make_async_copy(yb_hbm, yb, sems.at[7])
     loads = []
-    for s in range(1, 4):
+    for s in range(4):
         part = slice(s * 2 * size, (s + 1) * 2 * size)
         loads.append(pltpu.make_async_copy(tx_hbm.at[part], tx.at[part], sems.at[s]))
     load_xt = pltpu.make_async_copy(xt_hbm, xt, sems.at[4])
+    loads[0].start()
     load_f.start()
     load_v.start()
     load_b.start()
-    for copy in loads:
+    for copy in loads[1:]:
         copy.start()
     load_xt.start()
     for b in range(bands):
         r_scr[b * count : (b + 1) * count, :] = r_ref[b].astype(F32)
 
     for s in range(4):
-        if s > 0:
-            loads[s - 1].wait()
+        loads[s].wait()
         w = jnp.concatenate([r_ref[b] for b in range(bands)], axis=1)
-        g = dot(tx0[...] if s == 0 else tx[s * 2 * size : (s + 1) * 2 * size, :], w).astype(BF16)
+        g = dot(tx[s * 2 * size : (s + 1) * 2 * size, :], w).astype(BF16)
         left = jnp.concatenate(
             [
                 jnp.concatenate(
@@ -324,9 +321,9 @@
         pltpu.HBM((4, size, per_dev * size // 4), F32),
     )
     held = [pltpu.VMEM(t.shape, t.dtype) for t in tables]
-    x_table, x_back, v4, x_first = call(
+    x_table, x_back, v4 = call(
         prepare_kernel,
-        tables + (shape((2 * size, count), BF16),),
+        tables,
         held + [pltpu.SemaphoreType.DMA((6,))],
         2 * 2 * 4 * count * (2 * size) ** 2,
         (
@@ -354,8 +351,8 @@
             pltpu.SemaphoreType.DMA((8,)),
         ],
         2 * bands * 128 * 2 * 8 * size * count,
-        (got, x_first, x_table, x_back, v4, jnp.asarray(y_forward), jnp.asarray(y_backward)),
-        in_hbm=(2, 3, 4, 5, 6),
+        (got, x_table, x_back, v4, jnp.asarray(y_forward), jnp.asarray(y_backward)),
+        in_hbm=(1, 2, 3, 4, 5),
     )
     returned = lax.all_to_all(
         picked.reshape(devices, message // 2, 2, 128), AXES, split_axis=0, concat_axis=0, tiled=True

time: 88.4 us -> 87 us (0.984)
  local copies, waits for them, and re-layouts: 6.59 us -> 4.58 us
  waiting for transfers between devices: 15.1 us -> 16 us
    unnamed x19 -> x15, local copies, waits for them, and re-layouts: 4.45 us -> 2.43 us
where the time goes in v9:
time: 87 us; the launch traced here: 86.2 us
  blocking collectives  29.6 us (34%)
  Pallas kernels  23.7 us (27%)
  waiting for transfers between devices  16 us (18%)
  starting transfers between devices  11.3 us (13%)
  local copies, waits for them, and re-layouts  4.58 us (5%)
  between operations  0.99 us (1%)
    all_to_all x1, blocking collectives, body(): lax.all_to_all(picked.reshape(devices, message // 2, 2, 128), AXES, split...  29.6 us
    pallas_call x4, Pallas kernels, call(): pl.pallas_call(kernel, out_shape=outs, in_specs=[HBM if i in in_hbm else...  23.7 us
    all_to_all x1, waiting for transfers between devices, body(): lax.all_to_all(sent.reshape(devices, rows, 128), AXES, split_axis=0, conc...  16 us
    all_to_all x1, starting transfers between devices, body(): lax.all_to_all(sent.reshape(devices, rows, 128), AXES, split_axis=0, conc...  11.3 us
    unnamed x15, local copies, waits for them, and re-layouts  2.43 us
  transfers between devices with their start and end apart: 1, of which 1 were waited for; matrix products, arithmetic and copies ran while one was open for 2% of the time, Pallas kernels for 7%

profile of v9, /device:TPU:0, one launch (start us, length us, event | category | flops | bytes accessed | tf_op | source)
XLA Modules:
  0.0 86.2 jit_solution(13518366514310603738)
XLA Ops:
  0.6 0.0 copy-start
  0.6 1.8 %copy.15 = bf16[192,8,2,256]{3,1,2,0:T(8,128)(2,1)S(1)} copy(bf16[192,8,2,256]{3,2,1,0:T(2,128)(2,1)} %bitcast.17) | data formatting | bytes 3145728
  2.4 0.0 copy-done
  2.4 2.5 %shard_map.113 = bf16[6144,128]{1,0:T(8,128)(2,1)} custom-call(bf16[1536,512]{1,0:T(8,128)(2,1)S(1)} %bitcast.12, bf16[512,512]{1,0:T(8,128)(2,1)S(1)} %copy-done), custom_call_target="tpu_custom_call" | custom-call | flops 805306368 | bytes 3670016 | tf_op jit(solution)/shard_map/pallas_call | solution.py:268
  5.0 0.0 copy-start.6
  5.0 0.0 copy-start.2
  5.0 0.0 copy-start.3
  5.0 0.0 copy-start.4
  5.0 11.3 %all-to-all-start = ((bf16[128,48,128]{2,1,0:T(8,128)(2,1)}), bf16[128,48,128]{2,1,0:T(8,128)(2,1)S(1)}, u32[]{:S(2)}, u32[]{:S(2)}) async-start(bf16[128,48,128]{2,1,0:T(8,128)(2,1)} %bitcast.16), calls=%async_computation | async-start | bytes 3145728 | tf_op jit(solution)/shard_map/all_to_all | solution.py:310
  16.3 0.0 copy-done.6
  16.4 0.1 mul.19
  16.5 0.0 copy-start.5
  16.5 0.6 copy-done.5
  17.1 0.1 add.39.row_ref
  17.2 0.9 %add.42.col_ref = s32[768,1]{1,0:T(8,128)S(1)} reshape(s32[16,2,24]{2,1,0:T(2,128)} %copy-done.5) | data formatting | bytes 6144 | tf_op jit(solution)/shard_map/add | solution.py:315
  18.1 1.1 %constant_dynamic-slice_fusion.v_ref = f32[2,256,256]{2,1,0:T(8,128)S(1)} fusion(f32[16,256,256]{2,1,0:T(8,128)} %param.11, s32[]{:T(128)S(6)} %select_n.3), kind=kLoop, calls=%fused_computation.2 | loop fusion | bytes 1048580 | tf_op jit(solution)/shard_map/dynamic_slice | solution.py:316
  19.2 0.0 copy-done.2
  19.2 0.0 copy-done.3
  19.2 5.7 %shard_map.114 = (bf16[2048,768]{1,0:T(8,128)(2,1)}, bf16[768,2048]{1,0:T(8,128)(2,1)}, f32[4,256,128]{2,1,0:T(8,128)}) custom-call(s32[1,768]{1,0:T(1,128)S(1)} %add.39.row_ref, s32[768,1]{1,0:T(8,128)S(1)} %add.42.col_ref, f32[2,256,256]{2,1,0:T(8,128)S(1)} %constant_dynamic-slice_fusion.v_ref, bf16[512,512]{1,0:T(8,128)(2,1)S(1)} %copy-done.4, ...), custom_call_target="tpu_custom_call" | custom-call | flops 3221225472 | bytes 8919040 | tf_op jit(solution)/shard_map/pallas_call | solution.py:268
  24.9 16.0 %all-to-all-done = bf16[128,48,128]{2,1,0:T(8,128)(2,1)S(1)} async-done(((bf16[128,48,128]{2,1,0:T(8,128)(2,1)}), bf16[128,48,128]{2,1,0:T(8,128)(2,1)S(1)}, u32[]{:S(2)}, u32[]{:S(2)}) %all-to-all-start) | async-done | bytes 1572896 | tf_op jit(solution)/shard_map/all_to_all | solution.py:310
  40.9 12.8 %shard_map.115 = bf16[6400,128]{1,0:T(8,128)(2,1)S(1)} custom-call(bf16[8,768,128]{2,1,0:T(8,128)(2,1)S(1)} %bitcast.15, bf16[2048,768]{1,0:T(8,128)(2,1)} %get-tuple-element.7.tx_hbm, bf16[768,2048]{1,0:T(8,128)(2,1)} %get-tuple-element.8.xt_hbm, f32[4,256,128]{2,1,0:T(8,128)} %get-tuple-element.9.v4_hbm, bf16[4,256,256]{2,1,0:T(8,128)(2,1)} %constant.31.clone.yf_hbm, ...), custom_call_target="tpu_custom_call" | custom-call | flops 6442450944 | bytes 11075584 | tf_op jit(solution)/shard_map/pallas_call | solution.py:268
  53.7 0.0 copy-start.1
  53.7 29.6 %all_to_all.10 = bf16[128,25,2,128]{3,2,1,0:T(2,128)(2,1)S(1)} all-to-all(bf16[128,25,2,128]{3,2,1,0:T(2,128)(2,1)S(1)} %bitcast.13), channel_id=1, replica_groups=mesh['band'=8,'fft'=16] {'band','fft'}, dimensions={0} | all-to-all | bytes 3276800 | tf_op jit(solution)/shard_map/all_to_all | solution.py:357
  83.3 2.7 %shard_map.116 = (bf16[6144,128]{1,0:T(8,128)(2,1)}, f32[2,1,8]{2,1,0:T(1,128)}) custom-call(bf16[6400,128]{1,0:T(8,128)(2,1)S(1)} %bitcast.14, bf16[512,512]{1,0:T(8,128)(2,1)S(1)} %copy-done.1), custom_call_target="tpu_custom_call" | custom-call | flops 805306368 | bytes 3735616 | tf_op jit(solution)/shard_map/pallas_call | solution.py:268
  (4 shorter events, 0.0 us)
Async XLA Ops:
  0.6 1.8 %copy-start = (bf16[512,512]{1,0:T(8,128)(2,1)S(1)}, bf16[512,512]{1,0:T(8,128)(2,1)}, u32[]{:S(2)}) copy-start(bf16[512,512]{1,0:T(8,128)(2,1)} %constant.27.clone.t_ref) | copy-start | bytes 1572868
  5.0 11.4 %copy-start.6 = (s32[384]{0:T(512)S(1)}, s32[384]{0:T(512)}, u32[]{:S(2)}) copy-start(s32[384]{0:T(512)} %param.12) | copy-start | bytes 4612
  5.0 14.2 %copy-start.2 = (bf16[512,512]{1,0:T(8,128)(2,1)S(1)}, bf16[512,512]{1,0:T(8,128)(2,1)}, u32[]{:S(2)}) copy-start(bf16[512,512]{1,0:T(8,128)(2,1)} %constant.30.clone.ord_ref) | copy-start | bytes 1572868
  5.0 14.2 %copy-start.3 = (bf16[512,512]{1,0:T(8,128)(2,1)S(1)}, bf16[512,512]{1,0:T(8,128)(2,1)}, u32[]{:S(2)}) copy-start(bf16[512,512]{1,0:T(8,128)(2,1)} %constant.29.clone.b_ref) | copy-start | bytes 1572868
  5.0 14.2 %copy-start.4 = (bf16[512,512]{1,0:T(8,128)(2,1)S(1)}, bf16[512,512]{1,0:T(8,128)(2,1)}, u32[]{:S(2)}) copy-start(bf16[512,512]{1,0:T(8,128)(2,1)} %constant.28.clone.f_ref) | copy-start | bytes 1572868
  5.0 35.9 %all-to-all-start = ((bf16[128,48,128]{2,1,0:T(8,128)(2,1)}), bf16[128,48,128]{2,1,0:T(8,128)(2,1)S(1)}, u32[]{:S(2)}, u32[]{:S(2)}) async-start(bf16[128,48,128]{2,1,0:T(8,128)(2,1)} %bitcast.16), calls=%async_computation | async-start | bytes 3145728 | tf_op jit(solution)/shard_map/all_to_all | solution.py:310
  16.5 0.6 copy-start.5
  53.7 29.6 %copy-start.1 = (bf16[512,512]{1,0:T(8,128)(2,1)S(1)}, bf16[512,512]{1,0:T(8,128)(2,1)}, u32[]{:S(2)}) copy-start(bf16[512,512]{1,0:T(8,128)(2,1)} %constant.33.clone.t_ref) | copy-start | bytes 1572868

commit v10 on v9

--- a/solution.py
+++ b/solution.py
@@ -173,22 +173,28 @@
     load_f = pltpu.make_async_copy(yf_hbm, yf, sems.at[6])
     load_b = pltpu.make_async_copy(yb_hbm, yb, sems.at[7])
     loads = []
-    for s in range(4):
+    quarters = []
+    for i in range(4):
+        part = slice(i * size // 2, (i + 1) * size // 2)
+        quarters.append(pltpu.make_async_copy(tx_hbm.at[part], tx.at[part], sems.at[8 + i]))
+    for s in range(1, 4):
         part = slice(s * 2 * size, (s + 1) * 2 * size)
         loads.append(pltpu.make_async_copy(tx_hbm.at[part], tx.at[part], sems.at[s]))
     load_xt = pltpu.make_async_copy(xt_hbm, xt, sems.at[4])
-    loads[0].start()
+    for copy in quarters:
+        copy.start()
     load_f.start()
     load_v.start()
     load_b.start()
-    for copy in loads[1:]:
+    for copy in loads:
         copy.start()
     load_xt.start()
     for b in range(bands):
         r_scr[b * count : (b + 1) * count, :] = r_ref[b].astype(F32)
 
     for s in range(4):
-        loads[s].wait()
+        for copy in (quarters, [], loads[1:], [])[s]:
+            copy.wait()
         w = jnp.concatenate([r_ref[b] for b in range(bands)], axis=1)
         g = dot(tx[s * 2 * size : (s + 1) * 2 * size, :], w).astype(BF16)
         left = jnp.concatenate(
@@ -204,6 +210,7 @@
             load_f.wait()
             load_v.wait()
             load_b.wait()
+            loads[0].wait()
         v = jnp.concatenate([v4[s], v4[s]], axis=1)
         field = (dot(left, yf[s]) * jnp.concatenate([v] * bands, axis=0)).astype(BF16)
         back = dot(field, yb[s]).astype(BF16)
@@ -348,7 +355,7 @@
             pltpu.VMEM((8 * size, bands * 128), BF16),
             pltpu.VMEM((bands * count, 128), F32),
             pltpu.VMEM((devices * message, 128), F32),
-            pltpu.SemaphoreType.DMA((8,)),
+            pltpu.SemaphoreType.DMA((12,)),
         ],
         2 * bands * 128 * 2 * 8 * size * count,
         (got, x_table, x_back, v4, jnp.asarray(y_forward), jnp.asarray(y_backward)),

time: 87 us -> 86.5 us (level)
  transfers between devices with their start and end apart: 1 -> 1, of which waited for: 1 -> 1; matrix products, arithmetic and copies ran while one was open for 2% -> 3% of each run, Pallas kernels for 7% -> 7%
where the time goes in v10:
time: 86.5 us; the launch traced here: 85.7 us
  blocking collectives  29.6 us (34%)
  Pallas kernels  23.2 us (27%)
  waiting for transfers between devices  16 us (18%)
  starting transfers between devices  11.3 us (13%)
  local copies, waits for them, and re-layouts  4.58 us (5%)
  between operations  0.99 us (1%)
    all_to_all x1, blocking collectives, body(): lax.all_to_all(picked.reshape(devices, message // 2, 2, 128), AXES, split...  29.6 us
    pallas_call x4, Pallas kernels, call(): pl.pallas_call(kernel, out_shape=outs, in_specs=[HBM if i in in_hbm else...  23.2 us
    all_to_all x1, waiting for transfers between devices, body(): lax.all_to_all(sent.reshape(devices, rows, 128), AXES, split_axis=0, conc...  16 us
    all_to_all x1, starting transfers between devices, body(): lax.all_to_all(sent.reshape(devices, rows, 128), AXES, split_axis=0, conc...  11.3 us
    unnamed x15, local copies, waits for them, and re-layouts  2.43 us
  transfers between devices with their start and end apart: 1, of which 1 were waited for; matrix products, arithmetic and copies ran while one was open for 3% of the time, Pallas kernels for 7%

profile of v10, /device:TPU:0, one launch (start us, length us, event | category | flops | bytes accessed | tf_op | source)
XLA Modules:
  0.0 85.7 jit_solution(5150697450617375257)
XLA Ops:
  0.6 0.0 copy-start
  0.6 1.8 %copy.15 = bf16[192,8,2,256]{3,1,2,0:T(8,128)(2,1)S(1)} copy(bf16[192,8,2,256]{3,2,1,0:T(2,128)(2,1)} %bitcast.17) | data formatting | bytes 3145728
  2.4 0.0 copy-done
  2.4 2.5 %shard_map.113 = bf16[6144,128]{1,0:T(8,128)(2,1)} custom-call(bf16[1536,512]{1,0:T(8,128)(2,1)S(1)} %bitcast.12, bf16[512,512]{1,0:T(8,128)(2,1)S(1)} %copy-done), custom_call_target="tpu_custom_call" | custom-call | flops 805306368 | bytes 3670016 | tf_op jit(solution)/shard_map/pallas_call | solution.py:275
  5.0 0.0 copy-start.6
  5.0 0.0 copy-start.2
  5.0 0.0 copy-start.3
  5.0 0.0 copy-start.4
  5.0 11.3 %all-to-all-start = ((bf16[128,48,128]{2,1,0:T(8,128)(2,1)}), bf16[128,48,128]{2,1,0:T(8,128)(2,1)S(1)}, u32[]{:S(2)}, u32[]{:S(2)}) async-start(bf16[128,48,128]{2,1,0:T(8,128)(2,1)} %bitcast.16), calls=%async_computation | async-start | bytes 3145728 | tf_op jit(solution)/shard_map/all_to_all | solution.py:317
  16.3 0.0 copy-done.6
  16.4 0.1 mul.19
  16.5 0.0 copy-start.5
  16.5 0.6 copy-done.5
  17.1 0.1 add.39.row_ref
  17.2 0.9 %add.42.col_ref = s32[768,1]{1,0:T(8,128)S(1)} reshape(s32[16,2,24]{2,1,0:T(2,128)} %copy-done.5) | data formatting | bytes 6144 | tf_op jit(solution)/shard_map/add | solution.py:322
  18.1 1.1 %constant_dynamic-slice_fusion.v_ref = f32[2,256,256]{2,1,0:T(8,128)S(1)} fusion(f32[16,256,256]{2,1,0:T(8,128)} %param.11, s32[]{:T(128)S(6)} %select_n.3), kind=kLoop, calls=%fused_computation.2 | loop fusion | bytes 1048580 | tf_op jit(solution)/shard_map/dynamic_slice | solution.py:323
  19.2 0.0 copy-done.2
  19.2 5.7 %shard_map.114 = (bf16[2048,768]{1,0:T(8,128)(2,1)}, bf16[768,2048]{1,0:T(8,128)(2,1)}, f32[4,256,128]{2,1,0:T(8,128)}) custom-call(s32[1,768]{1,0:T(1,128)S(1)} %add.39.row_ref, s32[768,1]{1,0:T(8,128)S(1)} %add.42.col_ref, f32[2,256,256]{2,1,0:T(8,128)S(1)} %constant_dynamic-slice_fusion.v_ref, bf16[512,512]{1,0:T(8,128)(2,1)S(1)} %copy-done.4, ...), custom_call_target="tpu_custom_call" | custom-call | flops 3221225472 | bytes 8919040 | tf_op jit(solution)/shard_map/pallas_call | solution.py:275
  24.9 16.0 %all-to-all-done = bf16[128,48,128]{2,1,0:T(8,128)(2,1)S(1)} async-done(((bf16[128,48,128]{2,1,0:T(8,128)(2,1)}), bf16[128,48,128]{2,1,0:T(8,128)(2,1)S(1)}, u32[]{:S(2)}, u32[]{:S(2)}) %all-to-all-start) | async-done | bytes 1572896 | tf_op jit(solution)/shard_map/all_to_all | solution.py:317
  40.9 12.3 %shard_map.115 = bf16[6400,128]{1,0:T(8,128)(2,1)S(1)} custom-call(bf16[8,768,128]{2,1,0:T(8,128)(2,1)S(1)} %bitcast.15, bf16[2048,768]{1,0:T(8,128)(2,1)} %get-tuple-element.7.tx_hbm, bf16[768,2048]{1,0:T(8,128)(2,1)} %get-tuple-element.8.xt_hbm, f32[4,256,128]{2,1,0:T(8,128)} %get-tuple-element.9.v4_hbm, bf16[4,256,256]{2,1,0:T(8,128)(2,1)} %constant.31.clone.yf_hbm, ...), custom_call_target="tpu_custom_call" | custom-call | flops 6442450944 | bytes 11075584 | tf_op jit(solution)/shard_map/pallas_call | solution.py:275
  53.2 0.0 copy-start.1
  53.3 29.6 %all_to_all.10 = bf16[128,25,2,128]{3,2,1,0:T(2,128)(2,1)S(1)} all-to-all(bf16[128,25,2,128]{3,2,1,0:T(2,128)(2,1)S(1)} %bitcast.13), channel_id=1, replica_groups=mesh['band'=8,'fft'=16] {'band','fft'}, dimensions={0} | all-to-all | bytes 3276800 | tf_op jit(solution)/shard_map/all_to_all | solution.py:364
  82.9 0.0 copy-done.1
  82.9 2.7 %shard_map.116 = (bf16[6144,128]{1,0:T(8,128)(2,1)}, f32[2,1,8]{2,1,0:T(1,128)}) custom-call(bf16[6400,128]{1,0:T(8,128)(2,1)S(1)} %bitcast.14, bf16[512,512]{1,0:T(8,128)(2,1)S(1)} %copy-done.1), custom_call_target="tpu_custom_call" | custom-call | flops 805306368 | bytes 3735616 | tf_op jit(solution)/shard_map/pallas_call | solution.py:275
  (4 shorter events, 0.0 us)
Async XLA Ops:
  0.6 1.8 %copy-start = (bf16[512,512]{1,0:T(8,128)(2,1)S(1)}, bf16[512,512]{1,0:T(8,128)(2,1)}, u32[]{:S(2)}) copy-start(bf16[512,512]{1,0:T(8,128)(2,1)} %constant.27.clone.t_ref) | copy-start | bytes 1572868
  5.0 11.4 %copy-start.6 = (s32[384]{0:T(512)S(1)}, s32[384]{0:T(512)}, u32[]{:S(2)}) copy-start(s32[384]{0:T(512)} %param.12) | copy-start | bytes 4612
  5.0 14.2 %copy-start.2 = (bf16[512,512]{1,0:T(8,128)(2,1)S(1)}, bf16[512,512]{1,0:T(8,128)(2,1)}, u32[]{:S(2)}) copy-start(bf16[512,512]{1,0:T(8,128)(2,1)} %constant.30.clone.ord_ref) | copy-start | bytes 1572868
  5.0 14.2 %copy-start.3 = (bf16[512,512]{1,0:T(8,128)(2,1)S(1)}, bf16[512,512]{1,0:T(8,128)(2,1)}, u32[]{:S(2)}) copy-start(bf16[512,512]{1,0:T(8,128)(2,1)} %constant.29.clone.b_ref) | copy-start | bytes 1572868
  5.0 14.2 %copy-start.4 = (bf16[512,512]{1,0:T(8,128)(2,1)S(1)}, bf16[512,512]{1,0:T(8,128)(2,1)}, u32[]{:S(2)}) copy-start(bf16[512,512]{1,0:T(8,128)(2,1)} %constant.28.clone.f_ref) | copy-start | bytes 1572868
  5.0 35.9 %all-to-all-start = ((bf16[128,48,128]{2,1,0:T(8,128)(2,1)}), bf16[128,48,128]{2,1,0:T(8,128)(2,1)S(1)}, u32[]{:S(2)}, u32[]{:S(2)}) async-start(bf16[128,48,128]{2,1,0:T(8,128)(2,1)} %bitcast.16), calls=%async_computation | async-start | bytes 3145728 | tf_op jit(solution)/shard_map/all_to_all | solution.py:317
  16.5 0.6 copy-start.5
  53.2 29.6 %copy-start.1 = (bf16[512,512]{1,0:T(8,128)(2,1)S(1)}, bf16[512,512]{1,0:T(8,128)(2,1)}, u32[]{:S(2)}) copy-start(bf16[512,512]{1,0:T(8,128)(2,1)} %constant.33.clone.t_ref) | copy-start | bytes 1572868

commit v11 on v10

--- a/solution.py
+++ b/solution.py
@@ -162,7 +162,7 @@
 
 def planes_kernel(
     groups, r_ref, tx_hbm, xt_hbm, v4_hbm, yf_hbm, yb_hbm, o_ref,
-    tx, xt, v4, yf, yb, h, r_scr, p_scr, sems,
+    tx, xt, v4, yf, yb, h, r_scr, p_scr, stack, sems,
 ):
     size = v4.shape[1]
     bands, count = r_ref.shape[0], r_ref.shape[1]
@@ -244,16 +244,18 @@
                         add((i, j, 0), real * part[:blocks] + imag * part[blocks:])
                         add((i, j, 1), real * part[blocks:] - imag * part[:blocks])
             if first + group == ffts:
+                for i, j, c in [key for key in sums if key[1] >= 2 * n]:
+                    line = jnp.sum(sums.pop((i, j, c)), axis=0, keepdims=True)
+                    at = (2 * i + c) * bands + j
+                    stack[at : at + 1, :] = line
+                    if i < j:
+                        at = (2 * j + c) * bands + i
+                        stack[at : at + 1, :] = -line if c else line
                 done = slice(2 * n * ffts * message, (2 * n + 2) * ffts * message)
                 o_ref[done, :] = p_scr[done, :].astype(BF16)
         first += group
 
-    sums = {key: jnp.sum(value, axis=0, keepdims=True) for key, value in sums.items()}
-    lines = []
-    for i in range(bands):
-        lines += [sums[min(i, j), max(i, j), 0] for j in range(bands)]
-        lines += [sums[i, j, 1] if i <= j else -sums[j, i, 1] for j in range(bands)]
-    total = jnp.sum(jnp.transpose(jnp.concatenate(lines, axis=0)), axis=0, keepdims=True)
+    total = jnp.sum(jnp.transpose(stack[...]), axis=0, keepdims=True)
     high = total.astype(BF16).astype(F32)
     pair = jnp.concatenate([high, total - high], axis=0)
     for b in range(bands):
@@ -355,6 +357,7 @@
             pltpu.VMEM((8 * size, bands * 128), BF16),
             pltpu.VMEM((bands * count, 128), F32),
             pltpu.VMEM((devices * message, 128), F32),
+            pltpu.VMEM((2 * bands * bands, 128), F32),
             pltpu.SemaphoreType.DMA((12,)),
         ],
         2 * bands * 128 * 2 * 8 * size * count,

time: 86.5 us -> 86.5 us (level)
  no operation moved by 1% of the time
where the time goes in v11:
time: 86.5 us; the launch traced here: 85.7 us
  blocking collectives  29.6 us (34%)
  Pallas kernels  23.2 us (27%)
  waiting for transfers between devices  16 us (18%)
  starting transfers between devices  11.3 us (13%)
  local copies, waits for them, and re-layouts  4.58 us (5%)
  between operations  0.99 us (1%)
    all_to_all x1, blocking collectives, body(): lax.all_to_all(picked.reshape(devices, message // 2, 2, 128), AXES, split...  29.6 us
    pallas_call x4, Pallas kernels, call(): pl.pallas_call(kernel, out_shape=outs, in_specs=[HBM if i in in_hbm else...  23.2 us
    all_to_all x1, waiting for transfers between devices, body(): lax.all_to_all(sent.reshape(devices, rows, 128), AXES, split_axis=0, conc...  16 us
    all_to_all x1, starting transfers between devices, body(): lax.all_to_all(sent.reshape(devices, rows, 128), AXES, split_axis=0, conc...  11.3 us
    unnamed x15, local copies, waits for them, and re-layouts  2.43 us
  transfers between devices with their start and end apart: 1, of which 1 were waited for; matrix products, arithmetic and copies ran while one was open for 3% of the time, Pallas kernels for 7%

profile of v11, /device:TPU:0, one launch (start us, length us, event | category | flops | bytes accessed | tf_op | source)
XLA Modules:
  0.0 85.7 jit_solution(9393005512071322675)
XLA Ops:
  0.6 0.0 copy-start
  0.6 1.8 %copy.15 = bf16[192,8,2,256]{3,1,2,0:T(8,128)(2,1)S(1)} copy(bf16[192,8,2,256]{3,2,1,0:T(2,128)(2,1)} %bitcast.17) | data formatting | bytes 3145728
  2.4 0.0 copy-done
  2.4 2.5 %shard_map.113 = bf16[6144,128]{1,0:T(8,128)(2,1)} custom-call(bf16[1536,512]{1,0:T(8,128)(2,1)S(1)} %bitcast.12, bf16[512,512]{1,0:T(8,128)(2,1)S(1)} %copy-done), custom_call_target="tpu_custom_call" | custom-call | flops 805306368 | bytes 3670016 | tf_op jit(solution)/shard_map/pallas_call | solution.py:277
  5.0 0.0 copy-start.6
  5.0 0.0 copy-start.2
  5.0 0.0 copy-start.3
  5.0 0.0 copy-start.4
  5.0 11.3 %all-to-all-start = ((bf16[128,48,128]{2,1,0:T(8,128)(2,1)}), bf16[128,48,128]{2,1,0:T(8,128)(2,1)S(1)}, u32[]{:S(2)}, u32[]{:S(2)}) async-start(bf16[128,48,128]{2,1,0:T(8,128)(2,1)} %bitcast.16), calls=%async_computation | async-start | bytes 3145728 | tf_op jit(solution)/shard_map/all_to_all | solution.py:319
  16.3 0.0 copy-done.6
  16.4 0.1 mul.19
  16.5 0.0 copy-start.5
  16.5 0.6 copy-done.5
  17.1 0.1 add.39.row_ref
  17.2 0.9 %add.42.col_ref = s32[768,1]{1,0:T(8,128)S(1)} reshape(s32[16,2,24]{2,1,0:T(2,128)} %copy-done.5) | data formatting | bytes 6144 | tf_op jit(solution)/shard_map/add | solution.py:324
  18.1 1.1 %constant_dynamic-slice_fusion.v_ref = f32[2,256,256]{2,1,0:T(8,128)S(1)} fusion(f32[16,256,256]{2,1,0:T(8,128)} %param.11, s32[]{:T(128)S(6)} %select_n.3), kind=kLoop, calls=%fused_computation.2 | loop fusion | bytes 1048580 | tf_op jit(solution)/shard_map/dynamic_slice | solution.py:325
  19.2 0.0 copy-done.2
  19.2 0.0 copy-done.3
  19.2 5.7 %shard_map.114 = (bf16[2048,768]{1,0:T(8,128)(2,1)}, bf16[768,2048]{1,0:T(8,128)(2,1)}, f32[4,256,128]{2,1,0:T(8,128)}) custom-call(s32[1,768]{1,0:T(1,128)S(1)} %add.39.row_ref, s32[768,1]{1,0:T(8,128)S(1)} %add.42.col_ref, f32[2,256,256]{2,1,0:T(8,128)S(1)} %constant_dynamic-slice_fusion.v_ref, bf16[512,512]{1,0:T(8,128)(2,1)S(1)} %copy-done.4, ...), custom_call_target="tpu_custom_call" | custom-call | flops 3221225472 | bytes 8919040 | tf_op jit(solution)/shard_map/pallas_call | solution.py:277
  24.9 16.0 %all-to-all-done = bf16[128,48,128]{2,1,0:T(8,128)(2,1)S(1)} async-done(((bf16[128,48,128]{2,1,0:T(8,128)(2,1)}), bf16[128,48,128]{2,1,0:T(8,128)(2,1)S(1)}, u32[]{:S(2)}, u32[]{:S(2)}) %all-to-all-start) | async-done | bytes 1572896 | tf_op jit(solution)/shard_map/all_to_all | solution.py:319
  40.9 12.3 %shard_map.115 = bf16[6400,128]{1,0:T(8,128)(2,1)S(1)} custom-call(bf16[8,768,128]{2,1,0:T(8,128)(2,1)S(1)} %bitcast.15, bf16[2048,768]{1,0:T(8,128)(2,1)} %get-tuple-element.7.tx_hbm, bf16[768,2048]{1,0:T(8,128)(2,1)} %get-tuple-element.8.xt_hbm, f32[4,256,128]{2,1,0:T(8,128)} %get-tuple-element.9.v4_hbm, bf16[4,256,256]{2,1,0:T(8,128)(2,1)} %constant.31.clone.yf_hbm, ...), custom_call_target="tpu_custom_call" | custom-call | flops 6442450944 | bytes 11075584 | tf_op jit(solution)/shard_map/pallas_call | solution.py:277
  53.2 0.0 copy-start.1
  53.2 29.6 %all_to_all.10 = bf16[128,25,2,128]{3,2,1,0:T(2,128)(2,1)S(1)} all-to-all(bf16[128,25,2,128]{3,2,1,0:T(2,128)(2,1)S(1)} %bitcast.13), channel_id=1, replica_groups=mesh['band'=8,'fft'=16] {'band','fft'}, dimensions={0} | all-to-all | bytes 3276800 | tf_op jit(solution)/shard_map/all_to_all | solution.py:367
  82.8 2.7 %shard_map.116 = (bf16[6144,128]{1,0:T(8,128)(2,1)}, f32[2,1,8]{2,1,0:T(1,128)}) custom-call(bf16[6400,128]{1,0:T(8,128)(2,1)S(1)} %bitcast.14, bf16[512,512]{1,0:T(8,128)(2,1)S(1)} %copy-done.1), custom_call_target="tpu_custom_call" | custom-call | flops 805306368 | bytes 3735616 | tf_op jit(solution)/shard_map/pallas_call | solution.py:277
  (4 shorter events, 0.0 us)
Async XLA Ops:
  0.6 1.8 %copy-start = (bf16[512,512]{1,0:T(8,128)(2,1)S(1)}, bf16[512,512]{1,0:T(8,128)(2,1)}, u32[]{:S(2)}) copy-start(bf16[512,512]{1,0:T(8,128)(2,1)} %constant.27.clone.t_ref) | copy-start | bytes 1572868
  5.0 11.4 %copy-start.6 = (s32[384]{0:T(512)S(1)}, s32[384]{0:T(512)}, u32[]{:S(2)}) copy-start(s32[384]{0:T(512)} %param.12) | copy-start | bytes 4612
  5.0 14.2 %copy-start.2 = (bf16[512,512]{1,0:T(8,128)(2,1)S(1)}, bf16[512,512]{1,0:T(8,128)(2,1)}, u32[]{:S(2)}) copy-start(bf16[512,512]{1,0:T(8,128)(2,1)} %constant.30.clone.ord_ref) | copy-start | bytes 1572868
  5.0 14.2 %copy-start.3 = (bf16[512,512]{1,0:T(8,128)(2,1)S(1)}, bf16[512,512]{1,0:T(8,128)(2,1)}, u32[]{:S(2)}) copy-start(bf16[512,512]{1,0:T(8,128)(2,1)} %constant.29.clone.b_ref) | copy-start | bytes 1572868
  5.0 14.2 %copy-start.4 = (bf16[512,512]{1,0:T(8,128)(2,1)S(1)}, bf16[512,512]{1,0:T(8,128)(2,1)}, u32[]{:S(2)}) copy-start(bf16[512,512]{1,0:T(8,128)(2,1)} %constant.28.clone.f_ref) | copy-start | bytes 1572868
  5.0 35.9 %all-to-all-start = ((bf16[128,48,128]{2,1,0:T(8,128)(2,1)}), bf16[128,48,128]{2,1,0:T(8,128)(2,1)S(1)}, u32[]{:S(2)}, u32[]{:S(2)}) async-start(bf16[128,48,128]{2,1,0:T(8,128)(2,1)} %bitcast.16), calls=%async_computation | async-start | bytes 3145728 | tf_op jit(solution)/shard_map/all_to_all | solution.py:319
  16.5 0.6 copy-start.5
  53.2 29.6 %copy-start.1 = (bf16[512,512]{1,0:T(8,128)(2,1)S(1)}, bf16[512,512]{1,0:T(8,128)(2,1)}, u32[]{:S(2)}) copy-start(bf16[512,512]{1,0:T(8,128)(2,1)} %constant.33.clone.t_ref) | copy-start | bytes 1572868
